TPU v7x, 32 devices: a whole 2x2x4 slice. The times are simulated.
32 devices in a mesh: dp: 32 (over z, y, x, core).
Axes of the slice: x: 2, y: 2, z: 4, core: 2. Of those that a mesh axis runs over, the one named last changes fastest.
Arguments:
- frames: bfloat16 [65536, 256], P('dp'), may hold values from -16 to 16
- dw_first: bfloat16 [5, 25, 256], P(None, None, 'dp'), may hold values from -1.25 to 1.25
- dw_second: bfloat16 [5, 27, 256], P(None, None, 'dp'), may hold values from -1.25 to 1.25
- point: bfloat16 [2, 6, 256, 256], P(None, None, 'dp'), may hold values from -0.375 to 0.375
- gains: bfloat16 [2, 6, 256], P(None, None, 'dp'), may hold values from 0.099609375 to 1.8984375
- shifts: bfloat16 [2, 6, 256], P(None, None, 'dp'), may hold values from -1.5 to 1.5
- se_down: bfloat16 [2, 256, 32], P(None, 'dp'), may hold values from -0.375 to 0.375
- se_up: bfloat16 [2, 32, 256], P(None, None, 'dp'), may hold values from -1 to 1
- cotangent: float32 [32768, 256], P('dp'), may hold values from -6 to 6
- lengths: int32 [64], P('dp'), may hold values from 130 to 1150, as said below
Outputs:
- output: float32 [32768, 256], P('dp')
- frames_grad: float32 [65536, 256], P('dp')
- dw_first_grad: float32 [5, 25, 256], P(None, None, 'dp')
- dw_second_grad: float32 [5, 27, 256], P(None, None, 'dp')
- point_grad: float32 [2, 6, 256, 256], P(None, None, 'dp')
- gains_grad: float32 [2, 6, 256], P(None, None, 'dp')
- shifts_grad: float32 [2, 6, 256], P(None, None, 'dp')
- se_down_grad: float32 [2, 256, 32], P(None, 'dp')
- se_up_grad: float32 [2, 32, 256], P(None, None, 'dp')
Inputs may be any that keep to these rules, and one draw needn't show every extreme that they name: Entries 2 * j to 2 * j + 1 are device j's utterances; every length is even and positive; one device's lengths sum to at most 2048, and to exactly 2048 on some device.
All inputs are finite; a program needn't handle non-finite values.
Results may differ from a plain program's by a relative error of at most 0.025.
Values may be sent and summed in bfloat16 or wider, within the bound.
A program may use at most 320 MiB of HBM per device.

v0:
```python
import jax
import jax.numpy as jnp
from jax import lax
from jax.sharding import PartitionSpec as P

EPSILON = 1e-05
HIGHEST = lax.Precision.HIGHEST


def depthwise(signal, kernel, source_ids, target_ids, stride):
    tap_count = kernel.shape[0]
    margin = (tap_count - 1) // 2
    outputs = target_ids.shape[0]
    channels = signal.shape[1]
    padded = jnp.pad(signal, ((margin, margin), (0, 0)))
    padded_ids = jnp.pad(source_ids, (margin, margin), constant_values=-1)
    result = jnp.zeros((outputs, channels), jnp.float32)
    for k in range(tap_count):
        slice_end = k + stride * (outputs - 1) + 1
        window = lax.slice(padded, (k, 0), (slice_end, channels), (stride, 1))
        window_ids = lax.slice(padded_ids, (k,), (slice_end,), (stride,))
        same_utterance = (window_ids == target_ids).astype(jnp.float32)[:, None]
        result = result + window * same_utterance * kernel[k]
    return result


def contract_rows(left, right):
    return lax.dot_general(
        left, right, (((0,), (0,)), ((), ())), preferred_element_type=jnp.float32
    )


def contract_columns(left, right):
    return lax.dot_general(
        left, right, (((1,), (1,)), ((), ())), preferred_element_type=jnp.float32
    )


def body(frames, dw_first, dw_second, point, gains, shifts, se_down, se_up, cotangent, lengths):
    frame_slots = frames.shape[0]
    utterances_here = lengths.shape[0]
    utterance_ends = jnp.cumsum(lengths, dtype=jnp.int32)
    positions = jnp.arange(frame_slots, dtype=jnp.int32)
    segment_in = jnp.sum(
        (positions[:, None] >= utterance_ends[None, :]).astype(jnp.int32), axis=1, dtype=jnp.int32
    )
    valid_in = (segment_in < utterances_here).astype(jnp.float32)[:, None]
    segment_out = segment_in[::2]
    valid_out = valid_in[::2]
    member = (segment_out[:, None] == jnp.arange(utterances_here, dtype=jnp.int32)[None, :]).astype(
        jnp.float32
    )
    half_lengths = lengths.astype(jnp.float32) / 2.0
    local_count = jnp.sum(lengths, dtype=jnp.int32).astype(jnp.float32) / 2.0

    def statistics(product):
        sum_rows, frame_total = lax.psum((jnp.sum(product * valid_out, axis=0), local_count), "dp")
        center = sum_rows / frame_total
        centered = (product - center) * valid_out
        variance = lax.psum(jnp.sum(centered * centered, axis=0), "dp") / frame_total
        return (center, lax.rsqrt(variance + EPSILON), frame_total)

    def norm_back(grad_z, product, center, inv_std, frame_total, gain_row):
        normed = (product - center) * inv_std
        grad_shift, grad_gain = lax.psum(
            (jnp.sum(grad_z, axis=0), jnp.sum(grad_z * normed, axis=0)), "dp"
        )
        grad_p = (
            gain_row
            * inv_std
            * (grad_z - (grad_shift + normed * grad_gain) / frame_total)
            * valid_out
        )
        return (grad_p, grad_gain, grad_shift)

    def excite_tail(last_z, residual_z, squeeze, expand):
        means = (
            lax.dot_general(member, last_z, (((0,), (0,)), ((), ())), precision=HIGHEST)
            / half_lengths[:, None]
        )
        excited = jax.nn.silu(jnp.dot(means, squeeze, precision=HIGHEST))
        scale = jax.nn.sigmoid(jnp.dot(excited, expand, precision=HIGHEST))
        mixed = last_z * jnp.dot(member, scale, precision=HIGHEST)
        return jax.nn.silu(mixed + residual_z) * valid_out

    def fetch(kernels, block_index):
        return (
            lax.all_gather(kernels, "dp", axis=2, tiled=True),
            lax.all_gather(point[block_index], "dp", axis=1, tiled=True),
            lax.all_gather(gains[block_index], "dp", axis=1, tiled=True),
            lax.all_gather(shifts[block_index], "dp", axis=1, tiled=True),
            lax.all_gather(se_down[block_index], "dp", axis=0, tiled=True),
            lax.all_gather(se_up[block_index], "dp", axis=1, tiled=True),
        )

    def fetch_again(kernels, block_index):
        return (
            lax.all_gather(kernels, "dp", axis=2, tiled=True),
            lax.all_gather(point[block_index], "dp", axis=1, tiled=True),
            lax.all_gather(gains[block_index], "dp", axis=1, tiled=True),
            lax.all_gather(shifts[block_index], "dp", axis=1, tiled=True),
            lax.all_gather(se_down[block_index], "dp", axis=0, tiled=True),
            lax.all_gather(se_up[block_index], "dp", axis=1, tiled=True),
        )

    def reduce_grads(grads):
        return (
            lax.psum_scatter(grads[0], "dp", scatter_dimension=2, tiled=True),
            lax.psum_scatter(grads[1], "dp", scatter_dimension=1, tiled=True),
            lax.psum_scatter(grads[2], "dp", scatter_dimension=0, tiled=True),
            lax.psum_scatter(grads[3], "dp", scatter_dimension=1, tiled=True),
        )

    def block_forward(signal, source_ids, params, stride):
        kernels, matrices, gain_table, shift_table, squeeze, expand = params
        sub_blocks = kernels.shape[0]
        gain_table = gain_table.astype(jnp.float32)
        shift_table = shift_table.astype(jnp.float32)
        stored = []
        hidden = signal
        normed = None
        for r in range(sub_blocks):
            step_size = stride if r == 0 else 1
            segment_ids = source_ids if r == 0 else segment_out
            filtered = depthwise(
                hidden, kernels[r].astype(jnp.float32), segment_ids, segment_out, step_size
            )
            rounded = filtered.astype(jnp.bfloat16)
            product = jnp.dot(rounded, matrices[r], preferred_element_type=jnp.float32)
            center, inv_std, frame_total = statistics(product)
            normed = (product - center) * inv_std * gain_table[r] + shift_table[r]
            stored.append((hidden, rounded, product, center, inv_std))
            if r < sub_blocks - 1:
                hidden = jax.nn.silu(normed) * valid_out
        strided = signal[::stride].astype(jnp.bfloat16)
        residual = jnp.dot(strided, matrices[sub_blocks], preferred_element_type=jnp.float32)
        res_center, res_inv, frame_total = statistics(residual)
        residual_z = (residual - res_center) * res_inv * gain_table[sub_blocks] + shift_table[
            sub_blocks
        ]
        result, tail_back = jax.vjp(
            excite_tail, normed, residual_z, squeeze.astype(jnp.float32), expand.astype(jnp.float32)
        )
        return (result, (stored, strided, residual, res_center, res_inv, frame_total, tail_back))

    def block_backward(grad_out, source_ids, params, stride, kept):
        kernels, matrices, gain_table, shift_table, squeeze, expand = params
        stored, strided, residual, res_center, res_inv, frame_total, tail_back = kept
        sub_blocks = kernels.shape[0]
        gain_table = gain_table.astype(jnp.float32)
        shift_table = shift_table.astype(jnp.float32)
        grad_z, grad_res, grad_squeeze, grad_expand = tail_back(grad_out)
        grad_q, res_gain, res_shift = norm_back(
            grad_res, residual, res_center, res_inv, frame_total, gain_table[sub_blocks]
        )
        rounded_q = grad_q.astype(jnp.bfloat16)
        matrix_grads = [None] * (sub_blocks + 1)
        kernel_grads = [None] * sub_blocks
        gain_grads = [None] * (sub_blocks + 1)
        shift_grads = [None] * (sub_blocks + 1)
        matrix_grads[sub_blocks] = contract_rows(strided, rounded_q)
        gain_grads[sub_blocks] = res_gain
        shift_grads[sub_blocks] = res_shift
        grad_strided = contract_columns(rounded_q, matrices[sub_blocks])
        if stride == 2:
            grad_skip = jnp.stack([grad_strided, jnp.zeros_like(grad_strided)], axis=1).reshape(
                -1, grad_strided.shape[1]
            )
        else:
            grad_skip = grad_strided
        grad_hidden = None
        for r in reversed(range(sub_blocks)):
            hidden, rounded, product, center, inv_std = stored[r]
            if r < sub_blocks - 1:
                normed = (product - center) * inv_std * gain_table[r] + shift_table[r]
                sigmoid_z = jax.nn.sigmoid(normed)
                grad_z = grad_hidden * sigmoid_z * (1.0 + normed * (1.0 - sigmoid_z)) * valid_out
            grad_p, gain_grads[r], shift_grads[r] = norm_back(
                grad_z, product, center, inv_std, frame_total, gain_table[r]
            )
            rounded_p = grad_p.astype(jnp.bfloat16)
            matrix_grads[r] = contract_rows(rounded, rounded_p)
            grad_filtered = contract_columns(rounded_p, matrices[r])
            step_size = stride if r == 0 else 1
            segment_ids = source_ids if r == 0 else segment_out
            _, conv_back = jax.vjp(
                lambda signal_in, kernel_in: depthwise(
                    signal_in, kernel_in, segment_ids, segment_out, step_size
                ),
                hidden,
                kernels[r].astype(jnp.float32),
            )
            grad_hidden, kernel_grads[r] = conv_back(grad_filtered)
        grad_input = grad_hidden + grad_skip
        grads = (jnp.stack(kernel_grads), jnp.stack(matrix_grads), grad_squeeze, grad_expand)
        grads = reduce_grads(grads)
        return (grad_input, grads, jnp.stack(gain_grads), jnp.stack(shift_grads))

    signal = frames.astype(jnp.float32) * valid_in
    first_params = fetch(dw_first, 0)
    first_out, first_kept = block_forward(signal, segment_in, first_params, 2)
    second_params = fetch(dw_second, 1)
    output, second_kept = block_forward(first_out, segment_out, second_params, 1)
    second_back = fetch_again(dw_second, 1)
    grad_middle, second_owned, second_gain, second_shift = block_backward(
        cotangent, segment_out, second_back, 1, second_kept
    )
    first_back = fetch_again(dw_first, 0)
    grad_input, first_owned, first_gain, first_shift = block_backward(
        grad_middle, segment_in, first_back, 2, first_kept
    )
    shard_width = gains.shape[2]
    shard_start = lax.axis_index("dp") * shard_width
    owned_gains = jnp.stack(
        [
            lax.dynamic_slice_in_dim(first_gain, shard_start, shard_width, 1),
            lax.dynamic_slice_in_dim(second_gain, shard_start, shard_width, 1),
        ]
    )
    owned_shifts = jnp.stack(
        [
            lax.dynamic_slice_in_dim(first_shift, shard_start, shard_width, 1),
            lax.dynamic_slice_in_dim(second_shift, shard_start, shard_width, 1),
        ]
    )
    frames_grad = grad_input * valid_in
    return (
        output,
        frames_grad,
        first_owned[0],
        second_owned[0],
        jnp.stack([first_owned[1], second_owned[1]]),
        owned_gains,
        owned_shifts,
        jnp.stack([first_owned[2], second_owned[2]]),
        jnp.stack([first_owned[3], second_owned[3]]),
    )


def solution(mesh):
    return jax.shard_map(
        body,
        mesh=mesh,
        in_specs=(
            P("dp", None),
            P(None, None, "dp"),
            P(None, None, "dp"),
            P(None, None, "dp", None),
            P(None, None, "dp"),
            P(None, None, "dp"),
            P(None, "dp", None),
            P(None, None, "dp"),
            P("dp", None),
            P("dp"),
        ),
        out_specs=(
            P("dp", None),
            P("dp", None),
            P(None, None, "dp"),
            P(None, None, "dp"),
            P(None, None, "dp", None),
            P(None, None, "dp"),
            P(None, None, "dp"),
            P(None, "dp", None),
            P(None, None, "dp"),
        ),
        check_vma=False,
    )
```

profile of v0, /device:TPU:0, one launch (start us, length us, event | category | flops | bytes accessed | tf_op | source)
XLA Modules:
  0.0 2800.5 jit_solution(2213560499673049560)
XLA Ops:
  31.1 44.7 %all_gather.50 = bf16[5,27,256]{1,2,0:T(8,128)(2,1)S(1)} all-gather(bf16[5,27,8]{1,2,0:T(8,128)(2,1)} %param.12), channel_id=1, replica_groups=mesh['dp'=32] {'dp'}, dimensions={2}, use_global_device_ids=true | all-gather | bytes 71280 | tf_op jit(solution)/shard_map/all_gather | solution.py:88
  314.8 38.6 %all-gather.4 = bf16[1,32,256]{1,2,0:T(8,128)(2,1)S(1)} all-gather(bf16[1,32,8]{1,2,0:T(8,128)(2,1)S(1)} %get-tuple-element.983), channel_id=6, replica_groups=mesh['dp'=32] {'dp'}, dimensions={2}, use_global_device_ids=true | all-gather | bytes 16896 | tf_op jit(solution)/shard_map/all_gather | solution.py:93
  565.5 42.8 %all-gather.5 = bf16[1,6,256,256]{3,2,1,0:T(8,128)(2,1)} all-gather(bf16[1,6,8,256]{3,2,1,0:T(8,128)(2,1)S(1)} %get-tuple-element.973), channel_id=7, replica_groups=mesh['dp'=32] {'dp'}, dimensions={2}, use_global_device_ids=true | all-gather | bytes 811008 | tf_op jit(solution)/shard_map/all_gather | solution.py:89
  608.3 41.6 %all-gather = bf16[1,6,256,256]{3,2,1,0:T(8,128)(2,1)} all-gather(bf16[1,6,8,256]{3,2,1,0:T(8,128)(2,1)S(1)} %get-tuple-element.974), channel_id=2, replica_groups=mesh['dp'=32] {'dp'}, dimensions={2}, use_global_device_ids=true | all-gather | bytes 811008 | tf_op jit(solution)/shard_map/all_gather | solution.py:89
  710.0 42.6 %psum.378 = f32[256]{0:T(256)S(1)} all-reduce(f32[256]{0:T(256)S(1)} %get-tuple-element.625), channel_id=1, replica_groups=mesh['dp'=32] {'dp'}, use_global_device_ids=true, to_apply=%region_7.8 | all-reduce | flops 256 | bytes 2048 | tf_op jit(solution)/shard_map/psum | solution.py:60
  801.0 41.8 %psum.380 = f32[256]{0:T(256)S(1)} all-reduce(f32[256]{0:T(256)S(1)} %multiply_reduce_fusion.292), channel_id=1, replica_groups=mesh['dp'=32] {'dp'}, use_global_device_ids=true, to_apply=%region_11.12 | all-reduce | flops 256 | bytes 2048 | tf_op jit(solution)/shard_map/psum | solution.py:60
  890.6 41.6 %psum.382 = f32[256]{0:T(256)S(1)} all-reduce(f32[256]{0:T(256)S(1)} %multiply_reduce_fusion.290), channel_id=1, replica_groups=mesh['dp'=32] {'dp'}, use_global_device_ids=true, to_apply=%region_15.16 | all-reduce | flops 256 | bytes 2048 | tf_op jit(solution)/shard_map/psum | solution.py:60
  980.6 41.7 %psum.384 = f32[256]{0:T(256)S(1)} all-reduce(f32[256]{0:T(256)S(1)} %multiply_reduce_fusion.288), channel_id=1, replica_groups=mesh['dp'=32] {'dp'}, use_global_device_ids=true, to_apply=%region_19.20 | all-reduce | flops 256 | bytes 2048 | tf_op jit(solution)/shard_map/psum | solution.py:60
  1072.2 41.5 %all-reduce.549 = (f32[256]{0:T(256)S(1)}, f32[256]{0:T(256)S(1)}) all-reduce(f32[256]{0:T(256)S(1)} %multiply_reduce_fusion.286, f32[256]{0:T(256)S(1)} %copy-done.865), channel_id=1, replica_groups=mesh['dp'=32] {'dp'}, use_global_device_ids=true, to_apply=%region_23.24 | all-reduce | flops 512 | bytes 4096 | tf_op jit(solution)/shard_map/psum | solution.py:60
  1123.5 38.6 %psum.399 = f32[256]{0:T(256)S(1)} all-reduce(f32[256]{0:T(256)S(1)} %get-tuple-element.1073), channel_id=1, replica_groups=mesh['dp'=32] {'dp'}, use_global_device_ids=true, to_apply=%region_49.50 | all-reduce | flops 256 | bytes 2048 | tf_op jit(solution)/shard_map/psum | solution.py:57
  1171.6 41.5 %psum.389 = f32[256]{0:T(256)} all-reduce(f32[256]{0:T(256)} %get-tuple-element.623), channel_id=1, replica_groups=mesh['dp'=32] {'dp'}, use_global_device_ids=true, to_apply=%region_29.30 | all-reduce | flops 256 | bytes 2048 | tf_op jit(solution)/shard_map/psum | solution.py:57
  1215.8 39.2 %psum.390 = f32[256]{0:T(256)} all-reduce(f32[256]{0:T(256)} %multiply_reduce_fusion.282), channel_id=1, replica_groups=mesh['dp'=32] {'dp'}, use_global_device_ids=true, to_apply=%region_31.32 | all-reduce | flops 256 | bytes 2048 | tf_op jit(solution)/shard_map/psum | solution.py:60
  1268.5 41.9 %psum.391 = f32[256]{0:T(256)} all-reduce(f32[256]{0:T(256)} %get-tuple-element.1076), channel_id=1, replica_groups=mesh['dp'=32] {'dp'}, use_global_device_ids=true, to_apply=%region_33.34 | all-reduce | flops 256 | bytes 2048 | tf_op jit(solution)/shard_map/psum | solution.py:57
  1314.3 39.2 %psum.392 = f32[256]{0:T(256)} all-reduce(f32[256]{0:T(256)} %multiply_reduce_fusion.280), channel_id=1, replica_groups=mesh['dp'=32] {'dp'}, use_global_device_ids=true, to_apply=%region_35.36 | all-reduce | flops 256 | bytes 2048 | tf_op jit(solution)/shard_map/psum | solution.py:60
  1367.5 41.6 %psum.393 = f32[256]{0:T(256)} all-reduce(f32[256]{0:T(256)} %get-tuple-element.1078), channel_id=1, replica_groups=mesh['dp'=32] {'dp'}, use_global_device_ids=true, to_apply=%region_37.38 | all-reduce | flops 256 | bytes 2048 | tf_op jit(solution)/shard_map/psum | solution.py:57
  1413.1 39.3 %psum.394 = f32[256]{0:T(256)} all-reduce(f32[256]{0:T(256)} %multiply_reduce_fusion.278), channel_id=1, replica_groups=mesh['dp'=32] {'dp'}, use_global_device_ids=true, to_apply=%region_39.40 | all-reduce | flops 256 | bytes 2048 | tf_op jit(solution)/shard_map/psum | solution.py:60
  1466.5 41.6 %psum.395 = f32[256]{0:T(256)} all-reduce(f32[256]{0:T(256)} %get-tuple-element.1080), channel_id=1, replica_groups=mesh['dp'=32] {'dp'}, use_global_device_ids=true, to_apply=%region_41.42 | all-reduce | flops 256 | bytes 2048 | tf_op jit(solution)/shard_map/psum | solution.py:57
  1511.9 39.4 %psum.396 = f32[256]{0:T(256)} all-reduce(f32[256]{0:T(256)} %multiply_reduce_fusion.276), channel_id=1, replica_groups=mesh['dp'=32] {'dp'}, use_global_device_ids=true, to_apply=%region_43.44 | all-reduce | flops 256 | bytes 2048 | tf_op jit(solution)/shard_map/psum | solution.py:60
  1565.2 41.5 %psum.397 = f32[256]{0:T(256)} all-reduce(f32[256]{0:T(256)} %get-tuple-element.1082), channel_id=1, replica_groups=mesh['dp'=32] {'dp'}, use_global_device_ids=true, to_apply=%region_45.46 | all-reduce | flops 256 | bytes 2048 | tf_op jit(solution)/shard_map/psum | solution.py:57
  1610.7 39.8 %all-reduce.548 = (f32[256]{0:T(256)}, f32[256]{0:T(256)}) all-reduce(f32[256]{0:T(256)} %multiply_reduce_fusion.274, f32[256]{0:T(256)} %get-tuple-element.622), channel_id=1, replica_groups=mesh['dp'=32] {'dp'}, use_global_device_ids=true, to_apply=%region_47.48 | all-reduce | flops 512 | bytes 4096 | tf_op jit(solution)/shard_map/psum | solution.py:60
  1665.8 41.4 %all-reduce.547 = (f32[256]{0:T(256)S(1)}, f32[256]{0:T(256)S(1)}) all-reduce(f32[256]{0:T(256)S(1)} %get-tuple-element.335, f32[256]{0:T(256)S(1)} %get-tuple-element.334), channel_id=1, replica_groups=mesh['dp'=32] {'dp'}, use_global_device_ids=true, to_apply=%region_55.56 | all-reduce | flops 512 | bytes 4096 | tf_op jit(solution)/shard_map/psum | solution.py:65
  1724.9 39.1 %all-reduce.546 = (f32[256]{0:T(256)S(1)}, f32[256]{0:T(256)S(1)}) all-reduce(f32[256]{0:T(256)S(1)} %get-tuple-element.333, f32[256]{0:T(256)S(1)} %get-tuple-element.332), channel_id=1, replica_groups=mesh['dp'=32] {'dp'}, use_global_device_ids=true, to_apply=%region_59.60 | all-reduce | flops 512 | bytes 4096 | tf_op jit(solution)/shard_map/psum | solution.py:65
  1781.6 41.2 %all-reduce.545 = (f32[256]{0:T(256)S(1)}, f32[256]{0:T(256)S(1)}) all-reduce(f32[256]{0:T(256)S(1)} %get-tuple-element.331, f32[256]{0:T(256)S(1)} %get-tuple-element.330), channel_id=1, replica_groups=mesh['dp'=32] {'dp'}, use_global_device_ids=true, to_apply=%region_63.64 | all-reduce | flops 512 | bytes 4096 | tf_op jit(solution)/shard_map/psum | solution.py:65
  1839.9 39.3 %all-reduce.544 = (f32[256]{0:T(256)S(1)}, f32[256]{0:T(256)S(1)}) all-reduce(f32[256]{0:T(256)S(1)} %get-tuple-element.329, f32[256]{0:T(256)S(1)} %get-tuple-element.328), channel_id=1, replica_groups=mesh['dp'=32] {'dp'}, use_global_device_ids=true, to_apply=%region_67.68 | all-reduce | flops 512 | bytes 4096 | tf_op jit(solution)/shard_map/psum | solution.py:65
  1895.3 41.8 %all-reduce.543 = (f32[256]{0:T(256)S(1)}, f32[256]{0:T(256)S(1)}, f32[256]{0:T(256)S(1)}, f32[256]{0:T(256)S(1)}) all-reduce(f32[256]{0:T(256)} %get-tuple-element.337, f32[256]{0:T(256)} %get-tuple-element.336, f32[256]{0:T(256)} %get-tuple-element.327, f32[256]{0:T(256)} %get-tuple-element.326), channel_id=1, replica_groups=mesh['dp'=32] {'dp'}, use_global_device_ids=true, to_apply=%region_75.76 | all-reduce | flops 1024 | bytes 8192 | tf_op jit(solution)/shard_map/psum | solution.py:65
  1959.6 39.2 %all-reduce.542 = (f32[256]{0:T(256)S(1)}, f32[256]{0:T(256)S(1)}) all-reduce(f32[256]{0:T(256)S(1)} %get-tuple-element.323, f32[256]{0:T(256)S(1)} %get-tuple-element.322), channel_id=1, replica_groups=mesh['dp'=32] {'dp'}, use_global_device_ids=true, to_apply=%region_79.80 | all-reduce | flops 512 | bytes 4096 | tf_op jit(solution)/shard_map/psum | solution.py:65
  2015.8 41.1 %all-reduce.541 = (f32[256]{0:T(256)S(1)}, f32[256]{0:T(256)S(1)}) all-reduce(f32[256]{0:T(256)S(1)} %get-tuple-element.321, f32[256]{0:T(256)S(1)} %get-tuple-element.320), channel_id=1, replica_groups=mesh['dp'=32] {'dp'}, use_global_device_ids=true, to_apply=%region_83.84 | all-reduce | flops 512 | bytes 4096 | tf_op jit(solution)/shard_map/psum | solution.py:65
  2074.6 39.3 %all-reduce.540 = (f32[256]{0:T(256)S(1)}, f32[256]{0:T(256)S(1)}) all-reduce(f32[256]{0:T(256)S(1)} %get-tuple-element.319, f32[256]{0:T(256)S(1)} %get-tuple-element.318), channel_id=1, replica_groups=mesh['dp'=32] {'dp'}, use_global_device_ids=true, to_apply=%region_87.88 | all-reduce | flops 512 | bytes 4096 | tf_op jit(solution)/shard_map/psum | solution.py:65
  2131.5 41.2 %all-reduce.539 = (f32[256]{0:T(256)S(1)}, f32[256]{0:T(256)S(1)}) all-reduce(f32[256]{0:T(256)S(1)} %get-tuple-element.317, f32[256]{0:T(256)S(1)} %get-tuple-element.316), channel_id=1, replica_groups=mesh['dp'=32] {'dp'}, use_global_device_ids=true, to_apply=%region_91.92 | all-reduce | flops 512 | bytes 4096 | tf_op jit(solution)/shard_map/psum | solution.py:65
  2235.6 84.4 %all-reduce.553.cloned.1.call-done = (f32[256]{0:T(256)}, f32[256]{0:T(256)}, f32[256]{0:T(256)}, f32[256]{0:T(256)}, f32[256,32]{1,0:T(8,128)}, /*index=5*/f32[...) async-done(((f32[256]{0:T(256)}, f32[256]{0:T(256)}, f32[256]{0:T(256)}, f32[256]{0:T(256)}, f32[256,32]{1,0:T(8,128)}, /*index=5*/f32[256,32]{1,0:T(8,128)}, ...) | async-done | bytes 135184 | tf_op jit(solution)/shard_map/psum | solution.py:65
  2592.7 97.5 %reduce-scatter.11.cloned.1.call-done = f32[6,8,256]{2,1,0:T(8,128)} async-done(((f32[6,256,256]{2,1,0:T(8,128)}), f32[6,8,256]{2,1,0:T(8,128)}) %reduce-scatter.11.cloned.1.call-update) | async-done | bytes 49168 | tf_op jit(solution)/shard_map/reduce_scatter | solution.py:109
  2690.2 102.0 %reduce-scatter.9.cloned.1.call-done = f32[6,8,256]{2,1,0:T(8,128)} async-done(((f32[6,256,256]{2,1,0:T(8,128)}), f32[6,8,256]{2,1,0:T(8,128)}) %reduce-scatter.9.cloned.1.call-update) | async-done | bytes 49168 | tf_op jit(solution)/shard_map/reduce_scatter | solution.py:109
  (2161 shorter events, 1305.9 us)
Async XLA Ops:
  7.2 2312.9 %all-reduce.553.cloned.1.call-start = ((), (), s32[]{:S(2)}) async-start(), calls=%async_computation.8 | async-start | bytes 1056768 | tf_op jit(solution)/shard_map/psum | solution.py:65
  10.9 134.0 %copy-start.147 = (f32[2048]{0:T(1024)}, f32[2048]{0:T(1024)S(1)}, u32[]{:S(2)}) copy-start(f32[2048]{0:T(1024)S(1)} %get-tuple-element.699) | copy-start | bytes 24580
  559.5 98.4 %copy-start.56 = (f32[1024,256]{1,0:T(8,128)S(1)}, f32[1024,256]{1,0:T(8,128)}, u32[]{:S(2)}) copy-start(f32[1024,256]{1,0:T(8,128)} %slice.1624) | copy-start | bytes 3145732
  608.3 47.7 %copy-start.248 = (s32[1024]{0:T(1024)S(1)}, s32[1024]{0:T(1024)}, u32[]{:S(2)}) copy-start(s32[1024]{0:T(1024)} %slice.1574) | copy-start | bytes 12292
  608.3 47.7 %copy-start.249 = (s32[1024]{0:T(1024)S(1)}, s32[1024]{0:T(1024)}, u32[]{:S(2)}) copy-start(s32[1024]{0:T(1024)} %slice.1571) | copy-start | bytes 12292
  608.3 47.7 %copy-start.250 = (s32[1024]{0:T(1024)S(1)}, s32[1024]{0:T(1024)}, u32[]{:S(2)}) copy-start(s32[1024]{0:T(1024)} %slice.1568) | copy-start | bytes 12292
  608.3 49.7 %copy-start.52 = (f32[1024,256]{1,0:T(8,128)S(1)}, f32[1024,256]{1,0:T(8,128)}, u32[]{:S(2)}) copy-start(f32[1024,256]{1,0:T(8,128)} %slice.1630) | copy-start | bytes 3145732
  608.3 49.7 %copy-start.54 = (f32[1024,256]{1,0:T(8,128)S(1)}, f32[1024,256]{1,0:T(8,128)}, u32[]{:S(2)}) copy-start(f32[1024,256]{1,0:T(8,128)} %slice.1627) | copy-start | bytes 3145732
  669.5 84.3 %copy-start = (f32[1024,256]{1,0:T(8,128)}, f32[1024,256]{1,0:T(8,128)S(1)}, u32[]{:S(2)}) copy-start(f32[1024,256]{1,0:T(8,128)S(1)} %fusion.86) | copy-start | bytes 3145732
  671.0 84.0 %copy-start.80 = (f32[1024,256]{1,0:T(8,128)}, f32[1024,256]{1,0:T(8,128)S(1)}, u32[]{:S(2)}) copy-start(f32[1024,256]{1,0:T(8,128)S(1)} %get-tuple-element.1063) | copy-start | bytes 3145732
  671.0 81.6 %copy-start.222 = (f32[256]{0:T(256)S(1)}, f32[256]{0:T(256)}, u32[]{:S(2)}) copy-start(f32[256]{0:T(256)} %get-tuple-element.490) | copy-start | bytes 3076
  671.0 83.4 %copy-start.278 = (f32[256]{0:T(256)S(1)}, f32[256]{0:T(256)}, u32[]{:S(2)}) copy-start(f32[256]{0:T(256)} %get-tuple-element.496) | copy-start | bytes 3076
  761.4 81.4 %copy-start.224 = (f32[256]{0:T(256)S(1)}, f32[256]{0:T(256)}, u32[]{:S(2)}) copy-start(f32[256]{0:T(256)} %get-tuple-element.489) | copy-start | bytes 3076
  761.4 82.8 %copy-start.280 = (f32[256]{0:T(256)S(1)}, f32[256]{0:T(256)}, u32[]{:S(2)}) copy-start(f32[256]{0:T(256)} %get-tuple-element.495) | copy-start | bytes 3076
  761.8 82.7 %copy-start.18 = (f32[1024,256]{1,0:T(8,128)}, f32[1024,256]{1,0:T(8,128)S(1)}, u32[]{:S(2)}) copy-start(f32[1024,256]{1,0:T(8,128)S(1)} %get-tuple-element.1065) | copy-start | bytes 3145732
  850.9 81.3 %copy-start.228 = (f32[256]{0:T(256)S(1)}, f32[256]{0:T(256)}, u32[]{:S(2)}) copy-start(f32[256]{0:T(256)} %get-tuple-element.488) | copy-start | bytes 3076
  850.9 82.8 %copy-start.282 = (f32[256]{0:T(256)S(1)}, f32[256]{0:T(256)}, u32[]{:S(2)}) copy-start(f32[256]{0:T(256)} %get-tuple-element.494) | copy-start | bytes 3076
  851.4 82.7 %copy-start.20 = (f32[1024,256]{1,0:T(8,128)}, f32[1024,256]{1,0:T(8,128)S(1)}, u32[]{:S(2)}) copy-start(f32[1024,256]{1,0:T(8,128)S(1)} %get-tuple-element.1067) | copy-start | bytes 3145732
  940.5 81.8 %copy-start.230 = (f32[256]{0:T(256)S(1)}, f32[256]{0:T(256)}, u32[]{:S(2)}) copy-start(f32[256]{0:T(256)} %get-tuple-element.487) | copy-start | bytes 3076
  940.5 83.2 %copy-start.306 = (f32[256]{0:T(256)S(1)}, f32[256]{0:T(256)}, u32[]{:S(2)}) copy-start(f32[256]{0:T(256)} %get-tuple-element.493) | copy-start | bytes 3076
  1031.4 82.3 %copy-start.407 = (f32[256]{0:T(256)S(1)}, f32[256]{0:T(256)}, u32[]{:S(2)}) copy-start(f32[256]{0:T(256)} %get-tuple-element.486) | copy-start | bytes 3076
  1031.4 83.5 %copy-start.790 = (f32[256]{0:T(256)S(1)}, f32[256]{0:T(256)}, u32[]{:S(2)}) copy-start(f32[256]{0:T(256)} %get-tuple-element.492) | copy-start | bytes 3076
  1031.4 83.5 %copy-start.888 = (f32[2]{0:T(128)S(1)}, f32[2]{0:T(128)}, u32[]{:S(2)}) copy-start(f32[2]{0:T(128)} %convert_multiply_fusion.1) | copy-start | bytes 28
  1032.7 84.6 %copy-start.25 = (f32[1024,256]{1,0:T(8,128)}, f32[1024,256]{1,0:T(8,128)S(1)}, u32[]{:S(2)}) copy-start(f32[1024,256]{1,0:T(8,128)S(1)} %get-tuple-element.1071) | copy-start | bytes 3145732
  2190.9 365.5 %reduce-scatter.7.cloned.1.call-start = ((), (), s32[]{:S(2)}) async-start(), calls=%async_computation.5 | async-start | bytes 1081344 | tf_op jit(solution)/shard_map/reduce_scatter | solution.py:108
  2219.8 371.5 %reduce-scatter.5.cloned.1.call-start = ((), (), s32[]{:S(2)}) async-start(), calls=%async_computation.4 | async-start | bytes 1081344 | tf_op jit(solution)/shard_map/reduce_scatter | solution.py:108
  2233.5 86.5 %copy-start.82 = (f32[1024,256]{1,0:T(8,128)S(1)}, f32[1024,256]{1,0:T(8,128)}, u32[]{:S(2)}) copy-start(f32[1024,256]{1,0:T(8,128)} %copy-done.80) | copy-start | bytes 3145732
  2233.5 86.5 %copy-start.866 = (f32[256]{0:T(256)S(1)}, f32[256]{0:T(256)}, u32[]{:S(2)}) copy-start(f32[256]{0:T(256)} %get-tuple-element.663) | copy-start | bytes 3076
  2233.5 86.5 %copy-start.867 = (f32[256]{0:T(256)S(1)}, f32[256]{0:T(256)}, u32[]{:S(2)}) copy-start(f32[256]{0:T(256)} %get-tuple-element.665) | copy-start | bytes 3076
  2233.6 86.5 %copy-start.870 = (f32[256]{0:T(256)S(1)}, f32[256]{0:T(256)}, u32[]{:S(2)}) copy-start(f32[256]{0:T(256)} %copy-done.868) | copy-start | bytes 3076
  2346.9 343.3 %reduce-scatter.11.cloned.1.call-start = ((), (), s32[]{:S(2)}) async-start(), calls=%async_computation.7 | async-start | bytes 1622016 | tf_op jit(solution)/shard_map/reduce_scatter | solution.py:109
  2349.2 443.0 %reduce-scatter.9.cloned.1.call-start = ((), (), s32[]{:S(2)}) async-start(), calls=%async_computation.6 | async-start | bytes 1622016 | tf_op jit(solution)/shard_map/reduce_scatter | solution.py:109
  (864 other events, 4430.3 us)
Sparse Core Ops, SparseCore 0:
  2191.0 128.9 all-reduce.552
  2322.4 135.8 reduce-scatter.6
  2460.6 130.7 reduce-scatter.4
  2597.3 92.9 reduce-scatter.10
  2696.1 96.0 reduce-scatter.8
where the time goes:
time: 2810 us; the launch traced here: 2800 us
  blocking collectives  1680 us (60%)
  local copies, waits for them, and re-layouts  366 us (13%)
  other arithmetic  322 us (11%)
  waiting for transfers between devices  318 us (11%)
  matrix products  90 us (3%)
    psum x11, blocking collectives, statistics(): lax.psum((jnp.sum(product * valid_out, axis=0), local_count), 'dp')  438 us
    psum x10, blocking collectives, statistics(): lax.psum(jnp.sum(centered * centered, axis=0), 'dp') / frame_total  406 us
    psum x9, blocking collectives, norm_back(): lax.psum((jnp.sum(grad_z, axis=0), jnp.sum(grad_z * normed, axis=0)), 'dp')  364 us
    reduce_scatter x2, waiting for transfers between devices, reduce_grads(): lax.psum_scatter(grads[1], 'dp', scatter_dimension=1, tiled=True)  200 us
    pad x19, local copies, waits for them, and re-layouts, depthwise(): window = lax.slice(padded, (k, 0), (slice_end, channels), (stride, 1))  127 us
    slice x25, local copies, waits for them, and re-layouts, depthwise(): window = lax.slice(padded, (k, 0), (slice_end, channels), (stride, 1))  88.3 us
    psum x1, waiting for transfers between devices, norm_back(): lax.psum((jnp.sum(grad_z, axis=0), jnp.sum(grad_z * normed, axis=0)), 'dp')  84.4 us
    all_gather x2, blocking collectives, fetch(): lax.all_gather(point[block_index], 'dp', axis=1, tiled=True)  84.4 us
  transfers between devices with their start and end apart: 5, of which 4 were waited for; matrix products, arithmetic and copies ran while one was open for 10% of the time, Pallas kernels for 0%

commit v1 on v0

v1 whole, which is shorter than its diff:
```python
import functools

import jax
import jax.numpy as jnp
from jax import lax
from jax.experimental import pallas as pl
from jax.experimental.pallas import tpu as pltpu
from jax.sharding import PartitionSpec as P

EPSILON = 1e-05
HIGHEST = lax.Precision.HIGHEST
F32 = jnp.float32
BF16 = jnp.bfloat16
MESH = pl.DeviceIdType.MESH

GAP = 16
HALO = 13
LANES = 128


def sigmoid(v):
    return 0.5 * jnp.tanh(0.5 * v) + 0.5


class Plan:
    def __init__(self, slots, channels, taps_first, taps_second, sub_blocks, hidden, devices):
        self.slots = slots
        self.steps = (slots + GAP) // 8
        self.rows = 8 * self.steps
        self.channels = channels
        self.halves = channels // LANES
        self.taps = (taps_first, taps_second)
        self.max_taps = max(self.taps)
        self.sub = sub_blocks
        self.hidden = hidden
        self.devices = devices
        self.block = next(r for r in (26, 10, 2) if self.steps % r == 0)
        self.fine = next(r for r in (10, 26, 2) if self.steps % r == 0)
        self.pad = self.steps + 2 * HALO


def peers_of(me, n):
    if n != 32:
        return [lax.rem(me + k, n) for k in range(1, n)]
    core = lax.rem(me, 2)
    x = lax.rem(me // 2, 2)
    y = lax.rem(me // 4, 2)
    z = me // 8
    found = []
    for order, other in enumerate((3 - z, lax.rem(z + 2, 4), z + 1 - 2 * lax.rem(z, 2), z)):
        for dy in (1, 0):
            for dx in (1, 0):
                for dc in (0, 1):
                    if order == 3 and dy == 0 and dx == 0 and dc == 0:
                        continue
                    oy = lax.rem(y + dy, 2)
                    ox = lax.rem(x + dx, 2)
                    oc = lax.rem(core + dc, 2)
                    found.append((dy + dx + (3, 2, 1, 0)[order], other * 8 + oy * 4 + ox * 2 + oc))
    found.sort(key=lambda item: -item[0])
    return [item[1] for item in found]


def kernel(plan, lens, frames, cot, dw, point, gains, shifts, squeeze_t, expand,
           out, frames_grad, dw_grad, point_grad, gains_grad, shifts_grad, squeeze_grad, expand_grad,
           hid, acts, prods, gd, gz, gpb, gqb, pre, flat, wide, first_mask, second_mask, valid,
           stats, send4, recv4, counts, csend, send_sem, recv_sem, count_sems):
    N = plan.devices
    Q, R, RF = plan.steps, plan.block, plan.fine
    HV = range(plan.halves)
    SUB = plan.sub
    me = lax.axis_index("dp")
    peers = peers_of(me, N)

    barrier = pltpu.get_barrier_semaphore()
    for peer in peers:
        pl.semaphore_signal(barrier, inc=1, device_id=(peer,), device_id_type=MESH)

    len0 = lens[0]
    len1 = lens[1]
    half0 = len0 // 2
    half1 = len1 // 2
    count = (half0 + half1).astype(F32)
    inv_half = (1.0 / jnp.full((1, LANES), half0, jnp.int32).astype(F32),
                1.0 / jnp.full((1, LANES), half1, jnp.int32).astype(F32))

    def steps_loop(width, body, init=0):
        return lax.fori_loop(0, Q // width, lambda i, c: body(i * width, c), init)

    def mask_body(t0, c):
        step = t0 + lax.broadcasted_iota(jnp.int32, (RF, 8, LANES), 0)
        slot = step + Q * lax.broadcasted_iota(jnp.int32, (RF, 8, LANES), 1)
        a = (slot < half0).astype(F32)
        b = jnp.logical_and(slot >= half0 + GAP, slot < half0 + GAP + half1).astype(F32)
        first_mask[pl.ds(t0, RF)] = a
        second_mask[pl.ds(t0, RF)] = b
        valid[pl.ds(t0, RF)] = a + b
        return c

    steps_loop(RF, mask_body)

    top = 2 * GAP + 2 * plan.slots
    for h in HV:
        wide[h, 0:2 * GAP] = jnp.zeros((2 * GAP, LANES), F32)
        wide[h, top:] = jnp.zeros((wide.shape[1] - top, LANES), F32)

    def widen(i, c):
        rows = pl.ds(pl.multiple_of(i * 128, 128), 128)
        for h in HV:
            values = frames[rows, h * LANES:(h + 1) * LANES].astype(F32)
            wide[h, pl.ds(pl.multiple_of(i * 128 + 2 * GAP, 32), 128)] = values
        return c

    lax.fori_loop(0, 2 * plan.slots // 128, widen, 0)

    def set_halo(ref, half):
        sub = lax.broadcasted_iota(jnp.int32, (HALO, 8, LANES), 1)
        low = pltpu.roll(ref[half, pl.ds(Q, HALO)], 1, 1)
        ref[half, pl.ds(0, HALO)] = jnp.where(sub == 0, 0.0, low)
        high = pltpu.roll(ref[half, pl.ds(HALO, HALO)], 7, 1)
        ref[half, pl.ds(HALO + Q, HALO)] = jnp.where(sub == 7, 0.0, high)

    for phase in range(2):
        def deinterleave(t0, c):
            for j in range(RF):
                a_mask = first_mask[t0 + j]
                b_mask = second_mask[t0 + j]
                for h in HV:
                    a = wide[h, pl.ds(2 * (t0 + j) + 2 * GAP + phase, 8, stride=2 * Q)]
                    b = wide[h, pl.ds(2 * (t0 + j) + phase, 8, stride=2 * Q)]
                    hid[phase, h, HALO + t0 + j] = a * a_mask + b * b_mask
            return c
        steps_loop(RF, deinterleave)
        for h in HV:
            set_halo(hid.at[phase], h)

    csend[...] = jnp.full((4, LANES), count, F32)
    pl.semaphore_wait(barrier, N - 1)

    def send_to_all(src, dst, ssem, rsem):
        for peer in peers:
            pltpu.make_async_remote_copy(src_ref=src, dst_ref=dst, send_sem=ssem, recv_sem=rsem,
                                         device_id=(peer,), device_id_type=MESH).start()

    def wait_all(ref, sem):
        view = ref.at[pl.ds(0, N - 1)]
        pltpu.make_async_copy(view, view, sem).wait()

    send_to_all(csend, counts.at[me], count_sems.at[0], count_sems.at[1])
    counts[me] = csend[...]

    def exchange(slot, place, rows):
        send4[slot] = rows
        recv4[place, me] = rows
        send_to_all(send4.at[slot], recv4.at[place, me], send_sem.at[slot], recv_sem.at[slot])

    def received(slot, place):
        wait_all(recv4.at[place], recv_sem.at[slot])
        return recv4[place]

    def back_place(index):
        return lax.rem(index + SUB, 2 * SUB)

    def row(values):
        return values.reshape(1, 1, LANES)

    def accumulate(rows3):
        return jnp.sum(rows3, axis=0)

    def local_stats(index):
        def total(t0, c):
            v = valid[pl.ds(t0, R)]
            return tuple(c[h] + accumulate(prods[index, h, pl.ds(t0, R)] * v) for h in HV)
        zeros = tuple(jnp.zeros((8, LANES), F32) for h in HV)
        sums = steps_loop(R, total, zeros)
        means = [jnp.sum(sums[h], axis=0, keepdims=True) / jnp.full((1, LANES), count, F32) for h in HV]

        def squares(t0, c):
            v = valid[pl.ds(t0, R)]
            res = []
            for h in HV:
                d = (prods[index, h, pl.ds(t0, R)] - row(means[h])) * v
                res.append(c[h] + accumulate(d * d))
            return tuple(res)
        sq = steps_loop(R, squares, zeros)
        return jnp.concatenate(means + [jnp.sum(sq[h], axis=0, keepdims=True) for h in HV], axis=0)

    def merge_stats(slot, index):
        got = received(slot, slot)
        weight = counts[...]
        total = jnp.sum(weight, axis=0)
        mean = jnp.sum(weight * got, axis=0) / total
        mean4 = jnp.concatenate([mean[0:2], mean[0:2]], axis=0)
        diff = got - mean4
        between = jnp.sum(weight * diff * diff, axis=0)
        within = jnp.sum(got, axis=0)
        var = (within[2:4] + between[0:2]) / total[0:2]
        inv = lax.rsqrt(var + EPSILON)
        scale = inv * gains[index]
        offset = shifts[index] - mean[0:2] * scale
        stats[index] = jnp.concatenate([mean[0:2], inv, scale, offset], axis=0)

    def stat_row(index, kind, h):
        return row(stats[index, pl.ds(2 * kind + h, 1)])

    def layer_conv(index, pieces):
        def body(t0, c):
            for h in HV:
                acc = None
                for source, taps in pieces:
                    low = min(s for _, s in taps)
                    high = max(s for _, s in taps)
                    win = hid[source, h, pl.ds(t0 + HALO + low, R + high - low)]
                    for tap, shift in taps:
                        term = win[shift - low:shift - low + R] * dw[index, h, pl.ds(tap, 1)].reshape(1, 1, LANES)
                        acc = term if acc is None else acc + term
                rows = pl.ds(pl.multiple_of(8 * t0, 16), 8 * R)
                acts[index, rows, h * LANES:(h + 1) * LANES] = acc.reshape(8 * R, LANES).astype(BF16)
            return c
        steps_loop(R, body)

    def pointwise(act, index):
        def body(t0, c):
            rows = pl.ds(pl.multiple_of(8 * t0, 16), 8 * R)
            res = jnp.dot(acts[act, rows], point[index], preferred_element_type=F32)
            for h in HV:
                prods[index, h, pl.ds(t0, R)] = res[:, h * LANES:(h + 1) * LANES].reshape(R, 8, LANES)
            return c
        steps_loop(R, body)

    def activate(index, target):
        scales = [stat_row(index, 2, h) for h in HV]
        offsets = [stat_row(index, 3, h) for h in HV]

        def body(t0, c):
            v = valid[pl.ds(t0, RF)]
            for h in HV:
                z = prods[index, h, pl.ds(t0, RF)] * scales[h] + offsets[h]
                hid[target, h, pl.ds(HALO + t0, RF)] = z * sigmoid(z) * v
            return c
        steps_loop(RF, body)
        for h in HV:
            set_halo(hid.at[target], h)

    def block_pieces(b, r):
        taps = plan.taps[b]
        margin = (taps - 1) // 2
        if b == 0 and r == 0:
            even = [(k, (k - margin) // 2) for k in range(taps) if (k - margin) % 2 == 0]
            odd = [(k, (k - margin - 1) // 2) for k in range(taps) if (k - margin) % 2 == 1]
            return [(0, even), (1, odd)]
        return [(b * SUB + r + 1, [(k, k - margin) for k in range(taps)])]

    def residual_input(b):
        source = 0 if b == 0 else SUB + 1

        def body(t0, c):
            rows = pl.ds(pl.multiple_of(8 * t0, 16), 8 * R)
            for h in HV:
                values = hid[source, h, pl.ds(HALO + t0, R)].reshape(8 * R, LANES)
                acts[2 * SUB + b, rows, h * LANES:(h + 1) * LANES] = values.astype(BF16)
            return c
        steps_loop(R, body)

    def pair_rows(values):
        return jnp.concatenate([values, jnp.zeros((6, plan.channels), F32)], axis=0)

    def small(a, b, dims):
        return lax.dot_general(a, b, (dims, ((), ())), precision=HIGHEST, preferred_element_type=F32)

    def excite(b):
        last = b * SUB + SUB - 1
        scales = [stat_row(last, 2, h) for h in HV]
        offsets = [stat_row(last, 3, h) for h in HV]

        def sums(t0, c):
            a, s = first_mask[pl.ds(t0, RF)], second_mask[pl.ds(t0, RF)]
            res = []
            for h in HV:
                z = prods[last, h, pl.ds(t0, RF)] * scales[h] + offsets[h]
                res.append(c[2 * h] + accumulate(z * a))
                res.append(c[2 * h + 1] + accumulate(z * s))
            return tuple(res)
        tot = steps_loop(RF, sums, tuple(jnp.zeros((8, LANES), F32) for _ in range(2 * plan.halves)))
        means = jnp.concatenate(
            [jnp.concatenate([jnp.sum(tot[2 * h + u], axis=0, keepdims=True) * inv_half[u] for h in HV], axis=1)
             for u in range(2)], axis=0)
        means = pair_rows(means)
        inner = small(means, squeeze_t[b], ((1,), (1,)))
        excited = inner * sigmoid(inner)
        gate = sigmoid(small(excited, expand[b], ((1,), (0,))))
        return means, inner, excited, gate

    def gate_rows(gate):
        return [[row(gate[u:u + 1, h * LANES:(h + 1) * LANES]) for h in HV] for u in range(2)]

    def tail(b, gate, store):
        last, res = b * SUB + SUB - 1, 2 * SUB + b
        gates = gate_rows(gate)
        consts = [(stat_row(last, 2, h), stat_row(last, 3, h), stat_row(res, 2, h), stat_row(res, 3, h)) for h in HV]

        def body(t0, c):
            v = valid[pl.ds(t0, RF)]
            a = first_mask[pl.ds(t0, RF)]
            for h in HV:
                s1, o1, s2, o2 = consts[h]
                z = prods[last, h, pl.ds(t0, RF)] * s1 + o1
                y = prods[res, h, pl.ds(t0, RF)] * s2 + o2
                g = jnp.where(a > 0.5, gates[0][h], gates[1][h])
                s = z * g + y
                pre[b, h, pl.ds(t0, RF)] = s
                store(t0, h, s * sigmoid(s) * v)
            return c
        steps_loop(RF, body)

    def forward_block(b):
        def layer(r, pieces):
            index = b * SUB + r
            layer_conv(index, pieces)
            pointwise(index, index)
            exchange(index, index, local_stats(index))
        layer(0, block_pieces(b, 0))
        residual_input(b)
        pointwise(2 * SUB + b, 2 * SUB + b)
        exchange(2 * SUB + b, 2 * SUB + b, local_stats(2 * SUB + b))
        merge_stats(b * SUB, b * SUB)
        activate(b * SUB, b * SUB + 2)

        def rest(r, c):
            taps = plan.taps[b]
            margin = (taps - 1) // 2
            index = b * SUB + r
            layer(r, [(index + 1, [(k, k - margin) for k in range(taps)])])
            merge_stats(index, index)

            @pl.when(r < SUB - 1)
            def _():
                activate(index, index + 2)
            return c
        lax.fori_loop(1, SUB, rest, 0)
        merge_stats(2 * SUB + b, 2 * SUB + b)
        return excite(b)

    back_slot = 2 * SUB + 2

    def sum_rows(parts):
        return jnp.concatenate([jnp.sum(part, axis=0, keepdims=True) for part in parts], axis=0)

    def tail_back(b, kept, load):
        means, inner, excited, gate = kept
        last, res = b * SUB + SUB - 1, 2 * SUB + b
        gates = gate_rows(gate)
        consts = [(stat_row(last, 2, h), stat_row(last, 3, h)) for h in HV]

        def first(t0, c):
            v = valid[pl.ds(t0, RF)]
            a, q = first_mask[pl.ds(t0, RF)], second_mask[pl.ds(t0, RF)]
            out_c = []
            for h in HV:
                s = pre[b, h, pl.ds(t0, RF)]
                sg = sigmoid(s)
                gs = load(t0, h) * (sg * (1.0 + s * (1.0 - sg))) * v
                pre[b, h, pl.ds(t0, RF)] = gs
                z = prods[last, h, pl.ds(t0, RF)] * consts[h][0] + consts[h][1]
                gsz = gs * z
                out_c.append(c[2 * h] + accumulate(gsz * a))
                out_c.append(c[2 * h + 1] + accumulate(gsz * q))
            return tuple(out_c)
        zero4 = tuple(jnp.zeros((8, LANES), F32) for _ in range(2 * plan.halves))
        tot = steps_loop(RF, first, zero4)
        grad_gate = pair_rows(jnp.concatenate(
            [jnp.concatenate([jnp.sum(tot[2 * h + u], axis=0, keepdims=True) for h in HV], axis=1)
             for u in range(2)], axis=0))
        grad_up = grad_gate * gate * (1.0 - gate)
        expand_grad[b] = small(excited, grad_up, ((0,), (0,)))
        grad_excited = small(grad_up, expand[b], ((1,), (1,)))
        sg = sigmoid(inner)
        grad_inner = grad_excited * (sg * (1.0 + inner * (1.0 - sg)))
        squeeze_grad[b] = small(grad_inner, means, ((0,), (0,)))
        grad_means = small(grad_inner, squeeze_t[b], ((1,), (0,)))
        mean_rows = [[row(grad_means[u:u + 1, h * LANES:(h + 1) * LANES] * inv_half[u]) for h in HV]
                     for u in range(2)]
        norm1 = [(stat_row(last, 0, h), stat_row(last, 1, h)) for h in HV]
        norm2 = [(stat_row(res, 0, h), stat_row(res, 1, h)) for h in HV]

        def second(t0, c):
            a = first_mask[pl.ds(t0, RF)]
            v = valid[pl.ds(t0, RF)]
            out_c = []
            for h in HV:
                gs = pre[b, h, pl.ds(t0, RF)]
                g = jnp.where(a > 0.5, gates[0][h], gates[1][h])
                m = jnp.where(a > 0.5, mean_rows[0][h], mean_rows[1][h])
                grad = gs * g + m * v
                gz[h, pl.ds(t0, RF)] = grad
                x1 = (prods[last, h, pl.ds(t0, RF)] - norm1[h][0]) * norm1[h][1]
                x2 = (prods[res, h, pl.ds(t0, RF)] - norm2[h][0]) * norm2[h][1]
                out_c += [c[4 * h] + accumulate(grad), c[4 * h + 1] + accumulate(grad * x1),
                          c[4 * h + 2] + accumulate(gs), c[4 * h + 3] + accumulate(gs * x2)]
            return tuple(out_c)
        tot = steps_loop(RF, second, zero4 + zero4)
        exchange(back_slot + last, back_place(last), sum_rows([tot[0], tot[4], tot[1], tot[5]]))
        exchange(back_slot + res, 2 * SUB + 1 - b, sum_rows([tot[2], tot[6], tot[3], tot[7]]))

    def norm_back(index, place, load, target):
        sums = jnp.sum(received(back_slot + index, place), axis=0)
        shifts_grad[index] = sums[0:2]
        gains_grad[index] = sums[2:4]
        total = jnp.sum(counts[...], axis=0)[0:2]
        st = stats[index]
        mean, inv, scale = st[0:2], st[2:4], st[4:6]
        k1 = scale * sums[0:2] / total
        k2 = scale * sums[2:4] / total * inv
        rows3 = [[row(value[h:h + 1]) for value in (mean, scale, k1, k2)] for h in HV]

        def body(t0, c):
            v = valid[pl.ds(t0, R)]
            rows = pl.ds(pl.multiple_of(8 * t0, 16), 8 * R)
            for h in HV:
                mean_h, scale_h, k1_h, k2_h = rows3[h]
                grad = (scale_h * load(t0, h) - k1_h - k2_h * (prods[index, h, pl.ds(t0, R)] - mean_h)) * v
                target[rows, h * LANES:(h + 1) * LANES] = grad.reshape(8 * R, LANES).astype(BF16)
            return c
        steps_loop(R, body)

    def pointwise_back(index, source, store):
        def body(t0, c):
            rows = pl.ds(pl.multiple_of(8 * t0, 16), 8 * R)
            res = lax.dot_general(source[rows], point[index], (((1,), (1,)), ((), ())), preferred_element_type=F32)
            for h in HV:
                store(t0, h, res[:, h * LANES:(h + 1) * LANES].reshape(R, 8, LANES))
            return c
        steps_loop(R, body)

    def point_back(index, act, source):
        point_grad[index] = lax.dot_general(acts[act], source[...], (((0,), (0,)), ((), ())),
                                            preferred_element_type=F32)

    def store_gd(t0, h, values):
        gd[h, pl.ds(HALO + t0, R)] = values

    def conv_back_block(t0, h, index, taps):
        low = min(-s for _, s in taps)
        high = max(-s for _, s in taps)
        win = gd[h, pl.ds(t0 + HALO + low, R + high - low)]
        acc = None
        for tap, shift in taps:
            term = win[-shift - low:-shift - low + R] * dw[index, h, pl.ds(tap, 1)].reshape(1, 1, LANES)
            acc = term if acc is None else acc + term
        return acc

    def kernel_back(index, pieces):
        for source, taps in pieces:
            for h in HV:
                low = min(s for _, s in taps)
                high = max(s for _, s in taps)

                def body(t0, c):
                    g = gd[h, pl.ds(HALO + t0, RF)]
                    win = hid[source, h, pl.ds(t0 + HALO + low, RF + high - low)]
                    return tuple(acc + accumulate(g * win[s - low:s - low + RF]) for acc, (_, s) in zip(c, taps))
                accs = steps_loop(RF, body, tuple(jnp.zeros((8, LANES), F32) for _ in taps))
                for acc, (tap, _) in zip(accs, taps):
                    dw_grad[index, h, pl.ds(tap, 1)] = jnp.sum(acc, axis=0, keepdims=True)

    def hidden_back(index, taps):
        before = index - 1
        consts = [[stat_row(before, kind, h) for kind in range(4)] for h in HV]

        def body(t0, c):
            v = valid[pl.ds(t0, R)]
            res = []
            for h in HV:
                mean, inv, scale, offset = consts[h]
                p = prods[before, h, pl.ds(t0, R)]
                z = p * scale + offset
                sg = sigmoid(z)
                grad = conv_back_block(t0, h, index, taps) * (sg * (1.0 + z * (1.0 - sg))) * v
                gz[h, pl.ds(t0, R)] = grad
                xhat = (p - mean) * inv
                res += [c[2 * h] + accumulate(grad), c[2 * h + 1] + accumulate(grad * xhat)]
            return tuple(res)
        tot = steps_loop(R, body, tuple(jnp.zeros((8, LANES), F32) for _ in range(2 * plan.halves)))
        exchange(back_slot + before, back_place(before), sum_rows([tot[0], tot[2], tot[1], tot[3]]))

    def load_gz(t0, h):
        return gz[h, pl.ds(t0, R)]

    def backward_block(b):
        taps = plan.taps[b]
        margin = (taps - 1) // 2
        regular = [(k, k - margin) for k in range(taps)]
        res = 2 * SUB + b

        def step(j, c):
            r = SUB - 1 - j
            index = b * SUB + r
            norm_back(index, back_place(index), load_gz, gpb)
            pointwise_back(index, gpb, store_gd)
            for h in HV:
                set_halo(gd, h)
            hidden_back(index, regular)
            point_back(index, index, gpb)
            kernel_back(index, [(index + 1, regular)])
            return c
        lax.fori_loop(0, SUB - 1, step, 0)
        norm_back(res, 2 * SUB + 1 - b, lambda t0, h: pre[b, h, pl.ds(t0, R)], gqb)
        point_back(res, res, gqb)
        index = b * SUB
        norm_back(index, back_place(index), load_gz, gpb)
        pointwise_back(index, gpb, store_gd)
        for h in HV:
            set_halo(gd, h)

    wait_all(counts, count_sems.at[1])
    kept_first = forward_block(0)

    def store_middle(t0, h, values):
        hid[SUB + 1, h, pl.ds(HALO + t0, RF)] = values
    tail(0, kept_first[3], store_middle)
    for h in HV:
        set_halo(hid.at[SUB + 1], h)
    kept_second = forward_block(1)

    def store_out(t0, h, values):
        for j in range(RF):
            flat[h, pl.ds(t0 + j, 8, stride=Q)] = values[j]
    tail(1, kept_second[3], store_out)

    def ungap(i, c):
        rows = pl.ds(pl.multiple_of(i * 128, 128), 128)
        slot = i * 128 + lax.broadcasted_iota(jnp.int32, (128, LANES), 0)
        for h in HV:
            moved = flat[h, pl.ds(pl.multiple_of(i * 128 + GAP, 16), 128)]
            out[rows, h * LANES:(h + 1) * LANES] = jnp.where(slot < half0, flat[h, rows], moved)
        return c
    lax.fori_loop(0, plan.slots // 128, ungap, 0)

    for h in HV:
        flat[h, 0:GAP] = jnp.zeros((GAP, LANES), F32)
        flat[h, GAP + plan.slots:] = jnp.zeros((flat.shape[1] - GAP - plan.slots, LANES), F32)

    def place(i, c):
        rows = pl.ds(pl.multiple_of(i * 128, 128), 128)
        for h in HV:
            flat[h, pl.ds(pl.multiple_of(i * 128 + GAP, 16), 128)] = cot[rows, h * LANES:(h + 1) * LANES]
        return c
    lax.fori_loop(0, plan.slots // 128, place, 0)

    def load_cot(t0, h):
        parts = []
        for j in range(RF):
            a = flat[h, pl.ds(t0 + j + GAP, 8, stride=Q)]
            b = flat[h, pl.ds(t0 + j, 8, stride=Q)]
            parts.append(jnp.where(first_mask[t0 + j] > 0.5, a, b))
        return jnp.stack(parts, axis=0)

    tail_back(1, kept_second, load_cot)
    backward_block(1)
    margin = (plan.taps[1] - 1) // 2
    regular = [(k, k - margin) for k in range(plan.taps[1])]

    def store_gz(t0, h, values):
        gz[h, pl.ds(t0, R)] = values
    pointwise_back(2 * SUB + 1, gqb, store_gz)

    def middle(t0, c):
        for h in HV:
            gz[h, pl.ds(t0, R)] = gz[h, pl.ds(t0, R)] + conv_back_block(t0, h, SUB, regular)
        return c
    steps_loop(R, middle)
    tail_back(0, kept_first, lambda t0, h: gz[h, pl.ds(t0, RF)])
    point_back(SUB, SUB, gpb)
    kernel_back(SUB, [(SUB + 1, regular)])
    backward_block(0)
    pieces = block_pieces(0, 0)
    pointwise_back(2 * SUB, gqb, store_gz)

    def spread(t0, c):
        v = valid[pl.ds(t0, R)]
        for h in HV:
            even = (conv_back_block(t0, h, 0, pieces[0][1]) + gz[h, pl.ds(t0, R)]) * v
            odd = conv_back_block(t0, h, 0, pieces[1][1]) * v
            for j in range(R):
                wide[h, pl.ds(2 * (t0 + j), 8, stride=2 * Q)] = even[j]
                wide[h, pl.ds(2 * (t0 + j) + 1, 8, stride=2 * Q)] = odd[j]
        return c
    steps_loop(R, spread)

    def ungap_wide(i, c):
        rows = pl.ds(pl.multiple_of(i * 128, 128), 128)
        slot = i * 128 + lax.broadcasted_iota(jnp.int32, (128, LANES), 0)
        for h in HV:
            moved = wide[h, pl.ds(pl.multiple_of(i * 128 + 2 * GAP, 32), 128)]
            frames_grad[rows, h * LANES:(h + 1) * LANES] = jnp.where(slot < len0, wide[h, rows], moved)
        return c
    lax.fori_loop(0, 2 * plan.slots // 128, ungap_wide, 0)
    point_back(0, 0, gpb)
    kernel_back(0, pieces)

    wait_all(counts, count_sems.at[0])

    def drain(slot, c):
        wait_all(recv4.at[0], send_sem.at[slot])
        return c
    lax.fori_loop(0, send4.shape[0], drain, 0)


def body(frames, dw_first, dw_second, point, gains, shifts, se_down, se_up, cotangent, lengths, *, devices):
    sub, taps_first, shard = dw_first.shape
    taps_second = dw_second.shape[1]
    hidden = se_down.shape[2]
    channels = point.shape[3]
    plan = Plan(cotangent.shape[0], channels, taps_first, taps_second, sub, hidden, devices)
    halves, Q = plan.halves, plan.steps

    def gather(v, axis):
        return lax.all_gather(v, "dp", axis=axis, tiled=True)

    small = jnp.concatenate([
        dw_first.reshape(-1, shard), dw_second.reshape(-1, shard), gains.reshape(-1, shard),
        shifts.reshape(-1, shard), se_up.reshape(-1, shard),
        jnp.swapaxes(se_down, 1, 2).reshape(-1, shard)], axis=0)
    small = gather(small, 1)
    n1, n2, ng, ns = sub * taps_first, sub * taps_second, 2 * (sub + 1), 2 * hidden
    cuts = [0, n1, n1 + n2, n1 + n2 + ng, n1 + n2 + 2 * ng, n1 + n2 + 2 * ng + ns, n1 + n2 + 2 * ng + 2 * ns]
    part = [small[cuts[i]:cuts[i + 1]] for i in range(6)]
    K = 32

    def dw_layout(v, taps):
        v = v.astype(F32).reshape(sub, taps, halves, LANES).transpose(0, 2, 1, 3)
        return jnp.pad(v, ((0, 0), (0, 0), (0, K - taps), (0, 0)))
    dw = jnp.concatenate([dw_layout(part[0], taps_first), dw_layout(part[1], taps_second)], axis=0)

    def norm_layout(v):
        v = v.astype(F32).reshape(2, sub + 1, halves, LANES)
        return jnp.concatenate([v[:, :sub].reshape(2 * sub, halves, LANES), v[:, sub]], axis=0)
    matrices = gather(point, 2)
    matrices = jnp.concatenate([matrices[:, :sub].reshape(2 * sub, channels, channels), matrices[:, sub]], axis=0)
    expand = part[4].astype(F32).reshape(2, hidden, channels)
    squeeze_t = part[5].astype(F32).reshape(2, hidden, channels)

    layers = 2 * sub + 2
    slots = 2 * layers
    shapes = (
        jax.ShapeDtypeStruct((plan.slots, channels), F32),
        jax.ShapeDtypeStruct((2 * plan.slots, channels), F32),
        jax.ShapeDtypeStruct((2 * sub, halves, K, LANES), F32),
        jax.ShapeDtypeStruct((layers, channels, channels), F32),
        jax.ShapeDtypeStruct((layers, halves, LANES), F32),
        jax.ShapeDtypeStruct((layers, halves, LANES), F32),
        jax.ShapeDtypeStruct((2, hidden, channels), F32),
        jax.ShapeDtypeStruct((2, hidden, channels), F32),
    )
    vmem = pl.BlockSpec(memory_space=pltpu.VMEM)
    results = pl.pallas_call(
        functools.partial(kernel, plan),
        out_shape=shapes,
        in_specs=[pl.BlockSpec(memory_space=pltpu.SMEM)] + [vmem] * 8,
        out_specs=[vmem] * len(shapes),
        scratch_shapes=[
            pltpu.VMEM((2 * sub + 1, halves, plan.pad, 8, LANES), F32),
            pltpu.VMEM((layers, plan.rows, channels), BF16),
            pltpu.VMEM((layers, halves, Q, 8, LANES), F32),
            pltpu.VMEM((halves, plan.pad, 8, LANES), F32),
            pltpu.VMEM((halves, Q, 8, LANES), F32),
            pltpu.VMEM((plan.rows, channels), BF16),
            pltpu.VMEM((plan.rows, channels), BF16),
            pltpu.VMEM((2, halves, Q, 8, LANES), F32),
            pltpu.VMEM((halves, plan.slots + 2 * GAP, LANES), F32),
            pltpu.VMEM((halves, 2 * plan.slots + 4 * GAP, LANES), F32),
            pltpu.VMEM((Q, 8, LANES), F32),
            pltpu.VMEM((Q, 8, LANES), F32),
            pltpu.VMEM((Q, 8, LANES), F32),
            pltpu.VMEM((layers, 8, LANES), F32),
            pltpu.VMEM((slots, 4, LANES), F32),
            pltpu.VMEM((layers, devices, 4, LANES), F32),
            pltpu.VMEM((devices, 4, LANES), F32),
            pltpu.VMEM((4, LANES), F32),
            pltpu.SemaphoreType.DMA((slots,)),
            pltpu.SemaphoreType.DMA((slots,)),
            pltpu.SemaphoreType.DMA((2,)),
        ],
        compiler_params=pltpu.CompilerParams(
            collective_id=0, has_side_effects=True, vmem_limit_bytes=62 * 1024 * 1024),
    )(lengths, frames, cotangent, dw, matrices, norm_layout(gains_full(part[2], sub, channels)),
      norm_layout(gains_full(part[3], sub, channels)), squeeze_t, expand)
    output, frames_grad, dwg, pg, gg, sg, sqg, exg = results

    def scatter(v, axis):
        return lax.psum_scatter(v, "dp", scatter_dimension=axis, tiled=True)

    def dw_out(v, taps):
        return v[:, :, :taps].transpose(0, 2, 1, 3).reshape(sub * taps, channels)
    packed = jnp.concatenate([dw_out(dwg[:sub], taps_first), dw_out(dwg[sub:], taps_second),
                              sqg.reshape(-1, channels), exg.reshape(-1, channels)], axis=0)
    packed = scatter(packed, 1)
    g1 = packed[:n1].reshape(sub, taps_first, shard)
    g2 = packed[n1:n1 + n2].reshape(sub, taps_second, shard)
    gsq = jnp.swapaxes(packed[n1 + n2:n1 + n2 + ns].reshape(2, hidden, shard), 1, 2)
    gex = packed[n1 + n2 + ns:].reshape(2, hidden, shard)
    pg = jnp.concatenate([pg[:2 * sub].reshape(2, sub, channels, channels), pg[2 * sub:][:, None]], axis=1)
    pg = scatter(pg, 2)

    def norm_out(v):
        v = v.reshape(layers, channels)
        v = jnp.concatenate([v[:2 * sub].reshape(2, sub, channels), v[2 * sub:][:, None]], axis=1)
        return lax.dynamic_slice_in_dim(v, lax.axis_index("dp") * shard, shard, 2)
    return (output, frames_grad, g1, g2, pg, norm_out(gg), norm_out(sg), gsq, gex)


def gains_full(v, sub, channels):
    return v.reshape(2, sub + 1, channels)


def solution(mesh):
    return jax.shard_map(
        functools.partial(body, devices=mesh.shape["dp"]),
        mesh=mesh,
        in_specs=(
            P("dp", None),
            P(None, None, "dp"),
            P(None, None, "dp"),
            P(None, None, "dp", None),
            P(None, None, "dp"),
            P(None, None, "dp"),
            P(None, "dp", None),
            P(None, None, "dp"),
            P("dp", None),
            P("dp"),
        ),
        out_specs=(
            P("dp", None),
            P("dp", None),
            P(None, None, "dp"),
            P(None, None, "dp"),
            P(None, None, "dp", None),
            P(None, None, "dp"),
            P(None, None, "dp"),
            P(None, "dp", None),
            P(None, None, "dp"),
        ),
        check_vma=False,
    )
```

time: 2810 us -> 512 us (0.18)
  blocking collectives: 1680 us -> 44 us
  local copies, waits for them, and re-layouts: 366 us -> 22.4 us
  other arithmetic: 322 us -> 6.15 us
  Pallas kernels: 0 us -> 190 us
  matrix products: 90 us -> 0 us
  waiting for transfers between devices: 318 us -> 234 us
    psum x30 -> x0, blocking collectives: 1210 us -> none  [the longest x11 438 us: statistics(): lax.psum((jnp.sum(product * valid_out, axis=0), local_count), 'dp')]
    all_gather x12 -> x1, blocking collectives: 470 us -> 44 us  [gather(): return lax.all_gather(v, 'dp', axis=axis, tiled=True)]
    pallas_call x0 -> x1, Pallas kernels: none -> 190 us  [body(): pl.pallas_call(functools.partial(kernel, plan), out_shape=shapes, in_spec...]
    slice x82 -> x19, local copies, waits for them, and re-layouts: 170 us -> 4.51 us  [the longest x3 1.4 us: body(): matrices[:, :sub].reshape(2 * sub, channels, channels)]
    reduce_scatter x4 -> x1, waiting for transfers between devices: 233 us -> 99.2 us  [scatter(): return lax.psum_scatter(v, 'dp', scatter_dimension=axis, tiled=True)]
    pad x21 -> x0, local copies, waits for them, and re-layouts: 129 us -> none  [the longest x19 127 us: depthwise(): window = lax.slice(padded, (k, 0), (slice_end, channels), (stride, 1))]
    unnamed x5 -> x4, waiting for transfers between devices: 0.08 us -> 128 us
    reduce_sum x50 -> x0, other arithmetic: 105 us -> none  [the longest x30 74.5 us: depthwise(): result = result + window * same_utterance * kernel[k]]
  transfers between devices with their start and end apart: 5 -> 3, of which waited for: 4 -> 3; matrix products, arithmetic and copies ran while one was open for 10% -> 3% of each run, Pallas kernels for 0% -> 0%
where the time goes in v1:
time: 512 us
  waiting for transfers between devices  234 us (46%)
  Pallas kernels  190 us (37%)
  blocking collectives  44 us (9%)
  local copies, waits for them, and re-layouts  22.4 us (4%)
  between operations  14 us (3%)
  other arithmetic  6.15 us (1%)
    pallas_call x1, Pallas kernels, body(): pl.pallas_call(functools.partial(kernel, plan), out_shape=shapes, in_spec...  190 us
    unnamed x4, waiting for transfers between devices  128 us
    reduce_scatter x1, waiting for transfers between devices, scatter(): return lax.psum_scatter(v, 'dp', scatter_dimension=axis, tiled=True)  99.2 us
    all_gather x1, blocking collectives, gather(): return lax.all_gather(v, 'dp', axis=axis, tiled=True)  44 us
    unnamed x41, local copies, waits for them, and re-layouts  13.8 us
  transfers between devices with their start and end apart: 3, of which 3 were waited for; matrix products, arithmetic and copies ran while one was open for 3% of the time, Pallas kernels for 0%

profile of v1, /device:TPU:0, one launch (start us, length us, event | category | flops | bytes accessed | tf_op | source)
XLA Modules:
  0.0 511.6 jit_solution(10620968160537375289)
XLA Ops:
  7.2 1.4 copy.136
  8.7 0.8 copy.128
  9.6 0.8 copy.129
  10.5 0.7 copy.131
  11.2 0.7 copy.130
  12.0 0.7 copy.126
  12.8 0.7 copy.127
  13.7 44.0 %all_gather.6 = bf16[412,256]{0,1:T(8,128)(2,1)S(1)} all-gather(bf16[412,8]{0,1:T(8,128)(2,1)S(1)} %concatenate.29), channel_id=1, replica_groups=mesh['dp'=32] {'dp'}, dimensions={1}, use_global_device_ids=true | all-gather | bytes 217536 | tf_op jit(solution)/shard_map/all_gather | solution.py:618
  58.8 0.6 convert.14.expand
  59.6 0.6 convert.13.squeeze_t
  60.2 0.6 pad_maximum_fusion.3
  60.8 0.8 fusion.3.dw
  61.6 7.3 %all-gather.2.cloned.1.call-done = bf16[2,6,256,256]{3,2,0,1:T(8,128)(2,1)} async-done(((bf16[2,6,8,256]{3,2,0,1:T(8,128)(2,1)}), bf16[2,6,256,256]{3,2,0,1:T(8,128)(2,1)}) %all-gather.2.cloned.1.call-update) | async-done | bytes 1572880 | tf_op jit(solution)/shard_map/all_gather | solution.py:618
  68.9 1.3 slice-done
  70.8 1.3 pad_maximum_fusion.1.point
  72.1 190.3 %shard_map.169 = (f32[1024,256]{1,0:T(8,128)}, f32[2048,256]{1,0:T(8,128)}, f32[10,2,32,128]{3,2,1,0:T(8,128)}, f32[12,256,256]{2,1,0:T(8,128)}, f32[12,2,128]{2...) custom-call(s32[2]{0:T(128)} %lens.1, bf16[2048,256]{1,0:T(8,128)(2,1)} %frames.1, ...), custom_call_target="tpu_custom_call" | custom-call | tf_op jit(solution)/shard_map/pallas_call | solution.py:656
  262.4 1.0 slice_bitcast_fusion.2
  263.4 1.1 slice_bitcast_fusion.3
  264.9 1.0 copy.159
  266.3 2.0 pad_maximum_fusion
  268.4 0.7 copy-done.7
  270.5 127.9 %reduce-scatter.7.cloned.1.call-done = f32[8,388]{1,0:T(8,128)} async-done(((f32[256,388]{1,0:T(8,128)}), f32[8,388]{1,0:T(8,128)}) %reduce-scatter.7.cloned.1.call-update) | async-done | bytes 12432
  398.4 0.7 slice.116
  399.1 0.8 slice.117
  399.9 0.6 copy.154
  400.6 0.8 fusion.8
  401.5 0.7 copy.158
  402.2 0.6 copy.153
  403.0 0.6 copy.157
  403.6 99.2 %reduce-scatter.5.cloned.1.call-done = f32[2,6,8,256]{3,2,1,0:T(8,128)} async-done(((f32[2,6,256,256]{3,2,1,0:T(8,128)}), f32[2,6,8,256]{3,2,1,0:T(8,128)}) %reduce-scatter.5.cloned.1.call-update) | async-done | bytes 98320 | tf_op jit(solution)/shard_map/reduce_scatter | solution.py:691
  502.8 1.0 copy.182
  503.7 1.3 copy.183
  (75 shorter events, 4.9 us)
Async XLA Ops:
  7.2 61.8 %all-gather.2.cloned.1.call-start = ((), (), s32[]{:S(2)}) async-start(), calls=%async_computation.2 | async-start | bytes 1622016 | tf_op jit(solution)/shard_map/all_gather | solution.py:618
  8.7 389.7 %reduce-scatter.7.cloned.1.call-start = ((), (), s32[]{:S(2)}) async-start(), calls=%async_computation.4 | async-start | bytes 540672
  68.9 1.3 slice-start
  68.9 1.8 copy-start
  262.4 2.5 copy-start.4
  262.4 2.5 copy-start.5
  263.4 2.6 copy-start.1
  265.9 236.8 %reduce-scatter.5.cloned.1.call-start = ((), (), s32[]{:S(2)}) async-start(), calls=%async_computation.3 | async-start | bytes 3244032 | tf_op jit(solution)/shard_map/reduce_scatter | solution.py:691
  268.4 0.7 copy-start.7
  268.4 0.7 copy-start.6
  268.4 234.4 %copy-start.3 = (f32[1024,256]{1,0:T(8,128)S(1)}, f32[1024,256]{1,0:T(8,128)}, u32[]{:S(2)}) copy-start(f32[1024,256]{1,0:T(8,128)} %get-tuple-element.78) | copy-start | bytes 3145732
  268.4 235.3 %copy-start.2 = (f32[2048,256]{1,0:T(8,128)S(1)}, f32[2048,256]{1,0:T(8,128)}, u32[]{:S(2)}) copy-start(f32[2048,256]{1,0:T(8,128)} %get-tuple-element.79) | copy-start | bytes 6291460
Sparse Core Ops, SparseCore 0:
  11.5 57.4 all-gather.1
  266.0 132.3 reduce-scatter.6
  405.3 97.3 reduce-scatter.4

commit v2 on v1

--- a/solution.py
+++ b/solution.py
@@ -37,6 +37,24 @@
         self.block = next(r for r in (26, 10, 2) if self.steps % r == 0)
         self.fine = next(r for r in (10, 26, 2) if self.steps % r == 0)
         self.pad = self.steps + 2 * HALO
+        self.per = sub_blocks + 1
+        self.layers = 2 * self.per
+        self.tap_rows = 32
+        self.values = 2 * LANES
+        self.shard = channels // devices
+        self.fused = self.shard == 8 and devices % 2 == 0 and sub_blocks == 5 and hidden == 32 and self.max_taps <= 32
+
+    def tap_row(self, r):
+        return r * self.tap_rows + self.tap_rows * (r // 4)
+
+
+SQUEEZE_ROW, EXPAND_ROW, GAIN_ROW, SHIFT_ROW = 128, 192, 224, 232
+
+
+class Refs:
+    def __init__(self, names, refs):
+        for name, ref in zip(names, refs, strict=True):
+            setattr(self, name, ref)
 
 
 def peers_of(me, n):
@@ -61,16 +79,46 @@
     return [item[1] for item in found]
 
 
-def kernel(plan, lens, frames, cot, dw, point, gains, shifts, squeeze_t, expand,
-           out, frames_grad, dw_grad, point_grad, gains_grad, shifts_grad, squeeze_grad, expand_grad,
-           hid, acts, prods, gd, gz, gpb, gqb, pre, flat, wide, first_mask, second_mask, valid,
-           stats, send4, recv4, counts, csend, send_sem, recv_sem, count_sems):
+def same_core_peers(me, n):
+    if n != 32:
+        return [lax.rem(me + 2 * k, n) for k in range(1, n // 2)]
+    core = lax.rem(me, 2)
+    x = lax.rem(me // 2, 2)
+    y = lax.rem(me // 4, 2)
+    z = me // 8
+    found = []
+    for order, other in enumerate((3 - z, lax.rem(z + 2, 4), z + 1 - 2 * lax.rem(z, 2), z)):
+        for dy in (1, 0):
+            for dx in (1, 0):
+                if order == 3 and dy == 0 and dx == 0:
+                    continue
+                oy = lax.rem(y + dy, 2)
+                ox = lax.rem(x + dx, 2)
+                found.append((dy + dx + (3, 2, 1, 0)[order], other * 8 + oy * 4 + ox * 2 + core))
+    found.sort(key=lambda item: -item[0])
+    return [item[1] for item in found]
+
+
+def kernel(plan, names, *refs):
+    k = Refs(names, refs)
+    lens, frames, cot, dw, point, gains, shifts = k.lens, k.frames, k.cot, k.dw, k.point, k.gains, k.shifts
+    squeeze_t, expand = k.squeeze_t, k.expand
+    out, frames_grad = k.out, k.frames_grad
+    hid, acts, prods, gd, gz, gpb, gqb, pre = k.hid, k.acts, k.prods, k.gd, k.gz, k.gpb, k.gqb, k.pre
+    flat, wide, first_mask, second_mask, valid, stats = k.flat, k.wide, k.first_mask, k.second_mask, k.valid, k.stats
+    send4, recv4, counts, csend = k.send4, k.recv4, k.counts, k.csend
+    send_sem, recv_sem, count_sems = k.send_sem, k.recv_sem, k.count_sems
     N = plan.devices
     Q, R, RF = plan.steps, plan.block, plan.fine
     HV = range(plan.halves)
     SUB = plan.sub
+    PER = plan.per
     me = lax.axis_index("dp")
     peers = peers_of(me, N)
+    chips = N // 2
+    chip, core = me // 2, lax.rem(me, 2)
+    partner = me + 1 - 2 * core
+    same_core = same_core_peers(me, N)
 
     barrier = pltpu.get_barrier_semaphore()
     for peer in peers:
@@ -134,6 +182,69 @@
         for h in HV:
             set_halo(hid.at[phase], h)
 
+    def load_shard():
+        for b in range(2):
+            source = (k.dw_first, k.dw_second)[b]
+            k.packed[...] = jnp.zeros((plan.values, LANES), F32)
+            for r in range(SUB):
+                k.packed[pl.ds(plan.tap_row(r), plan.taps[b]), 0:plan.shard] = source[r].astype(F32)
+            k.packed[EXPAND_ROW:EXPAND_ROW + plan.hidden, 0:plan.shard] = k.se_up[b].astype(F32)
+            k.packed[GAIN_ROW:GAIN_ROW + PER, 0:plan.shard] = k.gains_in[b].astype(F32)
+            k.packed[SHIFT_ROW:SHIFT_ROW + PER, 0:plan.shard] = k.shifts_in[b].astype(F32)
+            for tile in range(2):
+                k.packed_t[8 * b:8 * b + 8, tile * LANES:(tile + 1) * LANES] = jnp.transpose(
+                    k.packed[tile * LANES:(tile + 1) * LANES])[0:8]
+            k.packed_t[8 * b:8 * b + 8, SQUEEZE_ROW:SQUEEZE_ROW + plan.hidden] = k.se_down[b].astype(F32)
+        k.gath[0, chip, core] = k.packed_t[...].astype(BF16)
+        for pair in range(PER):
+            rows = [k.point_in[i // PER, i % PER].astype(F32) for i in (2 * pair, 2 * pair + 1)]
+            k.gath[1 + pair, chip, core] = jnp.concatenate(rows, axis=0).astype(BF16)
+
+    def gather_send(unit):
+        view = k.gath.at[unit, chip, core]
+        for peer in same_core:
+            pltpu.make_async_remote_copy(src_ref=view, dst_ref=view, send_sem=k.unit_sems.at[0, unit],
+                                         recv_sem=k.unit_sems.at[1, unit], device_id=(peer,),
+                                         device_id_type=MESH).start()
+
+    def gather_forward(unit):
+        view = k.gath.at[unit, pl.ds(0, chips - 1), 0]
+        pltpu.make_async_copy(view, view, k.unit_sems.at[1, unit]).wait()
+        view = k.gath.at[unit, :, core]
+        pltpu.make_async_remote_copy(src_ref=view, dst_ref=view, send_sem=k.unit_sems.at[2, unit],
+                                     recv_sem=k.unit_sems.at[3, unit], device_id=(partner,),
+                                     device_id_type=MESH).start()
+
+    def gather_wait(unit):
+        view = k.gath.at[unit, :, 0]
+        pltpu.make_async_copy(view, view, k.unit_sems.at[3, unit]).wait()
+
+    def unpack_values():
+        got = k.gath[0].astype(F32).reshape(N, 16, plan.values)
+        for b in range(2):
+            block = got[:, 8 * b:8 * b + 8].reshape(plan.channels, plan.values)
+            for h in HV:
+                for tile in range(2):
+                    part = block[h * LANES:(h + 1) * LANES, tile * LANES:(tile + 1) * LANES]
+                    k.unpacked[tile * LANES:(tile + 1) * LANES] = jnp.transpose(part)
+                for r in range(SUB):
+                    dw[b * PER + r, h] = k.unpacked[plan.tap_row(r):plan.tap_row(r) + plan.tap_rows]
+                for r in range(PER):
+                    gains[b * PER + r, h:h + 1] = k.unpacked[GAIN_ROW + r:GAIN_ROW + r + 1]
+                    shifts[b * PER + r, h:h + 1] = k.unpacked[SHIFT_ROW + r:SHIFT_ROW + r + 1]
+                lanes = slice(h * LANES, (h + 1) * LANES)
+                expand[b, :, lanes] = k.unpacked[EXPAND_ROW:EXPAND_ROW + plan.hidden]
+                squeeze_t[b, :, lanes] = k.unpacked[SQUEEZE_ROW:SQUEEZE_ROW + plan.hidden]
+
+    def unpack_pair(pair):
+        got = k.gath[1 + pair].astype(F32).reshape(N, 16, plan.channels)
+        for side in range(2):
+            block = got[:, 8 * side:8 * side + 8].reshape(plan.channels, plan.channels)
+            point[2 * pair + side] = block.astype(BF16)
+
+    if plan.fused:
+        load_shard()
+
     csend[...] = jnp.full((4, LANES), count, F32)
     pl.semaphore_wait(barrier, N - 1)
 
@@ -146,7 +257,12 @@
         view = ref.at[pl.ds(0, N - 1)]
         pltpu.make_async_copy(view, view, sem).wait()
 
+    if plan.fused:
+        gather_send(0)
+        gather_send(1)
     send_to_all(csend, counts.at[me], count_sems.at[0], count_sems.at[1])
+    if plan.fused:
+        gather_send(2)
     counts[me] = csend[...]
 
     def exchange(slot, place, rows):
@@ -159,7 +275,7 @@
         return recv4[place]
 
     def back_place(index):
-        return lax.rem(index + SUB, 2 * SUB)
+        return lax.rem(index + PER, 2 * PER)
 
     def row(values):
         return values.reshape(1, 1, LANES)
@@ -242,25 +358,34 @@
         for h in HV:
             set_halo(hid.at[target], h)
 
-    def block_pieces(b, r):
-        taps = plan.taps[b]
-        margin = (taps - 1) // 2
-        if b == 0 and r == 0:
-            even = [(k, (k - margin) // 2) for k in range(taps) if (k - margin) % 2 == 0]
-            odd = [(k, (k - margin - 1) // 2) for k in range(taps) if (k - margin) % 2 == 1]
+    def hid_of(b, r):
+        return b * SUB + r + 1
+
+    def regular_taps(b):
+        margin = (plan.taps[b] - 1) // 2
+        return [(t, t - margin) for t in range(plan.taps[b])]
+
+    def block_pieces(b):
+        if b == 0:
+            taps = regular_taps(0)
+            even = [(t, s // 2) for t, s in taps if s % 2 == 0]
+            odd = [(t, (s - 1) // 2) for t, s in taps if s % 2 == 1]
             return [(0, even), (1, odd)]
-        return [(b * SUB + r + 1, [(k, k - margin) for k in range(taps)])]
-
-    def residual_input(b):
-        source = 0 if b == 0 else SUB + 1
+        return [(hid_of(1, 0), regular_taps(1))]
+
+    def residual_forward(b):
+        source = 0 if b == 0 else hid_of(1, 0)
+        res = b * PER + SUB
 
         def body(t0, c):
             rows = pl.ds(pl.multiple_of(8 * t0, 16), 8 * R)
             for h in HV:
                 values = hid[source, h, pl.ds(HALO + t0, R)].reshape(8 * R, LANES)
-                acts[2 * SUB + b, rows, h * LANES:(h + 1) * LANES] = values.astype(BF16)
+                acts[res, rows, h * LANES:(h + 1) * LANES] = values.astype(BF16)
             return c
         steps_loop(R, body)
+        pointwise(res, res)
+        exchange(res, res, local_stats(res))
 
     def pair_rows(values):
         return jnp.concatenate([values, jnp.zeros((6, plan.channels), F32)], axis=0)
@@ -269,7 +394,7 @@
         return lax.dot_general(a, b, (dims, ((), ())), precision=HIGHEST, preferred_element_type=F32)
 
     def excite(b):
-        last = b * SUB + SUB - 1
+        last = b * PER + SUB - 1
         scales = [stat_row(last, 2, h) for h in HV]
         offsets = [stat_row(last, 3, h) for h in HV]
 
@@ -295,7 +420,7 @@
         return [[row(gate[u:u + 1, h * LANES:(h + 1) * LANES]) for h in HV] for u in range(2)]
 
     def tail(b, gate, store):
-        last, res = b * SUB + SUB - 1, 2 * SUB + b
+        last, res = b * PER + SUB - 1, b * PER + SUB
         gates = gate_rows(gate)
         consts = [(stat_row(last, 2, h), stat_row(last, 3, h), stat_row(res, 2, h), stat_row(res, 3, h)) for h in HV]
 
@@ -313,42 +438,63 @@
             return c
         steps_loop(RF, body)
 
+    def forward_aside(b, r):
+        if plan.fused:
+            step = b * SUB + r
+
+            @pl.when(jnp.logical_and(step >= 1, step < PER))
+            def _():
+                gather_wait(1 + step)
+                unpack_pair(step)
+
+            @pl.when(step < PER - 1)
+            def _():
+                gather_forward(2 + step)
+
+            @pl.when(step < PER - 2)
+            def _():
+                gather_send(3 + step)
+
+        @pl.when(r == SUB - 2)
+        def _():
+            residual_forward(b)
+
     def forward_block(b):
-        def layer(r, pieces):
-            index = b * SUB + r
+        def layer(r, pieces, before=None):
+            index = b * PER + r
             layer_conv(index, pieces)
+            if before is not None:
+                before()
             pointwise(index, index)
             exchange(index, index, local_stats(index))
-        layer(0, block_pieces(b, 0))
-        residual_input(b)
-        pointwise(2 * SUB + b, 2 * SUB + b)
-        exchange(2 * SUB + b, 2 * SUB + b, local_stats(2 * SUB + b))
-        merge_stats(b * SUB, b * SUB)
-        activate(b * SUB, b * SUB + 2)
+            forward_aside(b, r)
+            merge_stats(index, index)
+
+        def first_matrices():
+            gather_wait(1)
+            unpack_pair(0)
+        layer(0, block_pieces(b), first_matrices if plan.fused and b == 0 else None)
+        activate(b * PER, hid_of(b, 1))
 
         def rest(r, c):
-            taps = plan.taps[b]
-            margin = (taps - 1) // 2
-            index = b * SUB + r
-            layer(r, [(index + 1, [(k, k - margin) for k in range(taps)])])
-            merge_stats(index, index)
+            layer(r, [(hid_of(b, r), regular_taps(b))])
 
             @pl.when(r < SUB - 1)
             def _():
-                activate(index, index + 2)
+                activate(b * PER + r, hid_of(b, r + 1))
             return c
         lax.fori_loop(1, SUB, rest, 0)
-        merge_stats(2 * SUB + b, 2 * SUB + b)
+        merge_stats(b * PER + SUB, b * PER + SUB)
         return excite(b)
 
-    back_slot = 2 * SUB + 2
+    back_slot = 2 * PER
 
     def sum_rows(parts):
         return jnp.concatenate([jnp.sum(part, axis=0, keepdims=True) for part in parts], axis=0)
 
     def tail_back(b, kept, load):
         means, inner, excited, gate = kept
-        last, res = b * SUB + SUB - 1, 2 * SUB + b
+        last, res = b * PER + SUB - 1, b * PER + SUB
         gates = gate_rows(gate)
         consts = [(stat_row(last, 2, h), stat_row(last, 3, h)) for h in HV]
 
@@ -372,11 +518,11 @@
             [jnp.concatenate([jnp.sum(tot[2 * h + u], axis=0, keepdims=True) for h in HV], axis=1)
              for u in range(2)], axis=0))
         grad_up = grad_gate * gate * (1.0 - gate)
-        expand_grad[b] = small(excited, grad_up, ((0,), (0,)))
+        k.expand_grad[b] = small(excited, grad_up, ((0,), (0,)))
         grad_excited = small(grad_up, expand[b], ((1,), (1,)))
         sg = sigmoid(inner)
         grad_inner = grad_excited * (sg * (1.0 + inner * (1.0 - sg)))
-        squeeze_grad[b] = small(grad_inner, means, ((0,), (0,)))
+        k.squeeze_grad[b] = small(grad_inner, means, ((0,), (0,)))
         grad_means = small(grad_inner, squeeze_t[b], ((1,), (0,)))
         mean_rows = [[row(grad_means[u:u + 1, h * LANES:(h + 1) * LANES] * inv_half[u]) for h in HV]
                      for u in range(2)]
@@ -400,12 +546,12 @@
             return tuple(out_c)
         tot = steps_loop(RF, second, zero4 + zero4)
         exchange(back_slot + last, back_place(last), sum_rows([tot[0], tot[4], tot[1], tot[5]]))
-        exchange(back_slot + res, 2 * SUB + 1 - b, sum_rows([tot[2], tot[6], tot[3], tot[7]]))
-
-    def norm_back(index, place, load, target):
-        sums = jnp.sum(received(back_slot + index, place), axis=0)
-        shifts_grad[index] = sums[0:2]
-        gains_grad[index] = sums[2:4]
+        exchange(back_slot + res, back_place(res), sum_rows([tot[2], tot[6], tot[3], tot[7]]))
+
+    def norm_back(index, load, target):
+        sums = jnp.sum(received(back_slot + index, back_place(index)), axis=0)
+        k.shifts_grad[index] = sums[0:2]
+        k.gains_grad[index] = sums[2:4]
         total = jnp.sum(counts[...], axis=0)[0:2]
         st = stats[index]
         mean, inv, scale = st[0:2], st[2:4], st[4:6]
@@ -432,9 +578,10 @@
             return c
         steps_loop(R, body)
 
-    def point_back(index, act, source):
-        point_grad[index] = lax.dot_general(acts[act], source[...], (((0,), (0,)), ((), ())),
-                                            preferred_element_type=F32)
+    def point_back(index, source):
+        place = lax.rem(index, 2) if plan.fused else index
+        k.point_grad[place] = lax.dot_general(acts[index], source[...], (((0,), (0,)), ((), ())),
+                                              preferred_element_type=F32)
 
     def store_gd(t0, h, values):
         gd[h, pl.ds(HALO + t0, R)] = values
@@ -461,7 +608,7 @@
                     return tuple(acc + accumulate(g * win[s - low:s - low + RF]) for acc, (_, s) in zip(c, taps))
                 accs = steps_loop(RF, body, tuple(jnp.zeros((8, LANES), F32) for _ in taps))
                 for acc, (tap, _) in zip(accs, taps):
-                    dw_grad[index, h, pl.ds(tap, 1)] = jnp.sum(acc, axis=0, keepdims=True)
+                    k.dw_grad[index, h, pl.ds(tap, 1)] = jnp.sum(acc, axis=0, keepdims=True)
 
     def hidden_back(index, taps):
         before = index - 1
@@ -486,40 +633,143 @@
     def load_gz(t0, h):
         return gz[h, pl.ds(t0, R)]
 
+    def scatter_start(unit, place):
+        pltpu.make_async_remote_copy(src_ref=k.shares.at[place, :, 1 - core], dst_ref=k.inbox.at[unit],
+                                     send_sem=k.unit_sems.at[4, unit], recv_sem=k.unit_sems.at[5, unit],
+                                     device_id=(partner,), device_id_type=MESH).start()
+
+    def scatter_send(unit, place):
+        view = k.inbox.at[unit]
+        pltpu.make_async_copy(view, view, k.unit_sems.at[5, unit]).wait()
+        pltpu.make_async_copy(view, view, k.unit_sems.at[4, unit]).wait()
+        k.sums[unit] = (k.shares[place, :, core].astype(F32) + k.inbox[unit].astype(F32)).astype(BF16)
+        k.gained[unit, chip] = k.sums[unit, chip]
+        for peer in same_core:
+            pltpu.make_async_remote_copy(src_ref=k.sums.at[unit, peer // 2], dst_ref=k.gained.at[unit, chip],
+                                         send_sem=k.unit_sems.at[6, unit], recv_sem=k.unit_sems.at[7, unit],
+                                         device_id=(peer,), device_id_type=MESH).start()
+
+    def scatter_finish(unit):
+        view = k.gained.at[unit, pl.ds(0, chips - 1)]
+        pltpu.make_async_copy(view, view, k.unit_sems.at[7, unit]).wait()
+        return jnp.sum(k.gained[unit].astype(F32), axis=0)
+
+    def pair_start(pair):
+        both = [k.point_grad[side].reshape(N, 8, plan.channels) for side in range(2)]
+        k.shares[0] = jnp.concatenate(both, axis=1).astype(BF16).reshape(chips, 2, 16, plan.channels)
+        scatter_start(1 + pair, 0)
+
+    def pair_finish(pair):
+        total = scatter_finish(1 + pair)
+        b = pair // (PER // 2)
+        r = 2 * lax.rem(pair, PER // 2)
+        k.point_out[b, r] = total[0:8]
+        k.point_out[b, r + 1] = total[8:16]
+
+    def values_start():
+        k.packed[...] = jnp.zeros((plan.values, LANES), F32)
+        blocks = []
+        for b in range(2):
+            columns = []
+            for h in HV:
+                for r in range(SUB):
+                    k.packed[plan.tap_row(r):plan.tap_row(r) + plan.tap_rows] = k.dw_grad[b * PER + r, h]
+                lanes = slice(h * LANES, (h + 1) * LANES)
+                k.packed[EXPAND_ROW:EXPAND_ROW + plan.hidden] = k.expand_grad[b, :, lanes]
+                k.packed[SQUEEZE_ROW:SQUEEZE_ROW + plan.hidden] = k.squeeze_grad[b, :, lanes]
+                for r in range(PER):
+                    k.packed[GAIN_ROW + r:GAIN_ROW + r + 1] = k.gains_grad[b * PER + r, h:h + 1]
+                    k.packed[SHIFT_ROW + r:SHIFT_ROW + r + 1] = k.shifts_grad[b * PER + r, h:h + 1]
+                columns.append(jnp.concatenate(
+                    [jnp.transpose(k.packed[t * LANES:(t + 1) * LANES]) for t in range(2)], axis=1))
+            whole = jnp.concatenate(columns, axis=0)
+            k.own_norm[b] = whole[:, LANES:]
+            blocks.append(whole.reshape(N, 8, plan.values))
+        k.shares[1] = jnp.concatenate(blocks, axis=1).astype(BF16).reshape(chips, 2, 16, plan.values)
+        scatter_start(0, 1)
+
+    def values_finish():
+        total = scatter_finish(0)
+        mine = pl.ds(pl.multiple_of(me * 8, 8), 8)
+        for b in range(2):
+            rows = total[8 * b:8 * b + 8]
+            k.squeeze_out[b] = rows[:, SQUEEZE_ROW:SQUEEZE_ROW + plan.hidden]
+            fill = jnp.zeros((LANES - 8, LANES), F32)
+            for t in range(2):
+                k.packed[t * LANES:(t + 1) * LANES] = jnp.transpose(
+                    jnp.concatenate([rows[:, t * LANES:(t + 1) * LANES], fill], axis=0))
+            dw_out = (k.dw_first_out, k.dw_second_out)[b]
+            for r in range(SUB):
+                dw_out[r] = k.packed[plan.tap_row(r):plan.tap_row(r) + plan.taps[b], 0:plan.shard]
+            k.expand_out[b] = k.packed[EXPAND_ROW:EXPAND_ROW + plan.hidden, 0:plan.shard]
+            k.packed[LANES:] = jnp.transpose(jnp.concatenate([k.own_norm[b, mine], fill], axis=0))
+            k.gains_out[b] = k.packed[GAIN_ROW:GAIN_ROW + PER, 0:plan.shard]
+            k.shifts_out[b] = k.packed[SHIFT_ROW:SHIFT_ROW + PER, 0:plan.shard]
+
+    HALF = PER // 2
+
+    def backward_aside(b, r):
+        index = b * PER + r
+        if plan.fused:
+            if b == 0:
+                @pl.when(r == SUB - 1)
+                def _():
+                    scatter_send(1 + HALF, 0)
+
+                @pl.when(r == SUB - 2)
+                def _():
+                    pair_finish(HALF)
+
+            @pl.when(lax.rem(r, 2) == 1)
+            def _():
+                scatter_send(1 + HALF * b + (r + 1) // 2, 0)
+
+            @pl.when(jnp.logical_and(lax.rem(r, 2) == 0, r < SUB - 1))
+            def _():
+                pair_finish(HALF * b + r // 2 + 1)
+        point_back(index, gpb)
+
+        @pl.when(r == SUB - 1)
+        def _():
+            res = b * PER + SUB
+            norm_back(res, lambda t0, h: pre[b, h, pl.ds(t0, R)], gqb)
+            point_back(res, gqb)
+        if plan.fused:
+            @pl.when(lax.rem(r, 2) == 0)
+            def _():
+                pair_start(HALF * b + r // 2)
+
     def backward_block(b):
-        taps = plan.taps[b]
-        margin = (taps - 1) // 2
-        regular = [(k, k - margin) for k in range(taps)]
-        res = 2 * SUB + b
+        def filtered(index):
+            norm_back(index, load_gz, gpb)
+            pointwise_back(index, gpb, store_gd)
+            for h in HV:
+                set_halo(gd, h)
 
         def step(j, c):
             r = SUB - 1 - j
-            index = b * SUB + r
-            norm_back(index, back_place(index), load_gz, gpb)
-            pointwise_back(index, gpb, store_gd)
-            for h in HV:
-                set_halo(gd, h)
-            hidden_back(index, regular)
-            point_back(index, index, gpb)
-            kernel_back(index, [(index + 1, regular)])
+            index = b * PER + r
+            filtered(index)
+            hidden_back(index, regular_taps(b))
+            backward_aside(b, r)
+            kernel_back(index, [(hid_of(b, r), regular_taps(b))])
             return c
         lax.fori_loop(0, SUB - 1, step, 0)
-        norm_back(res, 2 * SUB + 1 - b, lambda t0, h: pre[b, h, pl.ds(t0, R)], gqb)
-        point_back(res, res, gqb)
-        index = b * SUB
-        norm_back(index, back_place(index), load_gz, gpb)
-        pointwise_back(index, gpb, store_gd)
-        for h in HV:
-            set_halo(gd, h)
-
+        filtered(b * PER)
+
+    if plan.fused:
+        for unit in range(2):
+            gather_forward(unit)
+        gather_wait(0)
+        unpack_values()
     wait_all(counts, count_sems.at[1])
     kept_first = forward_block(0)
 
     def store_middle(t0, h, values):
-        hid[SUB + 1, h, pl.ds(HALO + t0, RF)] = values
+        hid[hid_of(1, 0), h, pl.ds(HALO + t0, RF)] = values
     tail(0, kept_first[3], store_middle)
     for h in HV:
-        set_halo(hid.at[SUB + 1], h)
+        set_halo(hid.at[hid_of(1, 0)], h)
     kept_second = forward_block(1)
 
     def store_out(t0, h, values):
@@ -557,24 +807,28 @@
 
     tail_back(1, kept_second, load_cot)
     backward_block(1)
-    margin = (plan.taps[1] - 1) // 2
-    regular = [(k, k - margin) for k in range(plan.taps[1])]
 
     def store_gz(t0, h, values):
         gz[h, pl.ds(t0, R)] = values
-    pointwise_back(2 * SUB + 1, gqb, store_gz)
+    pointwise_back(PER + SUB, gqb, store_gz)
 
     def middle(t0, c):
         for h in HV:
-            gz[h, pl.ds(t0, R)] = gz[h, pl.ds(t0, R)] + conv_back_block(t0, h, SUB, regular)
+            gz[h, pl.ds(t0, R)] = gz[h, pl.ds(t0, R)] + conv_back_block(t0, h, PER, regular_taps(1))
         return c
     steps_loop(R, middle)
     tail_back(0, kept_first, lambda t0, h: gz[h, pl.ds(t0, RF)])
-    point_back(SUB, SUB, gpb)
-    kernel_back(SUB, [(SUB + 1, regular)])
+    backward_aside(1, 0)
+    kernel_back(PER, [(hid_of(1, 0), regular_taps(1))])
     backward_block(0)
-    pieces = block_pieces(0, 0)
-    pointwise_back(2 * SUB, gqb, store_gz)
+    pieces = block_pieces(0)
+    backward_aside(0, 0)
+    kernel_back(0, pieces)
+    if plan.fused:
+        values_start()
+        scatter_send(1, 0)
+        scatter_send(0, 1)
+    pointwise_back(SUB, gqb, store_gz)
 
     def spread(t0, c):
         v = valid[pl.ds(t0, R)]
@@ -595,8 +849,9 @@
             frames_grad[rows, h * LANES:(h + 1) * LANES] = jnp.where(slot < len0, wide[h, rows], moved)
         return c
     lax.fori_loop(0, 2 * plan.slots // 128, ungap_wide, 0)
-    point_back(0, 0, gpb)
-    kernel_back(0, pieces)
+    if plan.fused:
+        pair_finish(0)
+        values_finish()
 
     wait_all(counts, count_sems.at[0])
 
@@ -604,6 +859,106 @@
         wait_all(recv4.at[0], send_sem.at[slot])
         return c
     lax.fori_loop(0, send4.shape[0], drain, 0)
+    if plan.fused:
+        def drain_units(unit, c):
+            view = k.gath.at[0, pl.ds(0, chips - 1), 0]
+            pltpu.make_async_copy(view, view, k.unit_sems.at[0, unit]).wait()
+            view = k.gath.at[0, :, 0]
+            pltpu.make_async_copy(view, view, k.unit_sems.at[2, unit]).wait()
+            view = k.gained.at[0, pl.ds(0, chips - 1)]
+            pltpu.make_async_copy(view, view, k.unit_sems.at[6, unit]).wait()
+            return c
+        lax.fori_loop(0, 1 + PER, drain_units, 0)
+
+
+def call_kernel(plan, inputs):
+    layers, halves, Q, channels = plan.layers, plan.halves, plan.steps, plan.channels
+    vals, shard, hidden, devices = plan.values, plan.shard, plan.hidden, plan.devices
+    slots = 2 * layers
+
+    def shape(*dims, dtype=F32):
+        return jax.ShapeDtypeStruct(dims, dtype)
+    outs = {
+        "out": shape(plan.slots, channels),
+        "frames_grad": shape(2 * plan.slots, channels),
+    }
+    params = {
+        "dw": shape(layers, halves, plan.tap_rows, LANES),
+        "point": shape(layers, channels, channels, dtype=BF16),
+        "gains": shape(layers, halves, LANES),
+        "shifts": shape(layers, halves, LANES),
+        "squeeze_t": shape(2, hidden, channels),
+        "expand": shape(2, hidden, channels),
+    }
+    grads = {
+        "dw_grad": shape(layers, halves, plan.tap_rows, LANES),
+        "point_grad": shape(2 if plan.fused else layers, channels, channels),
+        "gains_grad": shape(layers, halves, LANES),
+        "shifts_grad": shape(layers, halves, LANES),
+        "squeeze_grad": shape(2, hidden, channels),
+        "expand_grad": shape(2, hidden, channels),
+    }
+    scratch = {
+        "hid": shape(2 * plan.sub + 1, halves, plan.pad, 8, LANES),
+        "acts": shape(layers, plan.rows, channels, dtype=BF16),
+        "prods": shape(layers, halves, Q, 8, LANES),
+        "gd": shape(halves, plan.pad, 8, LANES),
+        "gz": shape(halves, Q, 8, LANES),
+        "gpb": shape(plan.rows, channels, dtype=BF16),
+        "gqb": shape(plan.rows, channels, dtype=BF16),
+        "pre": shape(2, halves, Q, 8, LANES),
+        "flat": shape(halves, plan.slots + 2 * GAP, LANES),
+        "wide": shape(halves, 2 * plan.slots + 4 * GAP, LANES),
+        "first_mask": shape(Q, 8, LANES),
+        "second_mask": shape(Q, 8, LANES),
+        "valid": shape(Q, 8, LANES),
+        "stats": shape(layers, 8, LANES),
+        "send4": shape(slots, 4, LANES),
+        "recv4": shape(layers, devices, 4, LANES),
+        "counts": shape(devices, 4, LANES),
+        "csend": shape(4, LANES),
+    }
+    sems = {"send_sem": (slots,), "recv_sem": (slots,), "count_sems": (2,)}
+    if plan.fused:
+        units, chips = 1 + plan.per, devices // 2
+        outs.update({
+            "dw_first_out": shape(plan.sub, plan.taps[0], shard),
+            "dw_second_out": shape(plan.sub, plan.taps[1], shard),
+            "point_out": shape(2, plan.per, shard, channels),
+            "gains_out": shape(2, plan.per, shard),
+            "shifts_out": shape(2, plan.per, shard),
+            "squeeze_out": shape(2, shard, hidden),
+            "expand_out": shape(2, hidden, shard),
+        })
+        scratch.update(params)
+        scratch.update(grads)
+        scratch.update({
+            "packed": shape(vals, LANES),
+            "packed_t": shape(16, vals),
+            "unpacked": shape(vals, LANES),
+            "gath": shape(units, chips, 2, 16, channels, dtype=BF16),
+            "shares": shape(2, chips, 2, 16, channels, dtype=BF16),
+            "inbox": shape(units, chips, 16, channels, dtype=BF16),
+            "sums": shape(units, chips, 16, channels, dtype=BF16),
+            "gained": shape(units, chips, 16, channels, dtype=BF16),
+            "own_norm": shape(2, channels, LANES),
+        })
+        sems["unit_sems"] = (8, units)
+    else:
+        outs.update(grads)
+    vmem = pl.BlockSpec(memory_space=pltpu.VMEM)
+    names = list(inputs) + list(outs) + list(scratch) + list(sems)
+    results = pl.pallas_call(
+        functools.partial(kernel, plan, names),
+        out_shape=list(outs.values()),
+        in_specs=[pl.BlockSpec(memory_space=pltpu.SMEM) if name == "lens" else vmem for name in inputs],
+        out_specs=[vmem] * len(outs),
+        scratch_shapes=[pltpu.VMEM(v.shape, v.dtype) for v in scratch.values()]
+        + [pltpu.SemaphoreType.DMA(v) for v in sems.values()],
+        compiler_params=pltpu.CompilerParams(
+            collective_id=0, has_side_effects=True, vmem_limit_bytes=62 * 1024 * 1024),
+    )(*inputs.values())
+    return dict(zip(outs, results, strict=True))
 
 
 def body(frames, dw_first, dw_second, point, gains, shifts, se_down, se_up, cotangent, lengths, *, devices):
@@ -612,105 +967,56 @@
     hidden = se_down.shape[2]
     channels = point.shape[3]
     plan = Plan(cotangent.shape[0], channels, taps_first, taps_second, sub, hidden, devices)
-    halves, Q = plan.halves, plan.steps
+    if plan.fused:
+        res = call_kernel(plan, {
+            "lens": lengths, "frames": frames, "cot": cotangent, "dw_first": dw_first, "dw_second": dw_second,
+            "point_in": point, "gains_in": gains, "shifts_in": shifts, "se_down": se_down, "se_up": se_up})
+        return tuple(res[name] for name in (
+            "out", "frames_grad", "dw_first_out", "dw_second_out", "point_out", "gains_out", "shifts_out",
+            "squeeze_out", "expand_out"))
+
+    per, layers, halves = plan.per, plan.layers, plan.halves
 
     def gather(v, axis):
         return lax.all_gather(v, "dp", axis=axis, tiled=True)
-
     small = jnp.concatenate([
         dw_first.reshape(-1, shard), dw_second.reshape(-1, shard), gains.reshape(-1, shard),
         shifts.reshape(-1, shard), se_up.reshape(-1, shard),
         jnp.swapaxes(se_down, 1, 2).reshape(-1, shard)], axis=0)
-    small = gather(small, 1)
-    n1, n2, ng, ns = sub * taps_first, sub * taps_second, 2 * (sub + 1), 2 * hidden
-    cuts = [0, n1, n1 + n2, n1 + n2 + ng, n1 + n2 + 2 * ng, n1 + n2 + 2 * ng + ns, n1 + n2 + 2 * ng + 2 * ns]
-    part = [small[cuts[i]:cuts[i + 1]] for i in range(6)]
-    K = 32
+    small = gather(small, 1).astype(F32)
+    sizes = [sub * taps_first, sub * taps_second, layers, layers, 2 * hidden, 2 * hidden]
+    part = jnp.split(small, [sum(sizes[:i]) for i in range(1, 6)], axis=0)
 
     def dw_layout(v, taps):
-        v = v.astype(F32).reshape(sub, taps, halves, LANES).transpose(0, 2, 1, 3)
-        return jnp.pad(v, ((0, 0), (0, 0), (0, K - taps), (0, 0)))
-    dw = jnp.concatenate([dw_layout(part[0], taps_first), dw_layout(part[1], taps_second)], axis=0)
-
-    def norm_layout(v):
-        v = v.astype(F32).reshape(2, sub + 1, halves, LANES)
-        return jnp.concatenate([v[:, :sub].reshape(2 * sub, halves, LANES), v[:, sub]], axis=0)
-    matrices = gather(point, 2)
-    matrices = jnp.concatenate([matrices[:, :sub].reshape(2 * sub, channels, channels), matrices[:, sub]], axis=0)
-    expand = part[4].astype(F32).reshape(2, hidden, channels)
-    squeeze_t = part[5].astype(F32).reshape(2, hidden, channels)
-
-    layers = 2 * sub + 2
-    slots = 2 * layers
-    shapes = (
-        jax.ShapeDtypeStruct((plan.slots, channels), F32),
-        jax.ShapeDtypeStruct((2 * plan.slots, channels), F32),
-        jax.ShapeDtypeStruct((2 * sub, halves, K, LANES), F32),
-        jax.ShapeDtypeStruct((layers, channels, channels), F32),
-        jax.ShapeDtypeStruct((layers, halves, LANES), F32),
-        jax.ShapeDtypeStruct((layers, halves, LANES), F32),
-        jax.ShapeDtypeStruct((2, hidden, channels), F32),
-        jax.ShapeDtypeStruct((2, hidden, channels), F32),
-    )
-    vmem = pl.BlockSpec(memory_space=pltpu.VMEM)
-    results = pl.pallas_call(
-        functools.partial(kernel, plan),
-        out_shape=shapes,
-        in_specs=[pl.BlockSpec(memory_space=pltpu.SMEM)] + [vmem] * 8,
-        out_specs=[vmem] * len(shapes),
-        scratch_shapes=[
-            pltpu.VMEM((2 * sub + 1, halves, plan.pad, 8, LANES), F32),
-            pltpu.VMEM((layers, plan.rows, channels), BF16),
-            pltpu.VMEM((layers, halves, Q, 8, LANES), F32),
-            pltpu.VMEM((halves, plan.pad, 8, LANES), F32),
-            pltpu.VMEM((halves, Q, 8, LANES), F32),
-            pltpu.VMEM((plan.rows, channels), BF16),
-            pltpu.VMEM((plan.rows, channels), BF16),
-            pltpu.VMEM((2, halves, Q, 8, LANES), F32),
-            pltpu.VMEM((halves, plan.slots + 2 * GAP, LANES), F32),
-            pltpu.VMEM((halves, 2 * plan.slots + 4 * GAP, LANES), F32),
-            pltpu.VMEM((Q, 8, LANES), F32),
-            pltpu.VMEM((Q, 8, LANES), F32),
-            pltpu.VMEM((Q, 8, LANES), F32),
-            pltpu.VMEM((layers, 8, LANES), F32),
-            pltpu.VMEM((slots, 4, LANES), F32),
-            pltpu.VMEM((layers, devices, 4, LANES), F32),
-            pltpu.VMEM((devices, 4, LANES), F32),
-            pltpu.VMEM((4, LANES), F32),
-            pltpu.SemaphoreType.DMA((slots,)),
-            pltpu.SemaphoreType.DMA((slots,)),
-            pltpu.SemaphoreType.DMA((2,)),
-        ],
-        compiler_params=pltpu.CompilerParams(
-            collective_id=0, has_side_effects=True, vmem_limit_bytes=62 * 1024 * 1024),
-    )(lengths, frames, cotangent, dw, matrices, norm_layout(gains_full(part[2], sub, channels)),
-      norm_layout(gains_full(part[3], sub, channels)), squeeze_t, expand)
-    output, frames_grad, dwg, pg, gg, sg, sqg, exg = results
+        v = v.reshape(sub, taps, halves, LANES).transpose(0, 2, 1, 3)
+        return jnp.pad(v, ((0, 1), (0, 0), (0, plan.tap_rows - taps), (0, 0)))
+    res = call_kernel(plan, {
+        "lens": lengths, "frames": frames, "cot": cotangent,
+        "dw": jnp.concatenate([dw_layout(part[0], taps_first), dw_layout(part[1], taps_second)], axis=0),
+        "point": gather(point, 2).reshape(layers, channels, channels),
+        "gains": part[2].reshape(layers, halves, LANES),
+        "shifts": part[3].reshape(layers, halves, LANES),
+        "squeeze_t": part[5].reshape(2, hidden, channels),
+        "expand": part[4].reshape(2, hidden, channels)})
 
     def scatter(v, axis):
         return lax.psum_scatter(v, "dp", scatter_dimension=axis, tiled=True)
 
     def dw_out(v, taps):
-        return v[:, :, :taps].transpose(0, 2, 1, 3).reshape(sub * taps, channels)
-    packed = jnp.concatenate([dw_out(dwg[:sub], taps_first), dw_out(dwg[sub:], taps_second),
-                              sqg.reshape(-1, channels), exg.reshape(-1, channels)], axis=0)
-    packed = scatter(packed, 1)
-    g1 = packed[:n1].reshape(sub, taps_first, shard)
-    g2 = packed[n1:n1 + n2].reshape(sub, taps_second, shard)
-    gsq = jnp.swapaxes(packed[n1 + n2:n1 + n2 + ns].reshape(2, hidden, shard), 1, 2)
-    gex = packed[n1 + n2 + ns:].reshape(2, hidden, shard)
-    pg = jnp.concatenate([pg[:2 * sub].reshape(2, sub, channels, channels), pg[2 * sub:][:, None]], axis=1)
-    pg = scatter(pg, 2)
+        return v[:sub, :, :taps].transpose(0, 2, 1, 3).reshape(sub * taps, channels)
+    grads = res["dw_grad"]
+    packed = scatter(jnp.concatenate(
+        [dw_out(grads[:per], taps_first), dw_out(grads[per:], taps_second),
+         res["squeeze_grad"].reshape(-1, channels), res["expand_grad"].reshape(-1, channels)], axis=0), 1)
+    g1, g2, gsq, gex = jnp.split(packed, [sizes[0], sizes[0] + sizes[1], sizes[0] + sizes[1] + sizes[5]], axis=0)
 
     def norm_out(v):
-        v = v.reshape(layers, channels)
-        v = jnp.concatenate([v[:2 * sub].reshape(2, sub, channels), v[2 * sub:][:, None]], axis=1)
-        return lax.dynamic_slice_in_dim(v, lax.axis_index("dp") * shard, shard, 2)
-    return (output, frames_grad, g1, g2, pg, norm_out(gg), norm_out(sg), gsq, gex)
-
-
-def gains_full(v, sub, channels):
-    return v.reshape(2, sub + 1, channels)
+        return lax.dynamic_slice_in_dim(v.reshape(2, per, channels), lax.axis_index("dp") * shard, shard, 2)
+    return (
+        res["out"], res["frames_grad"], g1.reshape(sub, taps_first, shard), g2.reshape(sub, taps_second, shard),
+        scatter(res["point_grad"].reshape(2, per, channels, channels), 2),
+        norm_out(res["gains_grad"]), norm_out(res["shifts_grad"]),
+        jnp.swapaxes(gsq.reshape(2, hidden, shard), 1, 2), gex.reshape(2, hidden, shard))
 
 
 def solution(mesh):

time: 512 us -> 230 us (0.45)
  waiting for transfers between devices: 234 us -> 0 us
  blocking collectives: 44 us -> 0 us
  Pallas kernels: 190 us -> 210 us
  between operations: 14 us -> 0.67 us
  other arithmetic: 6.15 us -> 0 us
    unnamed x4 -> x0, waiting for transfers between devices: 128 us -> none
    reduce_scatter x1 -> x0, waiting for transfers between devices: 99.2 us -> none  [scatter(): return lax.psum_scatter(v, 'dp', scatter_dimension=axis, tiled=True)]
    all_gather x1 -> x0, blocking collectives: 44 us -> none  [gather(): return lax.all_gather(v, 'dp', axis=axis, tiled=True)]
    pallas_call x1, Pallas kernels: 190 us -> 210 us  [call_kernel(): pl.pallas_call(functools.partial(kernel, plan, names), out_shape=list(out...]
    all_gather x1 -> x0, waiting for transfers between devices: 7.34 us -> none  [gather(): return lax.all_gather(v, 'dp', axis=axis, tiled=True)]
    pallas_call x0 -> x5, local copies, waits for them, and re-layouts: none -> 7.33 us  [call_kernel(): pl.pallas_call(functools.partial(kernel, plan, names), out_shape=list(out...]
    unnamed x41 -> x15, local copies, waits for them, and re-layouts: 13.8 us -> 11.6 us
  transfers between devices with their start and end apart: 3 -> 0, of which waited for: 3 -> 0; matrix products, arithmetic and copies ran while one was open for 3% -> 0% of each run, Pallas kernels for 0% -> 0%
where the time goes in v2:
time: 230 us; the launch traced here: 229 us
  Pallas kernels  210 us (91%)
  local copies, waits for them, and re-layouts  19 us (8%)
    pallas_call x1, Pallas kernels, call_kernel(): pl.pallas_call(functools.partial(kernel, plan, names), out_shape=list(out...  210 us
    unnamed x15, local copies, waits for them, and re-layouts  11.6 us
    pallas_call x5, local copies, waits for them, and re-layouts, call_kernel(): pl.pallas_call(functools.partial(kernel, plan, names), out_shape=list(out...  7.33 us

profile of v2, /device:TPU:0, one launch (start us, length us, event | category | flops | bytes accessed | tf_op | source)
XLA Modules:
  0.0 229.2 jit_solution(11418889517886802937)
XLA Ops:
  0.6 1.3 copy.21.refs_6_
  1.9 1.3 copy.22.refs_7_
  3.2 1.4 copy.23.refs_9_
  4.6 1.4 copy.19.refs_3_
  6.0 1.4 copy.20.refs_4_
  7.4 209.6 %shard_map.169 = (f32[1024,256]{1,0:T(8,128)}, f32[2048,256]{1,0:T(8,128)}, f32[5,25,8]{2,1,0:T(8,128)}, f32[5,27,8]{2,1,0:T(8,128)}, f32[2,6,8,256]{3,2,1,0:T(8...) custom-call(s32[2]{0:T(128)} %refs_0_.1, ...), custom_call_target="tpu_custom_call" | custom-call | tf_op jit(solution)/shard_map/pallas_call | solution.py:951
  217.1 0.0 copy-start
  217.1 1.4 copy.26
  218.5 1.3 copy.27
  219.8 1.4 copy.28
  221.2 1.6 copy.24
  222.8 1.6 copy.25
  224.4 2.3 copy.33
  226.7 0.0 copy-done
  226.7 0.0 copy-start.1
  226.7 0.0 copy-start.2
  226.7 1.3 copy.34
  228.0 0.0 copy-done.1
  228.0 0.6 copy.35
  228.6 0.0 copy-done.2
  228.7 0.6 copy.36
Async XLA Ops:
  217.1 9.6 %copy-start = (f32[2048,256]{1,0:T(8,128)S(1)}, f32[2048,256]{1,0:T(8,128)}, u32[]{:S(2)}) copy-start(f32[2048,256]{1,0:T(8,128)} %get-tuple-element.28) | copy-start | bytes 6291460
  226.7 1.3 copy-start.1
  226.7 2.0 copy-start.2

commit v3 on v2

--- a/solution.py
+++ b/solution.py
@@ -40,6 +40,8 @@
         self.per = sub_blocks + 1
         self.layers = 2 * self.per
         self.tap_rows = 32
+        self.tap_sets = (32, 48, 64, 80)
+        self.dw_rows = 96
         self.values = 2 * LANES
         self.shard = channels // devices
         self.fused = self.shard == 8 and devices % 2 == 0 and sub_blocks == 5 and hidden == 32 and self.max_taps <= 32
@@ -105,7 +107,8 @@
     squeeze_t, expand = k.squeeze_t, k.expand
     out, frames_grad = k.out, k.frames_grad
     hid, acts, prods, gd, gz, gpb, gqb, pre = k.hid, k.acts, k.prods, k.gd, k.gz, k.gpb, k.gqb, k.pre
-    flat, wide, first_mask, second_mask, valid, stats = k.flat, k.wide, k.first_mask, k.second_mask, k.valid, k.stats
+    wide, first_mask, valid, stats = k.wide, k.first_mask, k.valid, k.stats
+    flat = wide.at[:, pl.ds(0, plan.slots + 2 * GAP)]
     send4, recv4, counts, csend = k.send4, k.recv4, k.counts, k.csend
     send_sem, recv_sem, count_sems = k.send_sem, k.recv_sem, k.count_sems
     N = plan.devices
@@ -129,9 +132,6 @@
     half0 = len0 // 2
     half1 = len1 // 2
     count = (half0 + half1).astype(F32)
-    inv_half = (1.0 / jnp.full((1, LANES), half0, jnp.int32).astype(F32),
-                1.0 / jnp.full((1, LANES), half1, jnp.int32).astype(F32))
-
     def steps_loop(width, body, init=0):
         return lax.fori_loop(0, Q // width, lambda i, c: body(i * width, c), init)
 
@@ -141,7 +141,6 @@
         a = (slot < half0).astype(F32)
         b = jnp.logical_and(slot >= half0 + GAP, slot < half0 + GAP + half1).astype(F32)
         first_mask[pl.ds(t0, RF)] = a
-        second_mask[pl.ds(t0, RF)] = b
         valid[pl.ds(t0, RF)] = a + b
         return c
 
@@ -172,7 +171,7 @@
         def deinterleave(t0, c):
             for j in range(RF):
                 a_mask = first_mask[t0 + j]
-                b_mask = second_mask[t0 + j]
+                b_mask = valid[t0 + j] - a_mask
                 for h in HV:
                     a = wide[h, pl.ds(2 * (t0 + j) + 2 * GAP + phase, 8, stride=2 * Q)]
                     b = wide[h, pl.ds(2 * (t0 + j) + phase, 8, stride=2 * Q)]
@@ -182,19 +181,27 @@
         for h in HV:
             set_halo(hid.at[phase], h)
 
+    def spread_lanes(values, lane):
+        k.tile[...] = jnp.zeros((8, LANES), F32)
+        k.tile[:, 0:values.shape[1]] = values
+        return pltpu.roll(k.tile[...], lane, 1) if lane else k.tile[...]
+
     def load_shard():
         for b in range(2):
             source = (k.dw_first, k.dw_second)[b]
-            k.packed[...] = jnp.zeros((plan.values, LANES), F32)
+            tiles = [jnp.zeros((8, LANES), F32) for _ in range(2)]
             for r in range(SUB):
-                k.packed[pl.ds(plan.tap_row(r), plan.taps[b]), 0:plan.shard] = source[r].astype(F32)
-            k.packed[EXPAND_ROW:EXPAND_ROW + plan.hidden, 0:plan.shard] = k.se_up[b].astype(F32)
-            k.packed[GAIN_ROW:GAIN_ROW + PER, 0:plan.shard] = k.gains_in[b].astype(F32)
-            k.packed[SHIFT_ROW:SHIFT_ROW + PER, 0:plan.shard] = k.shifts_in[b].astype(F32)
+                tile, lane = divmod(plan.tap_row(r), LANES)
+                tiles[tile] = tiles[tile] + spread_lanes(source[r].astype(F32), lane)
+            tiles[1] = tiles[1] + spread_lanes(k.se_up[b].astype(F32), EXPAND_ROW - LANES)
+            tiles[1] = tiles[1] + spread_lanes(k.se_down[b].astype(F32), SQUEEZE_ROW - LANES)
+            k.packed[0:LANES] = jnp.zeros((LANES, LANES), F32)
+            for r in range(PER):
+                k.packed[GAIN_ROW - LANES + r:GAIN_ROW - LANES + r + 1, 0:8] = k.gains_in[r, b:b + 1].astype(F32)
+                k.packed[SHIFT_ROW - LANES + r:SHIFT_ROW - LANES + r + 1, 0:8] = k.shifts_in[r, b:b + 1].astype(F32)
+            tiles[1] = tiles[1] + jnp.transpose(k.packed[0:LANES])[0:8]
             for tile in range(2):
-                k.packed_t[8 * b:8 * b + 8, tile * LANES:(tile + 1) * LANES] = jnp.transpose(
-                    k.packed[tile * LANES:(tile + 1) * LANES])[0:8]
-            k.packed_t[8 * b:8 * b + 8, SQUEEZE_ROW:SQUEEZE_ROW + plan.hidden] = k.se_down[b].astype(F32)
+                k.packed_t[8 * b:8 * b + 8, tile * LANES:(tile + 1) * LANES] = tiles[tile]
         k.gath[0, chip, core] = k.packed_t[...].astype(BF16)
         for pair in range(PER):
             rows = [k.point_in[i // PER, i % PER].astype(F32) for i in (2 * pair, 2 * pair + 1)]
@@ -219,6 +226,19 @@
         view = k.gath.at[unit, :, 0]
         pltpu.make_async_copy(view, view, k.unit_sems.at[3, unit]).wait()
 
+    def split_taps(b, r, h):
+        taps = plan.taps[b]
+        row0, row1, row2, row3 = plan.tap_sets
+        low, high = (taps + 1) // 2, taps // 2
+        rows = [dw[b * PER + r, h, t:t + 1] for t in range(taps)] + [jnp.zeros((1, LANES), F32)]
+        dw[b * PER + r, h, row0:row0 + low] = jnp.concatenate(rows[0:taps:2], axis=0)
+        dw[b * PER + r, h, row1:row1 + high] = jnp.concatenate(rows[1:taps:2], axis=0)
+        dw[b * PER + r, h, row2:row2 + low] = jnp.concatenate(
+            [rows[2 * j + 1] - rows[2 * j] for j in range(low)], axis=0)
+        back = rows[taps - 1::-1] + [rows[taps]]
+        dw[b * PER + r, h, row3:row3 + low] = jnp.concatenate(
+            [back[2 * j + 1] - back[2 * j] for j in range(low)], axis=0)
+
     def unpack_values():
         got = k.gath[0].astype(F32).reshape(N, 16, plan.values)
         for b in range(2):
@@ -228,7 +248,8 @@
                     part = block[h * LANES:(h + 1) * LANES, tile * LANES:(tile + 1) * LANES]
                     k.unpacked[tile * LANES:(tile + 1) * LANES] = jnp.transpose(part)
                 for r in range(SUB):
-                    dw[b * PER + r, h] = k.unpacked[plan.tap_row(r):plan.tap_row(r) + plan.tap_rows]
+                    dw[b * PER + r, h, 0:plan.tap_rows] = k.unpacked[plan.tap_row(r):plan.tap_row(r) + plan.tap_rows]
+                    split_taps(b, r, h)
                 for r in range(PER):
                     gains[b * PER + r, h:h + 1] = k.unpacked[GAIN_ROW + r:GAIN_ROW + r + 1]
                     shifts[b * PER + r, h:h + 1] = k.unpacked[SHIFT_ROW + r:SHIFT_ROW + r + 1]
@@ -241,6 +262,7 @@
         for side in range(2):
             block = got[:, 8 * side:8 * side + 8].reshape(plan.channels, plan.channels)
             point[2 * pair + side] = block.astype(BF16)
+            k.point_t[2 * pair + side] = jnp.transpose(block).astype(BF16)
 
     if plan.fused:
         load_shard()
@@ -282,24 +304,6 @@
 
     def accumulate(rows3):
         return jnp.sum(rows3, axis=0)
-
-    def local_stats(index):
-        def total(t0, c):
-            v = valid[pl.ds(t0, R)]
-            return tuple(c[h] + accumulate(prods[index, h, pl.ds(t0, R)] * v) for h in HV)
-        zeros = tuple(jnp.zeros((8, LANES), F32) for h in HV)
-        sums = steps_loop(R, total, zeros)
-        means = [jnp.sum(sums[h], axis=0, keepdims=True) / jnp.full((1, LANES), count, F32) for h in HV]
-
-        def squares(t0, c):
-            v = valid[pl.ds(t0, R)]
-            res = []
-            for h in HV:
-                d = (prods[index, h, pl.ds(t0, R)] - row(means[h])) * v
-                res.append(c[h] + accumulate(d * d))
-            return tuple(res)
-        sq = steps_loop(R, squares, zeros)
-        return jnp.concatenate(means + [jnp.sum(sq[h], axis=0, keepdims=True) for h in HV], axis=0)
 
     def merge_stats(slot, index):
         got = received(slot, slot)
@@ -319,40 +323,87 @@
     def stat_row(index, kind, h):
         return row(stats[index, pl.ds(2 * kind + h, 1)])
 
+    def tap(index, h, t):
+        return dw[index, h, pl.ds(t, 1)].reshape(1, 1, LANES)
+
+    def direct(win, low, index, h, taps):
+        acc = None
+        for t, shift in taps:
+            term = win[shift - low:shift - low + R] * tap(index, h, t)
+            acc = term if acc is None else acc + term
+        return acc
+
+    def paired(win, index, h, taps, back):
+        low, high = (taps + 1) // 2, taps // 2
+        row0, row1, row2, row3 = plan.tap_sets
+        m = R // 2
+        split = win.reshape(-1, 2, 8, LANES)
+        x0, x1 = split[:, 0], split[:, 1]
+        both = x0[:m + low - 1] + x1[:m + low - 1]
+        late = x0[1:m + high] + x1[:m + high - 1]
+
+        def run(x, count, row):
+            acc = None
+            for j in range(count):
+                term = x[j:j + m] * tap(index, h, row(j))
+                acc = term if acc is None else acc + term
+            return acc
+        shared = run(x1, low, lambda j: (row3 if back else row2) + j)
+        first = run(both, low, lambda j: row0 + (low - 1 - j if back else j)) + shared
+        second = run(late, high, lambda j: row1 + (high - 1 - j if back else j)) - shared
+        return jnp.stack([first, second], axis=1).reshape(R, 8, LANES)
+
     def layer_conv(index, pieces):
         def body(t0, c):
             for h in HV:
                 acc = None
-                for source, taps in pieces:
-                    low = min(s for _, s in taps)
-                    high = max(s for _, s in taps)
-                    win = hid[source, h, pl.ds(t0 + HALO + low, R + high - low)]
-                    for tap, shift in taps:
-                        term = win[shift - low:shift - low + R] * dw[index, h, pl.ds(tap, 1)].reshape(1, 1, LANES)
-                        acc = term if acc is None else acc + term
+                if len(pieces) == 1:
+                    source, taps = pieces[0]
+                    low = taps[0][1]
+                    acc = paired(hid[source, h, pl.ds(t0 + HALO + low, R + len(taps) - 1)], index, h, len(taps), False)
+                else:
+                    for source, taps in pieces:
+                        low, high = taps[0][1], taps[-1][1]
+                        part = direct(hid[source, h, pl.ds(t0 + HALO + low, R + high - low)], low, index, h, taps)
+                        acc = part if acc is None else acc + part
                 rows = pl.ds(pl.multiple_of(8 * t0, 16), 8 * R)
                 acts[index, rows, h * LANES:(h + 1) * LANES] = acc.reshape(8 * R, LANES).astype(BF16)
             return c
         steps_loop(R, body)
 
-    def pointwise(act, index):
-        def body(t0, c):
-            rows = pl.ds(pl.multiple_of(8 * t0, 16), 8 * R)
-            res = jnp.dot(acts[act, rows], point[index], preferred_element_type=F32)
-            for h in HV:
-                prods[index, h, pl.ds(t0, R)] = res[:, h * LANES:(h + 1) * LANES].reshape(R, 8, LANES)
-            return c
-        steps_loop(R, body)
+    def half_lanes(values, h):
+        return values[:, h * LANES:(h + 1) * LANES]
+
+    def pointwise(index):
+        pivot = [None] * plan.halves
+        sums = [jnp.zeros((8, LANES), F32) for _ in HV]
+        squares = [jnp.zeros((8, LANES), F32) for _ in HV]
+        for t0 in range(0, Q, R):
+            res = jnp.dot(acts[index, 8 * t0:8 * (t0 + R)], point[index], preferred_element_type=F32)
+            v = valid[t0:t0 + R]
+            for h in HV:
+                p = half_lanes(res, h).reshape(R, 8, LANES)
+                prods[index, h, t0:t0 + R] = p
+                if t0 == 0:
+                    pivot[h] = p[0, 0:1]
+                d = p - row(pivot[h])
+                dv = d * v
+                sums[h] = sums[h] + accumulate(dv)
+                squares[h] = squares[h] + accumulate(dv * d)
+        n = jnp.full((1, LANES), count, F32)
+        shift = [jnp.sum(sums[h], axis=0, keepdims=True) / n for h in HV]
+        spread = [jnp.sum(squares[h], axis=0, keepdims=True) - n * shift[h] * shift[h] for h in HV]
+        return jnp.concatenate([pivot[h] + shift[h] for h in HV] + spread, axis=0)
 
     def activate(index, target):
-        scales = [stat_row(index, 2, h) for h in HV]
-        offsets = [stat_row(index, 3, h) for h in HV]
+        scales = [0.5 * stat_row(index, 2, h) for h in HV]
+        offsets = [0.5 * stat_row(index, 3, h) for h in HV]
 
         def body(t0, c):
             v = valid[pl.ds(t0, RF)]
             for h in HV:
-                z = prods[index, h, pl.ds(t0, RF)] * scales[h] + offsets[h]
-                hid[target, h, pl.ds(HALO + t0, RF)] = z * sigmoid(z) * v
+                u = prods[index, h, pl.ds(t0, RF)] * scales[h] + offsets[h]
+                hid[target, h, pl.ds(HALO + t0, RF)] = (u + u * jnp.tanh(u)) * v
             return c
         steps_loop(RF, body)
         for h in HV:
@@ -384,61 +435,96 @@
                 acts[res, rows, h * LANES:(h + 1) * LANES] = values.astype(BF16)
             return c
         steps_loop(R, body)
-        pointwise(res, res)
-        exchange(res, res, local_stats(res))
-
-    def pair_rows(values):
-        return jnp.concatenate([values, jnp.zeros((6, plan.channels), F32)], axis=0)
+        exchange(res, res, pointwise(res))
 
     def small(a, b, dims):
         return lax.dot_general(a, b, (dims, ((), ())), precision=HIGHEST, preferred_element_type=F32)
 
+    def thin(a, matrix, dim):
+        hi = a.astype(BF16).astype(F32)
+        mid = (a - hi).astype(BF16).astype(F32)
+        low = a - hi - mid
+        rows = jnp.concatenate([hi, mid, low, jnp.zeros_like(a)], axis=0).astype(BF16)
+        res = lax.dot_general(rows, matrix.astype(BF16), (((1,), (dim,)), ((), ())), preferred_element_type=F32)
+        return res[0:2] + res[2:4] + res[4:6]
+
+    def eight(values):
+        return jnp.concatenate([values, jnp.zeros((6, values.shape[1]), F32)], axis=0)
+
+    def whole_row(index, kind):
+        return jnp.concatenate([stats[index, pl.ds(2 * kind + h, 1)] for h in HV], axis=1)
+
+    def join(parts):
+        return jnp.concatenate([jnp.sum(part, axis=0, keepdims=True) for part in parts], axis=1)
+
+    half_count = [jnp.full((1, plan.channels), n, jnp.int32).astype(F32) for n in (half0, half1)]
+
+    def utterance_sums(b):
+        last = b * PER + SUB - 1
+
+        def sums(t0, c):
+            a = first_mask[pl.ds(t0, RF)]
+            s = valid[pl.ds(t0, RF)] - a
+            res = []
+            for h in HV:
+                p = prods[last, h, pl.ds(t0, RF)]
+                res += [c[2 * h] + accumulate(p * a), c[2 * h + 1] + accumulate(p * s)]
+            return tuple(res)
+        tot = steps_loop(RF, sums, tuple(jnp.zeros((8, LANES), F32) for _ in range(2 * plan.halves)))
+        for u in range(2):
+            k.psum[b, u:u + 1] = join([tot[2 * h + u] for h in HV])
+
     def excite(b):
         last = b * PER + SUB - 1
-        scales = [stat_row(last, 2, h) for h in HV]
-        offsets = [stat_row(last, 3, h) for h in HV]
-
-        def sums(t0, c):
-            a, s = first_mask[pl.ds(t0, RF)], second_mask[pl.ds(t0, RF)]
-            res = []
-            for h in HV:
-                z = prods[last, h, pl.ds(t0, RF)] * scales[h] + offsets[h]
-                res.append(c[2 * h] + accumulate(z * a))
-                res.append(c[2 * h + 1] + accumulate(z * s))
-            return tuple(res)
-        tot = steps_loop(RF, sums, tuple(jnp.zeros((8, LANES), F32) for _ in range(2 * plan.halves)))
-        means = jnp.concatenate(
-            [jnp.concatenate([jnp.sum(tot[2 * h + u], axis=0, keepdims=True) * inv_half[u] for h in HV], axis=1)
-             for u in range(2)], axis=0)
-        means = pair_rows(means)
-        inner = small(means, squeeze_t[b], ((1,), (1,)))
+        scale, offset = whole_row(last, 2), whole_row(last, 3)
+        means = jnp.concatenate([scale * (k.psum[b, u:u + 1] / half_count[u]) + offset for u in range(2)], axis=0)
+        inner = thin(means, squeeze_t[b], 1)
         excited = inner * sigmoid(inner)
-        gate = sigmoid(small(excited, expand[b], ((1,), (0,))))
+        gate = sigmoid(thin(excited, expand[b], 0))
         return means, inner, excited, gate
 
-    def gate_rows(gate):
-        return [[row(gate[u:u + 1, h * LANES:(h + 1) * LANES]) for h in HV] for u in range(2)]
+    def tail_half(b, gate):
+        last, res = b * PER + SUB - 1, b * PER + SUB
+        consts = []
+        for h in HV:
+            g = [half_lanes(gate[u:u + 1], h) for u in range(2)]
+            s1, o1, s2, o2 = [0.5 * stats[i, pl.ds(2 * kind + h, 1)] for i, kind in
+                              ((last, 2), (last, 3), (res, 2), (res, 3))]
+            consts.append([row(v) for v in (s1 * g[0], s1 * g[1], s2, o1 * g[0] + o2, o1 * g[1] + o2)])
+
+        def get(t0, h):
+            a0, a1, s2, b0, b1 = consts[h]
+            a = first_mask[pl.ds(t0, RF)] > 0.5
+            return (prods[last, h, pl.ds(t0, RF)] * jnp.where(a, a0, a1)
+                    + prods[res, h, pl.ds(t0, RF)] * s2 + jnp.where(a, b0, b1))
+        return get
 
     def tail(b, gate, store):
-        last, res = b * PER + SUB - 1, b * PER + SUB
-        gates = gate_rows(gate)
-        consts = [(stat_row(last, 2, h), stat_row(last, 3, h), stat_row(res, 2, h), stat_row(res, 3, h)) for h in HV]
+        get = tail_half(b, gate)
 
         def body(t0, c):
             v = valid[pl.ds(t0, RF)]
-            a = first_mask[pl.ds(t0, RF)]
-            for h in HV:
-                s1, o1, s2, o2 = consts[h]
-                z = prods[last, h, pl.ds(t0, RF)] * s1 + o1
-                y = prods[res, h, pl.ds(t0, RF)] * s2 + o2
-                g = jnp.where(a > 0.5, gates[0][h], gates[1][h])
-                s = z * g + y
-                pre[b, h, pl.ds(t0, RF)] = s
-                store(t0, h, s * sigmoid(s) * v)
+            for h in HV:
+                u = get(t0, h)
+                store(t0, h, (u + u * jnp.tanh(u)) * v)
             return c
         steps_loop(RF, body)
 
-    def forward_aside(b, r):
+    def slope_of(u):
+        t = jnp.tanh(u)
+        return (0.5 * t + 0.5) * (1.0 + u - u * t)
+
+    def tail_slope(b, gate):
+        get = tail_half(b, gate)
+
+        def body(t0, c):
+            v = valid[pl.ds(t0, RF)]
+            for h in HV:
+                pre[b, h, pl.ds(t0, RF)] = slope_of(get(t0, h)) * v
+            return c
+        steps_loop(RF, body)
+
+    def forward_aside(b, r, extras):
         if plan.fused:
             step = b * SUB + r
 
@@ -459,15 +545,20 @@
         def _():
             residual_forward(b)
 
-    def forward_block(b):
+        @pl.when(r == SUB - 1)
+        def _():
+            utterance_sums(b)
+        for when, extra in extras:
+            pl.when(r == when)(extra)
+
+    def forward_block(b, extras=()):
         def layer(r, pieces, before=None):
             index = b * PER + r
             layer_conv(index, pieces)
             if before is not None:
                 before()
-            pointwise(index, index)
-            exchange(index, index, local_stats(index))
-            forward_aside(b, r)
+            exchange(index, index, pointwise(index))
+            forward_aside(b, r, extras)
             merge_stats(index, index)
 
         def first_matrices():
@@ -494,61 +585,68 @@
 
     def tail_back(b, kept, load):
         means, inner, excited, gate = kept
-        last, res = b * PER + SUB - 1, b * PER + SUB
-        gates = gate_rows(gate)
-        consts = [(stat_row(last, 2, h), stat_row(last, 3, h)) for h in HV]
+        last = b * PER + SUB - 1
+        mean = [stat_row(last, 0, h) for h in HV]
 
         def first(t0, c):
-            v = valid[pl.ds(t0, RF)]
-            a, q = first_mask[pl.ds(t0, RF)], second_mask[pl.ds(t0, RF)]
-            out_c = []
-            for h in HV:
-                s = pre[b, h, pl.ds(t0, RF)]
-                sg = sigmoid(s)
-                gs = load(t0, h) * (sg * (1.0 + s * (1.0 - sg))) * v
+            a = first_mask[pl.ds(t0, RF)]
+            res = []
+            for h in HV:
+                gs = load(t0, h)
                 pre[b, h, pl.ds(t0, RF)] = gs
-                z = prods[last, h, pl.ds(t0, RF)] * consts[h][0] + consts[h][1]
-                gsz = gs * z
-                out_c.append(c[2 * h] + accumulate(gsz * a))
-                out_c.append(c[2 * h + 1] + accumulate(gsz * q))
-            return tuple(out_c)
-        zero4 = tuple(jnp.zeros((8, LANES), F32) for _ in range(2 * plan.halves))
-        tot = steps_loop(RF, first, zero4)
-        grad_gate = pair_rows(jnp.concatenate(
-            [jnp.concatenate([jnp.sum(tot[2 * h + u], axis=0, keepdims=True) for h in HV], axis=1)
-             for u in range(2)], axis=0))
+                gx = gs * (prods[last, h, pl.ds(t0, RF)] - mean[h])
+                res += [c[4 * h] + accumulate(gs * a), c[4 * h + 1] + accumulate(gs),
+                        c[4 * h + 2] + accumulate(gx * a), c[4 * h + 3] + accumulate(gx)]
+            return tuple(res)
+        tot = steps_loop(RF, first, tuple(jnp.zeros((8, LANES), F32) for _ in range(4 * plan.halves)))
+        s0, s_all, x0, x_all = [join([tot[4 * h + i] for h in HV]) for i in range(4)]
+        gs_sum = (s0, s_all - s0)
+        gx_sum = (x0, x_all - x0)
+        mean_row, inv_row, scale_row = [whole_row(last, kind) for kind in range(3)]
+        shift_row = jnp.concatenate([shifts[last, h:h + 1] for h in HV], axis=1)
+        grad_gate = jnp.concatenate([scale_row * gx_sum[u] + shift_row * gs_sum[u] for u in range(2)], axis=0)
         grad_up = grad_gate * gate * (1.0 - gate)
-        k.expand_grad[b] = small(excited, grad_up, ((0,), (0,)))
-        grad_excited = small(grad_up, expand[b], ((1,), (1,)))
         sg = sigmoid(inner)
-        grad_inner = grad_excited * (sg * (1.0 + inner * (1.0 - sg)))
-        k.squeeze_grad[b] = small(grad_inner, means, ((0,), (0,)))
-        grad_means = small(grad_inner, squeeze_t[b], ((1,), (0,)))
-        mean_rows = [[row(grad_means[u:u + 1, h * LANES:(h + 1) * LANES] * inv_half[u]) for h in HV]
-                     for u in range(2)]
-        norm1 = [(stat_row(last, 0, h), stat_row(last, 1, h)) for h in HV]
-        norm2 = [(stat_row(res, 0, h), stat_row(res, 1, h)) for h in HV]
+        grad_inner = thin(grad_up, expand[b], 1) * (sg * (1.0 + inner * (1.0 - sg)))
+        grad_means = thin(grad_inner, squeeze_t[b], 0)
+        per_slot = [grad_means[u:u + 1] / half_count[u] for u in range(2)]
+        sum1, sum2 = 0.0, 0.0
+        for u in range(2):
+            g = gate[u:u + 1]
+            sum1 = sum1 + g * gs_sum[u] + grad_means[u:u + 1]
+            sum2 = sum2 + g * gx_sum[u] + per_slot[u] * (k.psum[b, u:u + 1] - half_count[u] * mean_row)
+        sum2 = sum2 * inv_row
+        exchange(back_slot + last, back_place(last),
+                 jnp.concatenate([half_lanes(v, h) for v in (sum1, sum2) for h in HV], axis=0))
+        return grad_up, grad_inner, per_slot
+
+    def tail_back_aside(b, kept, found):
+        means, inner, excited, gate = kept
+        grad_up, grad_inner, per_slot = found
+        res = b * PER + SUB
+        gates = [[row(half_lanes(gate[u:u + 1], h)) for h in HV] for u in range(2)]
+        slots = [[row(half_lanes(per_slot[u], h)) for h in HV] for u in range(2)]
+        norm = [(stat_row(res, 0, h), stats[res, pl.ds(2 + h, 1)]) for h in HV]
 
         def second(t0, c):
-            a = first_mask[pl.ds(t0, RF)]
+            a = first_mask[pl.ds(t0, RF)] > 0.5
             v = valid[pl.ds(t0, RF)]
             out_c = []
             for h in HV:
                 gs = pre[b, h, pl.ds(t0, RF)]
-                g = jnp.where(a > 0.5, gates[0][h], gates[1][h])
-                m = jnp.where(a > 0.5, mean_rows[0][h], mean_rows[1][h])
-                grad = gs * g + m * v
-                gz[h, pl.ds(t0, RF)] = grad
-                x1 = (prods[last, h, pl.ds(t0, RF)] - norm1[h][0]) * norm1[h][1]
-                x2 = (prods[res, h, pl.ds(t0, RF)] - norm2[h][0]) * norm2[h][1]
-                out_c += [c[4 * h] + accumulate(grad), c[4 * h + 1] + accumulate(grad * x1),
-                          c[4 * h + 2] + accumulate(gs), c[4 * h + 3] + accumulate(gs * x2)]
+                gz[h, pl.ds(t0, RF)] = (gs * jnp.where(a, gates[0][h], gates[1][h])
+                                        + jnp.where(a, slots[0][h], slots[1][h]) * v)
+                x = prods[res, h, pl.ds(t0, RF)] - norm[h][0]
+                out_c += [c[2 * h] + accumulate(gs), c[2 * h + 1] + accumulate(gs * x)]
             return tuple(out_c)
-        tot = steps_loop(RF, second, zero4 + zero4)
-        exchange(back_slot + last, back_place(last), sum_rows([tot[0], tot[4], tot[1], tot[5]]))
-        exchange(back_slot + res, back_place(res), sum_rows([tot[2], tot[6], tot[3], tot[7]]))
-
-    def norm_back(index, load, target):
+        tot = steps_loop(RF, second, tuple(jnp.zeros((8, LANES), F32) for _ in range(2 * plan.halves)))
+        sums = [jnp.sum(part, axis=0, keepdims=True) for part in tot]
+        exchange(back_slot + res, back_place(res), jnp.concatenate(
+            [sums[2 * h] for h in HV] + [sums[2 * h + 1] * norm[h][1] for h in HV], axis=0))
+        k.expand_grad[b] = small(eight(excited), eight(grad_up), ((0,), (0,)))
+        k.squeeze_grad[b] = small(eight(grad_inner), eight(means), ((0,), (0,)))
+
+    def norm_back(index, load, target, store):
         sums = jnp.sum(received(back_slot + index, back_place(index)), axis=0)
         k.shifts_grad[index] = sums[0:2]
         k.gains_grad[index] = sums[2:4]
@@ -558,25 +656,21 @@
         k1 = scale * sums[0:2] / total
         k2 = scale * sums[2:4] / total * inv
         rows3 = [[row(value[h:h + 1]) for value in (mean, scale, k1, k2)] for h in HV]
-
-        def body(t0, c):
-            v = valid[pl.ds(t0, R)]
-            rows = pl.ds(pl.multiple_of(8 * t0, 16), 8 * R)
+        for t0 in range(0, Q, R):
+            v = valid[t0:t0 + R]
+            parts = []
             for h in HV:
                 mean_h, scale_h, k1_h, k2_h = rows3[h]
-                grad = (scale_h * load(t0, h) - k1_h - k2_h * (prods[index, h, pl.ds(t0, R)] - mean_h)) * v
-                target[rows, h * LANES:(h + 1) * LANES] = grad.reshape(8 * R, LANES).astype(BF16)
-            return c
-        steps_loop(R, body)
-
-    def pointwise_back(index, source, store):
-        def body(t0, c):
-            rows = pl.ds(pl.multiple_of(8 * t0, 16), 8 * R)
-            res = lax.dot_general(source[rows], point[index], (((1,), (1,)), ((), ())), preferred_element_type=F32)
-            for h in HV:
-                store(t0, h, res[:, h * LANES:(h + 1) * LANES].reshape(R, 8, LANES))
-            return c
-        steps_loop(R, body)
+                grad = scale_h * load(t0, h) - (k1_h + k2_h * (prods[index, h, t0:t0 + R] - mean_h)) * v
+                parts.append(grad.reshape(8 * R, LANES).astype(BF16))
+            both = jnp.concatenate(parts, axis=1)
+            target[8 * t0:8 * (t0 + R)] = both
+            if plan.fused:
+                res = jnp.dot(both, k.point_t[index], preferred_element_type=F32)
+            else:
+                res = lax.dot_general(both, point[index], (((1,), (1,)), ((), ())), preferred_element_type=F32)
+            for h in HV:
+                store(t0, h, half_lanes(res, h).reshape(R, 8, LANES))
 
     def point_back(index, source):
         place = lax.rem(index, 2) if plan.fused else index
@@ -584,17 +678,17 @@
                                               preferred_element_type=F32)
 
     def store_gd(t0, h, values):
-        gd[h, pl.ds(HALO + t0, R)] = values
+        gd[h, HALO + t0:HALO + t0 + R] = values
+
+    def store_skip(t0, h, values):
+        k.skip[h, t0:t0 + R] = values
 
     def conv_back_block(t0, h, index, taps):
-        low = min(-s for _, s in taps)
-        high = max(-s for _, s in taps)
+        low, high = -taps[-1][1], -taps[0][1]
         win = gd[h, pl.ds(t0 + HALO + low, R + high - low)]
-        acc = None
-        for tap, shift in taps:
-            term = win[-shift - low:-shift - low + R] * dw[index, h, pl.ds(tap, 1)].reshape(1, 1, LANES)
-            acc = term if acc is None else acc + term
-        return acc
+        if len(taps) >= plan.taps[0]:
+            return paired(win, index, h, len(taps), True)
+        return direct(win, low, index, h, [(t, -shift) for t, shift in taps])
 
     def kernel_back(index, pieces):
         for source, taps in pieces:
@@ -610,28 +704,36 @@
                 for acc, (tap, _) in zip(accs, taps):
                     k.dw_grad[index, h, pl.ds(tap, 1)] = jnp.sum(acc, axis=0, keepdims=True)
 
+    def slopes(index):
+        scales = [0.5 * stat_row(index, 2, h) for h in HV]
+        offsets = [0.5 * stat_row(index, 3, h) for h in HV]
+
+        def body(t0, c):
+            v = valid[pl.ds(t0, RF)]
+            for h in HV:
+                k.slope[h, pl.ds(t0, RF)] = slope_of(prods[index, h, pl.ds(t0, RF)] * scales[h] + offsets[h]) * v
+            return c
+        steps_loop(RF, body)
+
     def hidden_back(index, taps):
         before = index - 1
-        consts = [[stat_row(before, kind, h) for kind in range(4)] for h in HV]
+        mean = [stat_row(before, 0, h) for h in HV]
 
         def body(t0, c):
-            v = valid[pl.ds(t0, R)]
             res = []
             for h in HV:
-                mean, inv, scale, offset = consts[h]
-                p = prods[before, h, pl.ds(t0, R)]
-                z = p * scale + offset
-                sg = sigmoid(z)
-                grad = conv_back_block(t0, h, index, taps) * (sg * (1.0 + z * (1.0 - sg))) * v
+                grad = conv_back_block(t0, h, index, taps) * k.slope[h, pl.ds(t0, R)]
                 gz[h, pl.ds(t0, R)] = grad
-                xhat = (p - mean) * inv
-                res += [c[2 * h] + accumulate(grad), c[2 * h + 1] + accumulate(grad * xhat)]
+                gx = grad * (prods[before, h, pl.ds(t0, R)] - mean[h])
+                res += [c[2 * h] + accumulate(grad), c[2 * h + 1] + accumulate(gx)]
             return tuple(res)
         tot = steps_loop(R, body, tuple(jnp.zeros((8, LANES), F32) for _ in range(2 * plan.halves)))
-        exchange(back_slot + before, back_place(before), sum_rows([tot[0], tot[2], tot[1], tot[3]]))
+        sums = [jnp.sum(part, axis=0, keepdims=True) for part in tot]
+        exchange(back_slot + before, back_place(before), jnp.concatenate(
+            [sums[2 * h] for h in HV] + [sums[2 * h + 1] * stats[before, pl.ds(2 + h, 1)] for h in HV], axis=0))
 
     def load_gz(t0, h):
-        return gz[h, pl.ds(t0, R)]
+        return gz[h, t0:t0 + R]
 
     def scatter_start(unit, place):
         pltpu.make_async_remote_copy(src_ref=k.shares.at[place, :, 1 - core], dst_ref=k.inbox.at[unit],
@@ -693,18 +795,21 @@
         mine = pl.ds(pl.multiple_of(me * 8, 8), 8)
         for b in range(2):
             rows = total[8 * b:8 * b + 8]
-            k.squeeze_out[b] = rows[:, SQUEEZE_ROW:SQUEEZE_ROW + plan.hidden]
-            fill = jnp.zeros((LANES - 8, LANES), F32)
-            for t in range(2):
-                k.packed[t * LANES:(t + 1) * LANES] = jnp.transpose(
-                    jnp.concatenate([rows[:, t * LANES:(t + 1) * LANES], fill], axis=0))
+
+            def lanes(start, size):
+                tile, lane = divmod(start, LANES)
+                part = rows[:, tile * LANES:(tile + 1) * LANES]
+                return (pltpu.roll(part, LANES - lane, 1) if lane else part)[:, 0:size]
             dw_out = (k.dw_first_out, k.dw_second_out)[b]
             for r in range(SUB):
-                dw_out[r] = k.packed[plan.tap_row(r):plan.tap_row(r) + plan.taps[b], 0:plan.shard]
-            k.expand_out[b] = k.packed[EXPAND_ROW:EXPAND_ROW + plan.hidden, 0:plan.shard]
-            k.packed[LANES:] = jnp.transpose(jnp.concatenate([k.own_norm[b, mine], fill], axis=0))
-            k.gains_out[b] = k.packed[GAIN_ROW:GAIN_ROW + PER, 0:plan.shard]
-            k.shifts_out[b] = k.packed[SHIFT_ROW:SHIFT_ROW + PER, 0:plan.shard]
+                dw_out[r] = lanes(plan.tap_row(r), plan.taps[b])
+            k.squeeze_out[b] = lanes(SQUEEZE_ROW, plan.hidden)
+            k.expand_out[b] = lanes(EXPAND_ROW, plan.hidden)
+            k.packed[0:LANES] = jnp.transpose(
+                jnp.concatenate([k.own_norm[b, mine], jnp.zeros((LANES - 8, LANES), F32)], axis=0))
+            for r in range(PER):
+                k.gains_out[r, b:b + 1] = k.packed[GAIN_ROW - LANES + r:GAIN_ROW - LANES + r + 1, 0:8]
+                k.shifts_out[r, b:b + 1] = k.packed[SHIFT_ROW - LANES + r:SHIFT_ROW - LANES + r + 1, 0:8]
 
     HALF = PER // 2
 
@@ -732,7 +837,7 @@
         @pl.when(r == SUB - 1)
         def _():
             res = b * PER + SUB
-            norm_back(res, lambda t0, h: pre[b, h, pl.ds(t0, R)], gqb)
+            norm_back(res, lambda t0, h: pre[b, h, t0:t0 + R], gqb, store_skip)
             point_back(res, gqb)
         if plan.fused:
             @pl.when(lax.rem(r, 2) == 0)
@@ -741,8 +846,7 @@
 
     def backward_block(b):
         def filtered(index):
-            norm_back(index, load_gz, gpb)
-            pointwise_back(index, gpb, store_gd)
+            norm_back(index, load_gz, gpb, store_gd)
             for h in HV:
                 set_halo(gd, h)
 
@@ -753,6 +857,10 @@
             hidden_back(index, regular_taps(b))
             backward_aside(b, r)
             kernel_back(index, [(hid_of(b, r), regular_taps(b))])
+
+            @pl.when(r >= 2)
+            def _():
+                slopes(index - 2)
             return c
         lax.fori_loop(0, SUB - 1, step, 0)
         filtered(b * PER)
@@ -762,6 +870,12 @@
             gather_forward(unit)
         gather_wait(0)
         unpack_values()
+    else:
+        dw[...] = k.dw_in[...]
+        for b in range(2):
+            for r in range(SUB):
+                for h in HV:
+                    split_taps(b, r, h)
     wait_all(counts, count_sems.at[1])
     kept_first = forward_block(0)
 
@@ -770,12 +884,38 @@
     tail(0, kept_first[3], store_middle)
     for h in HV:
         set_halo(hid.at[hid_of(1, 0)], h)
-    kept_second = forward_block(1)
+
+    def place_cot():
+        for h in HV:
+            flat[h, 0:GAP] = jnp.zeros((GAP, LANES), F32)
+            flat[h, GAP + plan.slots:] = jnp.zeros((flat.shape[1] - GAP - plan.slots, LANES), F32)
+
+        def place(i, c):
+            rows = pl.ds(pl.multiple_of(i * 128, 128), 128)
+            for h in HV:
+                flat[h, pl.ds(pl.multiple_of(i * 128 + GAP, 16), 128)] = cot[rows, h * LANES:(h + 1) * LANES]
+            return c
+        lax.fori_loop(0, plan.slots // 128, place, 0)
+
+        def pick(t0, c):
+            for h in HV:
+                for j in range(RF):
+                    here = flat[h, pl.ds(t0 + j + GAP, 8, stride=Q)]
+                    moved = flat[h, pl.ds(t0 + j, 8, stride=Q)]
+                    gz[h, t0 + j] = jnp.where(first_mask[t0 + j] > 0.5, here, moved)
+            return c
+        steps_loop(RF, pick)
+    kept_second = forward_block(1, ((0, lambda: tail_slope(0, kept_first[3])), (1, place_cot)))
+
+    last_half = tail_half(1, kept_second[3])
+
+    def load_last(t0, h):
+        return gz[h, pl.ds(t0, RF)] * (slope_of(last_half(t0, h)) * valid[pl.ds(t0, RF)])
+    found = tail_back(1, kept_second, load_last)
 
     def store_out(t0, h, values):
         for j in range(RF):
             flat[h, pl.ds(t0 + j, 8, stride=Q)] = values[j]
-    tail(1, kept_second[3], store_out)
 
     def ungap(i, c):
         rows = pl.ds(pl.multiple_of(i * 128, 128), 128)
@@ -784,40 +924,20 @@
             moved = flat[h, pl.ds(pl.multiple_of(i * 128 + GAP, 16), 128)]
             out[rows, h * LANES:(h + 1) * LANES] = jnp.where(slot < half0, flat[h, rows], moved)
         return c
+    tail_back_aside(1, kept_second, found)
+    slopes(PER + SUB - 2)
+    tail(1, kept_second[3], store_out)
     lax.fori_loop(0, plan.slots // 128, ungap, 0)
-
-    for h in HV:
-        flat[h, 0:GAP] = jnp.zeros((GAP, LANES), F32)
-        flat[h, GAP + plan.slots:] = jnp.zeros((flat.shape[1] - GAP - plan.slots, LANES), F32)
-
-    def place(i, c):
-        rows = pl.ds(pl.multiple_of(i * 128, 128), 128)
+    backward_block(1)
+
+    def sum_back(t0, c):
         for h in HV:
-            flat[h, pl.ds(pl.multiple_of(i * 128 + GAP, 16), 128)] = cot[rows, h * LANES:(h + 1) * LANES]
+            gz[h, pl.ds(t0, R)] = conv_back_block(t0, h, PER, regular_taps(1)) + k.skip[h, pl.ds(t0, R)]
         return c
-    lax.fori_loop(0, plan.slots // 128, place, 0)
-
-    def load_cot(t0, h):
-        parts = []
-        for j in range(RF):
-            a = flat[h, pl.ds(t0 + j + GAP, 8, stride=Q)]
-            b = flat[h, pl.ds(t0 + j, 8, stride=Q)]
-            parts.append(jnp.where(first_mask[t0 + j] > 0.5, a, b))
-        return jnp.stack(parts, axis=0)
-
-    tail_back(1, kept_second, load_cot)
-    backward_block(1)
-
-    def store_gz(t0, h, values):
-        gz[h, pl.ds(t0, R)] = values
-    pointwise_back(PER + SUB, gqb, store_gz)
-
-    def middle(t0, c):
-        for h in HV:
-            gz[h, pl.ds(t0, R)] = gz[h, pl.ds(t0, R)] + conv_back_block(t0, h, PER, regular_taps(1))
-        return c
-    steps_loop(R, middle)
-    tail_back(0, kept_first, lambda t0, h: gz[h, pl.ds(t0, RF)])
+    steps_loop(R, sum_back)
+    found = tail_back(0, kept_first, lambda t0, h: gz[h, pl.ds(t0, RF)] * pre[0, h, pl.ds(t0, RF)])
+    tail_back_aside(0, kept_first, found)
+    slopes(SUB - 2)
     backward_aside(1, 0)
     kernel_back(PER, [(hid_of(1, 0), regular_taps(1))])
     backward_block(0)
@@ -825,15 +945,14 @@
     backward_aside(0, 0)
     kernel_back(0, pieces)
     if plan.fused:
+        scatter_send(1, 0)
         values_start()
-        scatter_send(1, 0)
         scatter_send(0, 1)
-    pointwise_back(SUB, gqb, store_gz)
 
     def spread(t0, c):
         v = valid[pl.ds(t0, R)]
         for h in HV:
-            even = (conv_back_block(t0, h, 0, pieces[0][1]) + gz[h, pl.ds(t0, R)]) * v
+            even = (conv_back_block(t0, h, 0, pieces[0][1]) + k.skip[h, pl.ds(t0, R)]) * v
             odd = conv_back_block(t0, h, 0, pieces[1][1]) * v
             for j in range(R):
                 wide[h, pl.ds(2 * (t0 + j), 8, stride=2 * Q)] = even[j]
@@ -883,7 +1002,7 @@
         "frames_grad": shape(2 * plan.slots, channels),
     }
     params = {
-        "dw": shape(layers, halves, plan.tap_rows, LANES),
+        "dw": shape(layers, halves, plan.dw_rows, LANES),
         "point": shape(layers, channels, channels, dtype=BF16),
         "gains": shape(layers, halves, LANES),
         "shifts": shape(layers, halves, LANES),
@@ -907,11 +1026,12 @@
         "gpb": shape(plan.rows, channels, dtype=BF16),
         "gqb": shape(plan.rows, channels, dtype=BF16),
         "pre": shape(2, halves, Q, 8, LANES),
-        "flat": shape(halves, plan.slots + 2 * GAP, LANES),
         "wide": shape(halves, 2 * plan.slots + 4 * GAP, LANES),
         "first_mask": shape(Q, 8, LANES),
-        "second_mask": shape(Q, 8, LANES),
         "valid": shape(Q, 8, LANES),
+        "slope": shape(halves, Q, 8, LANES),
+        "skip": shape(halves, Q, 8, LANES),
+        "psum": shape(2, 8, channels),
         "stats": shape(layers, 8, LANES),
         "send4": shape(slots, 4, LANES),
         "recv4": shape(layers, devices, 4, LANES),
@@ -922,17 +1042,19 @@
     if plan.fused:
         units, chips = 1 + plan.per, devices // 2
         outs.update({
-            "dw_first_out": shape(plan.sub, plan.taps[0], shard),
-            "dw_second_out": shape(plan.sub, plan.taps[1], shard),
+            "dw_first_out": shape(plan.sub, shard, plan.taps[0]),
+            "dw_second_out": shape(plan.sub, shard, plan.taps[1]),
             "point_out": shape(2, plan.per, shard, channels),
-            "gains_out": shape(2, plan.per, shard),
-            "shifts_out": shape(2, plan.per, shard),
+            "gains_out": shape(plan.per, 2, shard),
+            "shifts_out": shape(plan.per, 2, shard),
             "squeeze_out": shape(2, shard, hidden),
-            "expand_out": shape(2, hidden, shard),
+            "expand_out": shape(2, shard, hidden),
         })
         scratch.update(params)
         scratch.update(grads)
         scratch.update({
+            "tile": shape(8, LANES),
+            "point_t": shape(layers, channels, channels, dtype=BF16),
             "packed": shape(vals, LANES),
             "packed_t": shape(16, vals),
             "unpacked": shape(vals, LANES),
@@ -946,6 +1068,7 @@
         sems["unit_sems"] = (8, units)
     else:
         outs.update(grads)
+        scratch["dw"] = params["dw"]
     vmem = pl.BlockSpec(memory_space=pltpu.VMEM)
     names = list(inputs) + list(outs) + list(scratch) + list(sems)
     results = pl.pallas_call(
@@ -956,7 +1079,7 @@
         scratch_shapes=[pltpu.VMEM(v.shape, v.dtype) for v in scratch.values()]
         + [pltpu.SemaphoreType.DMA(v) for v in sems.values()],
         compiler_params=pltpu.CompilerParams(
-            collective_id=0, has_side_effects=True, vmem_limit_bytes=62 * 1024 * 1024),
+            collective_id=0, has_side_effects=True, vmem_limit_bytes=63 * 1024 * 1024),
     )(*inputs.values())
     return dict(zip(outs, results, strict=True))
 
@@ -969,11 +1092,14 @@
     plan = Plan(cotangent.shape[0], channels, taps_first, taps_second, sub, hidden, devices)
     if plan.fused:
         res = call_kernel(plan, {
-            "lens": lengths, "frames": frames, "cot": cotangent, "dw_first": dw_first, "dw_second": dw_second,
-            "point_in": point, "gains_in": gains, "shifts_in": shifts, "se_down": se_down, "se_up": se_up})
-        return tuple(res[name] for name in (
-            "out", "frames_grad", "dw_first_out", "dw_second_out", "point_out", "gains_out", "shifts_out",
-            "squeeze_out", "expand_out"))
+            "lens": lengths, "frames": frames, "cot": cotangent,
+            "dw_first": jnp.swapaxes(dw_first, 1, 2), "dw_second": jnp.swapaxes(dw_second, 1, 2),
+            "point_in": point, "gains_in": jnp.swapaxes(gains, 0, 1), "shifts_in": jnp.swapaxes(shifts, 0, 1),
+            "se_down": se_down, "se_up": jnp.swapaxes(se_up, 1, 2)})
+        return (
+            res["out"], res["frames_grad"], jnp.swapaxes(res["dw_first_out"], 1, 2),
+            jnp.swapaxes(res["dw_second_out"], 1, 2), res["point_out"], jnp.swapaxes(res["gains_out"], 0, 1),
+            jnp.swapaxes(res["shifts_out"], 0, 1), res["squeeze_out"], jnp.swapaxes(res["expand_out"], 1, 2))
 
     per, layers, halves = plan.per, plan.layers, plan.halves
 
@@ -989,10 +1115,10 @@
 
     def dw_layout(v, taps):
         v = v.reshape(sub, taps, halves, LANES).transpose(0, 2, 1, 3)
-        return jnp.pad(v, ((0, 1), (0, 0), (0, plan.tap_rows - taps), (0, 0)))
+        return jnp.pad(v, ((0, 1), (0, 0), (0, plan.dw_rows - taps), (0, 0)))
     res = call_kernel(plan, {
         "lens": lengths, "frames": frames, "cot": cotangent,
-        "dw": jnp.concatenate([dw_layout(part[0], taps_first), dw_layout(part[1], taps_second)], axis=0),
+        "dw_in": jnp.concatenate([dw_layout(part[0], taps_first), dw_layout(part[1], taps_second)], axis=0),
         "point": gather(point, 2).reshape(layers, channels, channels),
         "gains": part[2].reshape(layers, halves, LANES),
         "shifts": part[3].reshape(layers, halves, LANES),

time: 230 us -> 184 us (0.80)
  Pallas kernels: 210 us -> 175 us
  local copies, waits for them, and re-layouts: 19 us -> 8 us
    pallas_call x1, Pallas kernels: 210 us -> 175 us  [call_kernel(): pl.pallas_call(functools.partial(kernel, plan, names), out_shape=list(out...]
    pallas_call x5 -> x0, local copies, waits for them, and re-layouts: 7.33 us -> none  [call_kernel(): pl.pallas_call(functools.partial(kernel, plan, names), out_shape=list(out...]
    unnamed x15 -> x25, local copies, waits for them, and re-layouts: 11.6 us -> 8 us
where the time goes in v3:
time: 184 us
  Pallas kernels  175 us (95%)
  local copies, waits for them, and re-layouts  8 us (4%)
    pallas_call x1, Pallas kernels, call_kernel(): pl.pallas_call(functools.partial(kernel, plan, names), out_shape=list(out...  175 us
    unnamed x25, local copies, waits for them, and re-layouts  8 us

profile of v3, /device:TPU:0, one launch (start us, length us, event | category | flops | bytes accessed | tf_op | source)
XLA Modules:
  0.0 183.9 jit_solution(10888309163435982300)
XLA Ops:
  0.6 175.2 %shard_map.169 = (f32[1024,256]{1,0:T(8,128)}, f32[2048,256]{1,0:T(8,128)}, f32[5,8,25]{2,1,0:T(8,128)}, f32[5,8,27]{2,1,0:T(8,128)}, f32[2,6,8,256]{3,2,1,0:T(8...) custom-call(s32[2]{0:T(128)} %refs_0_.1, ...), custom_call_target="tpu_custom_call" | custom-call | tf_op jit(solution)/shard_map/pallas_call | solution.py:1074
  175.9 0.0 copy-start
  175.9 2.4 %copy.28 = f32[1024,256]{1,0:T(8,128)} copy(f32[1024,256]{1,0:T(8,128)} %get-tuple-element.36) | data formatting | bytes 2097152
  178.3 0.0 copy-done
  178.3 0.0 copy-start.3
  178.3 0.0 copy-start.2
  178.3 0.0 copy-start.1
  178.3 0.0 copy-start.7
  178.3 0.0 copy-start.6
  178.3 0.0 copy-start.5
  178.3 0.0 copy-start.4
  178.4 1.3 copy.29
  179.7 0.0 copy-done.3
  179.7 0.6 copy.30
  180.3 0.0 copy-done.2
  180.3 0.6 copy.31
  180.9 0.0 copy-done.1
  180.9 0.6 copy.32
  181.5 0.0 copy-done.7
  181.5 0.6 copy.33
  182.1 0.0 copy-done.6
  182.1 0.6 copy.34
  182.7 0.0 copy-done.5
  182.7 0.6 copy.35
  183.3 0.0 copy-done.4
  183.3 0.6 copy.36
Async XLA Ops:
  175.9 2.4 %copy-start = (f32[2048,256]{1,0:T(8,128)S(1)}, f32[2048,256]{1,0:T(8,128)}, u32[]{:S(2)}) copy-start(f32[2048,256]{1,0:T(8,128)} %get-tuple-element.37) | copy-start | bytes 6291460
  178.3 1.4 copy-start.3
  178.3 2.0 %copy-start.2 = (f32[5,8,27]{2,1,0:T(8,128)S(1)}, f32[5,8,27]{2,1,0:T(8,128)}, u32[]{:S(2)}) copy-start(f32[5,8,27]{2,1,0:T(8,128)} %get-tuple-element.21) | copy-start | bytes 12964
  178.3 2.6 %copy-start.1 = (f32[2,6,8,256]{3,2,1,0:T(8,128)S(1)}, f32[2,6,8,256]{3,2,1,0:T(8,128)}, u32[]{:S(2)}) copy-start(f32[2,6,8,256]{3,2,1,0:T(8,128)} %get-tuple-element.40) | copy-start | bytes 294916
  178.3 3.2 %copy-start.7 = (f32[6,2,8]{2,1,0:T(2,128)S(1)}, f32[6,2,8]{2,1,0:T(2,128)}, u32[]{:S(2)}) copy-start(f32[6,2,8]{2,1,0:T(2,128)} %get-tuple-element.23) | copy-start | bytes 1156
  178.3 3.8 %copy-start.6 = (f32[6,2,8]{2,1,0:T(2,128)S(1)}, f32[6,2,8]{2,1,0:T(2,128)}, u32[]{:S(2)}) copy-start(f32[6,2,8]{2,1,0:T(2,128)} %get-tuple-element.24) | copy-start | bytes 1156
  178.3 4.4 %copy-start.5 = (f32[2,8,32]{2,1,0:T(8,128)S(1)}, f32[2,8,32]{2,1,0:T(8,128)}, u32[]{:S(2)}) copy-start(f32[2,8,32]{2,1,0:T(8,128)} %get-tuple-element.43) | copy-start | bytes 6148
  178.3 5.0 %copy-start.4 = (f32[2,8,32]{2,1,0:T(8,128)S(1)}, f32[2,8,32]{2,1,0:T(8,128)}, u32[]{:S(2)}) copy-start(f32[2,8,32]{2,1,0:T(8,128)} %get-tuple-element.26) | copy-start | bytes 6148

commit v4 on v3

--- a/solution.py
+++ b/solution.py
@@ -44,13 +44,16 @@
         self.dw_rows = 96
         self.values = 2 * LANES
         self.shard = channels // devices
-        self.fused = self.shard == 8 and devices % 2 == 0 and sub_blocks == 5 and hidden == 32 and self.max_taps <= 32
+        self.fused = self.shard == 8 and devices == 32 and sub_blocks == 5 and hidden == 32 and self.max_taps <= 32
 
     def tap_row(self, r):
         return r * self.tap_rows + self.tap_rows * (r // 4)
 
 
 SQUEEZE_ROW, EXPAND_ROW, GAIN_ROW, SHIFT_ROW = 128, 192, 224, 232
+
+
+PARAMS = ("dw_first", "dw_second", "point_in", "gains_in", "shifts_in", "se_down", "se_up")
 
 
 class Refs:
@@ -103,9 +106,8 @@
 
 def kernel(plan, names, *refs):
     k = Refs(names, refs)
-    lens, frames, cot, dw, point, gains, shifts = k.lens, k.frames, k.cot, k.dw, k.point, k.gains, k.shifts
+    lens, dw, point, gains, shifts = k.lens, k.dw, k.point, k.gains, k.shifts
     squeeze_t, expand = k.squeeze_t, k.expand
-    out, frames_grad = k.out, k.frames_grad
     hid, acts, prods, gd, gz, gpb, gqb, pre = k.hid, k.acts, k.prods, k.gd, k.gz, k.gpb, k.gqb, k.pre
     wide, first_mask, valid, stats = k.wide, k.first_mask, k.valid, k.stats
     flat = wide.at[:, pl.ds(0, plan.slots + 2 * GAP)]
@@ -121,12 +123,30 @@
     chips = N // 2
     chip, core = me // 2, lax.rem(me, 2)
     partner = me + 1 - 2 * core
+    depth, plane = me // 8, lax.rem(me // 2, 4)
+
+    def at_depth(d):
+        return lax.rem(depth + d, 4) * 8 + 2 * plane + core
+
+    def in_plane(d):
+        return depth * 8 + 2 * lax.rem(plane + d, 4) + core
+
     same_core = same_core_peers(me, N)
 
     barrier = pltpu.get_barrier_semaphore()
     for peer in peers:
         pl.semaphore_signal(barrier, inc=1, device_id=(peer,), device_id_type=MESH)
 
+    load_frames = pltpu.make_async_copy(k.frames, k.frames_v, k.io_sems.at[0])
+    load_params = []
+    if plan.fused:
+        for i, name in enumerate(PARAMS):
+            load_params.append(pltpu.make_async_copy(getattr(k, name), getattr(k, name + "_v"), k.param_sems.at[i]))
+            load_params[-1].start()
+    load_cot = pltpu.make_async_copy(k.cot, k.cot_v, k.io_sems.at[1])
+    save_out = pltpu.make_async_copy(k.cot_v, k.out, k.io_sems.at[2])
+    load_frames.start()
+    load_cot.start()
     len0 = lens[0]
     len1 = lens[1]
     half0 = len0 // 2
@@ -151,10 +171,12 @@
         wide[h, 0:2 * GAP] = jnp.zeros((2 * GAP, LANES), F32)
         wide[h, top:] = jnp.zeros((wide.shape[1] - top, LANES), F32)
 
+    load_frames.wait()
+
     def widen(i, c):
         rows = pl.ds(pl.multiple_of(i * 128, 128), 128)
         for h in HV:
-            values = frames[rows, h * LANES:(h + 1) * LANES].astype(F32)
+            values = k.frames_v[rows, h * LANES:(h + 1) * LANES].astype(F32)
             wide[h, pl.ds(pl.multiple_of(i * 128 + 2 * GAP, 32), 128)] = values
         return c
 
@@ -188,43 +210,60 @@
 
     def load_shard():
         for b in range(2):
-            source = (k.dw_first, k.dw_second)[b]
+            source = (k.dw_first_v, k.dw_second_v)[b]
             tiles = [jnp.zeros((8, LANES), F32) for _ in range(2)]
             for r in range(SUB):
                 tile, lane = divmod(plan.tap_row(r), LANES)
                 tiles[tile] = tiles[tile] + spread_lanes(source[r].astype(F32), lane)
-            tiles[1] = tiles[1] + spread_lanes(k.se_up[b].astype(F32), EXPAND_ROW - LANES)
-            tiles[1] = tiles[1] + spread_lanes(k.se_down[b].astype(F32), SQUEEZE_ROW - LANES)
+            tiles[1] = tiles[1] + spread_lanes(k.se_up_v[b].astype(F32), EXPAND_ROW - LANES)
+            tiles[1] = tiles[1] + spread_lanes(k.se_down_v[b].astype(F32), SQUEEZE_ROW - LANES)
             k.packed[0:LANES] = jnp.zeros((LANES, LANES), F32)
             for r in range(PER):
-                k.packed[GAIN_ROW - LANES + r:GAIN_ROW - LANES + r + 1, 0:8] = k.gains_in[r, b:b + 1].astype(F32)
-                k.packed[SHIFT_ROW - LANES + r:SHIFT_ROW - LANES + r + 1, 0:8] = k.shifts_in[r, b:b + 1].astype(F32)
+                k.packed[GAIN_ROW - LANES + r:GAIN_ROW - LANES + r + 1, 0:8] = k.gains_in_v[r, b:b + 1].astype(F32)
+                k.packed[SHIFT_ROW - LANES + r:SHIFT_ROW - LANES + r + 1, 0:8] = k.shifts_in_v[r, b:b + 1].astype(F32)
             tiles[1] = tiles[1] + jnp.transpose(k.packed[0:LANES])[0:8]
             for tile in range(2):
                 k.packed_t[8 * b:8 * b + 8, tile * LANES:(tile + 1) * LANES] = tiles[tile]
-        k.gath[0, chip, core] = k.packed_t[...].astype(BF16)
+            if b == 0:
+                lane = lax.broadcasted_iota(jnp.int32, (8, LANES), 1)
+                k.first[me] = jnp.where(lane == plan.tap_rows - 1, count, tiles[0])
+        k.gath[0, depth, plane, core] = k.packed_t[...].astype(BF16)
         for pair in range(PER):
-            rows = [k.point_in[i // PER, i % PER].astype(F32) for i in (2 * pair, 2 * pair + 1)]
-            k.gath[1 + pair, chip, core] = jnp.concatenate(rows, axis=0).astype(BF16)
+            rows = [k.point_in_v[i // PER, i % PER].astype(F32) for i in (2 * pair, 2 * pair + 1)]
+            k.gath[1 + pair, depth, plane, core] = jnp.concatenate(rows, axis=0).astype(BF16)
+
+    def remote(src, dst, sems, unit, to):
+        pltpu.make_async_remote_copy(src_ref=src, dst_ref=dst, send_sem=k.unit_sems.at[sems, unit],
+                                     recv_sem=k.unit_sems.at[sems + 1, unit], device_id=(to,),
+                                     device_id_type=MESH).start()
+
+    def blocks_wait(count, sem, unit):
+        view = k.gained.at[0, pl.ds(0, count)]
+        pltpu.make_async_copy(view, view, k.unit_sems.at[sem, unit]).wait()
 
     def gather_send(unit):
-        view = k.gath.at[unit, chip, core]
+        view = k.gath.at[unit, depth, plane, core]
         for peer in same_core:
-            pltpu.make_async_remote_copy(src_ref=view, dst_ref=view, send_sem=k.unit_sems.at[0, unit],
-                                         recv_sem=k.unit_sems.at[1, unit], device_id=(peer,),
-                                         device_id_type=MESH).start()
-
-    def gather_forward(unit):
-        view = k.gath.at[unit, pl.ds(0, chips - 1), 0]
-        pltpu.make_async_copy(view, view, k.unit_sems.at[1, unit]).wait()
-        view = k.gath.at[unit, :, core]
-        pltpu.make_async_remote_copy(src_ref=view, dst_ref=view, send_sem=k.unit_sems.at[2, unit],
-                                     recv_sem=k.unit_sems.at[3, unit], device_id=(partner,),
-                                     device_id_type=MESH).start()
+            remote(view, view, 0, unit, peer)
+
+    def gather_z(unit):
+        view = k.gath.at[unit, depth, plane, core]
+        for d in (2, 1, 3):
+            remote(view, view, 0, unit, at_depth(d))
+
+    def gather_plane(unit):
+        blocks_wait(3, 1, unit)
+        view = k.gath.at[unit, :, plane, core]
+        for d in (3, 2, 1):
+            remote(view, view, 2, unit, in_plane(d))
+
+    def gather_core(unit, straight):
+        blocks_wait(chips - 1 if straight else 12, 1 if straight else 3, unit)
+        view = k.gath.at[unit, :, :, core]
+        remote(view, view, 4, unit, partner)
 
     def gather_wait(unit):
-        view = k.gath.at[unit, :, 0]
-        pltpu.make_async_copy(view, view, k.unit_sems.at[3, unit]).wait()
+        blocks_wait(chips, 5, unit)
 
     def split_taps(b, r, h):
         taps = plan.taps[b]
@@ -239,6 +278,14 @@
         dw[b * PER + r, h, row3:row3 + low] = jnp.concatenate(
             [back[2 * j + 1] - back[2 * j] for j in range(low)], axis=0)
 
+    def unpack_first():
+        got = k.first[...]
+        counts[...] = jnp.broadcast_to(got[:, 0:4, plan.tap_rows - 1:plan.tap_rows], counts.shape)
+        block = got.reshape(plan.channels, LANES)
+        for h in HV:
+            k.unpacked[0:LANES] = jnp.transpose(block[h * LANES:(h + 1) * LANES])
+            dw[0, h, 0:plan.tap_rows] = k.unpacked[0:plan.tap_rows]
+
     def unpack_values():
         got = k.gath[0].astype(F32).reshape(N, 16, plan.values)
         for b in range(2):
@@ -265,9 +312,12 @@
             k.point_t[2 * pair + side] = jnp.transpose(block).astype(BF16)
 
     if plan.fused:
+        for copy in load_params:
+            copy.wait()
         load_shard()
 
-    csend[...] = jnp.full((4, LANES), count, F32)
+    if not plan.fused:
+        csend[...] = jnp.full((4, LANES), count, F32)
     pl.semaphore_wait(barrier, N - 1)
 
     def send_to_all(src, dst, ssem, rsem):
@@ -280,12 +330,13 @@
         pltpu.make_async_copy(view, view, sem).wait()
 
     if plan.fused:
+        send_to_all(k.first.at[me], k.first.at[me], count_sems.at[0], count_sems.at[1])
+        gather_send(1)
         gather_send(0)
-        gather_send(1)
-    send_to_all(csend, counts.at[me], count_sems.at[0], count_sems.at[1])
-    if plan.fused:
-        gather_send(2)
-    counts[me] = csend[...]
+        gather_z(2)
+    else:
+        send_to_all(csend, counts.at[me], count_sems.at[0], count_sems.at[1])
+        counts[me] = csend[...]
 
     def exchange(slot, place, rows):
         send4[slot] = rows
@@ -353,7 +404,7 @@
         second = run(late, high, lambda j: row1 + (high - 1 - j if back else j)) - shared
         return jnp.stack([first, second], axis=1).reshape(R, 8, LANES)
 
-    def layer_conv(index, pieces):
+    def layer_conv(index, pieces, between=None):
         def body(t0, c):
             for h in HV:
                 acc = None
@@ -369,7 +420,13 @@
                 rows = pl.ds(pl.multiple_of(8 * t0, 16), 8 * R)
                 acts[index, rows, h * LANES:(h + 1) * LANES] = acc.reshape(8 * R, LANES).astype(BF16)
             return c
-        steps_loop(R, body)
+        if between is None:
+            steps_loop(R, body)
+        else:
+            cut = Q // R - 2
+            lax.fori_loop(0, cut, lambda i, c: body(i * R, c), 0)
+            between()
+            lax.fori_loop(cut, Q // R, lambda i, c: body(i * R, c), 0)
 
     def half_lanes(values, h):
         return values[:, h * LANES:(h + 1) * LANES]
@@ -528,18 +585,17 @@
         if plan.fused:
             step = b * SUB + r
 
+            @pl.when(step == 0)
+            def _():
+                gather_core(0, True)
+                gather_wait(0)
+                unpack_values()
+
             @pl.when(jnp.logical_and(step >= 1, step < PER))
             def _():
+                gather_core(1 + step, False)
                 gather_wait(1 + step)
                 unpack_pair(step)
-
-            @pl.when(step < PER - 1)
-            def _():
-                gather_forward(2 + step)
-
-            @pl.when(step < PER - 2)
-            def _():
-                gather_send(3 + step)
 
         @pl.when(r == SUB - 2)
         def _():
@@ -554,12 +610,23 @@
     def forward_block(b, extras=()):
         def layer(r, pieces, before=None):
             index = b * PER + r
-            layer_conv(index, pieces)
-            if before is not None:
+            first = before is not None
+            layer_conv(index, pieces, (lambda: gather_core(1, True)) if first else None)
+            if first:
                 before()
             exchange(index, index, pointwise(index))
             forward_aside(b, r, extras)
             merge_stats(index, index)
+            if plan.fused:
+                step = b * SUB + r
+
+                @pl.when(step < PER - 2)
+                def _():
+                    gather_z(3 + step)
+
+                @pl.when(step < PER - 1)
+                def _():
+                    gather_plane(2 + step)
 
         def first_matrices():
             gather_wait(1)
@@ -646,8 +713,10 @@
         k.expand_grad[b] = small(eight(excited), eight(grad_up), ((0,), (0,)))
         k.squeeze_grad[b] = small(eight(grad_inner), eight(means), ((0,), (0,)))
 
-    def norm_back(index, load, target, store):
+    def norm_back(index, load, target, store, then=None):
         sums = jnp.sum(received(back_slot + index, back_place(index)), axis=0)
+        if then is not None:
+            then()
         k.shifts_grad[index] = sums[0:2]
         k.gains_grad[index] = sums[2:4]
         total = jnp.sum(counts[...], axis=0)[0:2]
@@ -736,37 +805,74 @@
         return gz[h, t0:t0 + R]
 
     def scatter_start(unit, place):
-        pltpu.make_async_remote_copy(src_ref=k.shares.at[place, :, 1 - core], dst_ref=k.inbox.at[unit],
-                                     send_sem=k.unit_sems.at[4, unit], recv_sem=k.unit_sems.at[5, unit],
-                                     device_id=(partner,), device_id_type=MESH).start()
-
-    def scatter_send(unit, place):
-        view = k.inbox.at[unit]
-        pltpu.make_async_copy(view, view, k.unit_sems.at[5, unit]).wait()
-        pltpu.make_async_copy(view, view, k.unit_sems.at[4, unit]).wait()
-        k.sums[unit] = (k.shares[place, :, core].astype(F32) + k.inbox[unit].astype(F32)).astype(BF16)
-        k.gained[unit, chip] = k.sums[unit, chip]
+        remote(k.shares.at[place, :, :, 1 - core], k.inbox.at[unit], 6, unit, partner)
+
+    def scatter_sum(unit, place):
+        blocks_wait(chips, 7, unit)
+        blocks_wait(chips, 6, unit)
+        slot = lax.rem(unit, 3)
+        k.sums[slot] = (k.shares[place, :, :, core].astype(F32) + k.inbox[unit].astype(F32)).astype(BF16)
+
+    def scatter_send(unit):
+        slot = lax.rem(unit, 3)
+        k.gained[unit, chip] = k.sums[slot, depth, plane]
         for peer in same_core:
-            pltpu.make_async_remote_copy(src_ref=k.sums.at[unit, peer // 2], dst_ref=k.gained.at[unit, chip],
-                                         send_sem=k.unit_sems.at[6, unit], recv_sem=k.unit_sems.at[7, unit],
-                                         device_id=(peer,), device_id_type=MESH).start()
+            remote(k.sums.at[slot, peer // 8, lax.rem(peer // 2, 4)], k.gained.at[unit, chip], 8, unit, peer)
 
     def scatter_finish(unit):
-        view = k.gained.at[unit, pl.ds(0, chips - 1)]
-        pltpu.make_async_copy(view, view, k.unit_sems.at[7, unit]).wait()
+        blocks_wait(chips - 1, 9, unit)
         return jnp.sum(k.gained[unit].astype(F32), axis=0)
+
+    def scatter_plane(unit):
+        slot = lax.rem(unit, 3)
+        k.by_plane[unit, plane] = k.sums[slot, :, plane]
+        for d in (3, 2, 1):
+            there = lax.rem(plane + d, 4)
+            remote(k.sums.at[slot, :, there], k.by_plane.at[unit, plane], 8, unit, in_plane(d))
+
+    def scatter_mid(unit):
+        blocks_wait(12, 9, unit)
+        blocks_wait(12, 8, unit)
+        k.line[unit] = jnp.sum(k.by_plane[unit].astype(F32), axis=0).astype(BF16)
+        k.by_depth[unit, depth] = k.line[unit, depth]
+
+    def scatter_z(unit):
+        for d in (2, 1, 3):
+            there = lax.rem(depth + d, 4)
+            remote(k.line.at[unit, there], k.by_depth.at[unit, depth], 10, unit, at_depth(d))
+
+    def scatter_end(unit):
+        blocks_wait(3, 11, unit)
+        return jnp.sum(k.by_depth[unit].astype(F32), axis=0)
 
     def pair_start(pair):
         both = [k.point_grad[side].reshape(N, 8, plan.channels) for side in range(2)]
-        k.shares[0] = jnp.concatenate(both, axis=1).astype(BF16).reshape(chips, 2, 16, plan.channels)
+        k.shares[0] = jnp.concatenate(both, axis=1).astype(BF16).reshape(4, 4, 2, 16, plan.channels)
         scatter_start(1 + pair, 0)
 
-    def pair_finish(pair):
-        total = scatter_finish(1 + pair)
+    def pair_finish(pair, straight=False):
+        total = scatter_finish(1 + pair) if straight else scatter_end(1 + pair)
         b = pair // (PER // 2)
         r = 2 * lax.rem(pair, PER // 2)
         k.point_out[b, r] = total[0:8]
         k.point_out[b, r + 1] = total[8:16]
+
+    def last_start():
+        k.packed[0:LANES] = jnp.zeros((LANES, LANES), F32)
+        columns = []
+        for h in HV:
+            k.packed[0:plan.tap_rows] = k.dw_grad[0, h]
+            columns.append(jnp.transpose(k.packed[0:LANES]))
+        k.last_mine[...] = jnp.concatenate(columns, axis=0).reshape(N, 8, LANES)
+        k.last[me] = k.last_mine[me]
+        for peer in peers:
+            pltpu.make_async_remote_copy(src_ref=k.last_mine.at[peer], dst_ref=k.last.at[me],
+                                         send_sem=k.last_sems.at[0], recv_sem=k.last_sems.at[1],
+                                         device_id=(peer,), device_id_type=MESH).start()
+
+    def last_finish():
+        wait_all(k.last, k.last_sems.at[1])
+        k.dw_first_out[0] = jnp.sum(k.last[...], axis=0)[:, 0:plan.taps[0]]
 
     def values_start():
         k.packed[...] = jnp.zeros((plan.values, LANES), F32)
@@ -774,25 +880,19 @@
         for b in range(2):
             columns = []
             for h in HV:
-                for r in range(SUB):
+                for r in range(1 - b, SUB):
                     k.packed[plan.tap_row(r):plan.tap_row(r) + plan.tap_rows] = k.dw_grad[b * PER + r, h]
                 lanes = slice(h * LANES, (h + 1) * LANES)
                 k.packed[EXPAND_ROW:EXPAND_ROW + plan.hidden] = k.expand_grad[b, :, lanes]
                 k.packed[SQUEEZE_ROW:SQUEEZE_ROW + plan.hidden] = k.squeeze_grad[b, :, lanes]
-                for r in range(PER):
-                    k.packed[GAIN_ROW + r:GAIN_ROW + r + 1] = k.gains_grad[b * PER + r, h:h + 1]
-                    k.packed[SHIFT_ROW + r:SHIFT_ROW + r + 1] = k.shifts_grad[b * PER + r, h:h + 1]
                 columns.append(jnp.concatenate(
                     [jnp.transpose(k.packed[t * LANES:(t + 1) * LANES]) for t in range(2)], axis=1))
-            whole = jnp.concatenate(columns, axis=0)
-            k.own_norm[b] = whole[:, LANES:]
-            blocks.append(whole.reshape(N, 8, plan.values))
-        k.shares[1] = jnp.concatenate(blocks, axis=1).astype(BF16).reshape(chips, 2, 16, plan.values)
+            blocks.append(jnp.concatenate(columns, axis=0).reshape(N, 8, plan.values))
+        k.shares[1] = jnp.concatenate(blocks, axis=1).astype(BF16).reshape(4, 4, 2, 16, plan.values)
         scatter_start(0, 1)
 
     def values_finish():
         total = scatter_finish(0)
-        mine = pl.ds(pl.multiple_of(me * 8, 8), 8)
         for b in range(2):
             rows = total[8 * b:8 * b + 8]
 
@@ -801,15 +901,26 @@
                 part = rows[:, tile * LANES:(tile + 1) * LANES]
                 return (pltpu.roll(part, LANES - lane, 1) if lane else part)[:, 0:size]
             dw_out = (k.dw_first_out, k.dw_second_out)[b]
-            for r in range(SUB):
+            for r in range(1 - b, SUB):
                 dw_out[r] = lanes(plan.tap_row(r), plan.taps[b])
             k.squeeze_out[b] = lanes(SQUEEZE_ROW, plan.hidden)
             k.expand_out[b] = lanes(EXPAND_ROW, plan.hidden)
-            k.packed[0:LANES] = jnp.transpose(
-                jnp.concatenate([k.own_norm[b, mine], jnp.zeros((LANES - 8, LANES), F32)], axis=0))
+
+    def own_norms():
+        mine = pl.ds(pl.multiple_of(me * 8, 8), 8)
+        k.packed[0:LANES] = jnp.zeros((LANES, LANES), F32)
+        for h in HV:
+            for b in range(2):
+                for r in range(PER):
+                    k.packed[16 * b + r:16 * b + r + 1] = k.gains_grad[b * PER + r, h:h + 1]
+                    k.packed[16 * b + 8 + r:16 * b + 9 + r] = k.shifts_grad[b * PER + r, h:h + 1]
+            k.own_norm[h * LANES:(h + 1) * LANES] = jnp.transpose(k.packed[0:LANES])
+        k.packed[0:LANES] = jnp.transpose(
+            jnp.concatenate([k.own_norm[mine], jnp.zeros((LANES - 8, LANES), F32)], axis=0))
+        for b in range(2):
             for r in range(PER):
-                k.gains_out[r, b:b + 1] = k.packed[GAIN_ROW - LANES + r:GAIN_ROW - LANES + r + 1, 0:8]
-                k.shifts_out[r, b:b + 1] = k.packed[SHIFT_ROW - LANES + r:SHIFT_ROW - LANES + r + 1, 0:8]
+                k.gains_out[r, b:b + 1] = k.packed[16 * b + r:16 * b + r + 1, 0:8]
+                k.shifts_out[r, b:b + 1] = k.packed[16 * b + 8 + r:16 * b + 9 + r, 0:8]
 
     HALF = PER // 2
 
@@ -819,19 +930,11 @@
             if b == 0:
                 @pl.when(r == SUB - 1)
                 def _():
-                    scatter_send(1 + HALF, 0)
-
-                @pl.when(r == SUB - 2)
-                def _():
-                    pair_finish(HALF)
+                    scatter_sum(1 + HALF, 0)
 
             @pl.when(lax.rem(r, 2) == 1)
             def _():
-                scatter_send(1 + HALF * b + (r + 1) // 2, 0)
-
-            @pl.when(jnp.logical_and(lax.rem(r, 2) == 0, r < SUB - 1))
-            def _():
-                pair_finish(HALF * b + r // 2 + 1)
+                scatter_sum(1 + HALF * b + (r + 1) // 2, 0)
         point_back(index, gpb)
 
         @pl.when(r == SUB - 1)
@@ -844,16 +947,62 @@
             def _():
                 pair_start(HALF * b + r // 2)
 
+    def backward_late(b, r):
+        if not plan.fused:
+            return
+        if b == 0:
+            @pl.when(r == SUB - 1)
+            def _():
+                pair_finish(HALF + 1)
+
+            @pl.when(r == SUB - 2)
+            def _():
+                scatter_mid(1 + HALF)
+
+            @pl.when(r == SUB - 3)
+            def _():
+                pair_finish(HALF)
+
+        @pl.when(jnp.logical_or(r == 2, r == 0))
+        def _():
+            scatter_mid(1 + HALF * b + r // 2 + 1)
+
+        @pl.when(r == 1)
+        def _():
+            pair_finish(HALF * b + 2)
+
     def backward_block(b):
-        def filtered(index):
-            norm_back(index, load_gz, gpb, store_gd)
+        def go(r):
+            if plan.fused:
+                @pl.when(jnp.logical_or(r == 2, r == 0))
+                def _():
+                    scatter_plane(1 + HALF * b + r // 2 + 1)
+
+                @pl.when(r == 1)
+                def _():
+                    scatter_z(1 + HALF * b + 2)
+                if b == 0:
+                    @pl.when(r == SUB - 1)
+                    def _():
+                        scatter_z(1 + HALF + 1)
+
+                    @pl.when(r == SUB - 2)
+                    def _():
+                        scatter_plane(1 + HALF)
+
+                    @pl.when(r == SUB - 3)
+                    def _():
+                        scatter_z(1 + HALF)
+
+        def filtered(r):
+            norm_back(b * PER + r, load_gz, gpb, store_gd, lambda: go(r))
             for h in HV:
                 set_halo(gd, h)
 
         def step(j, c):
             r = SUB - 1 - j
             index = b * PER + r
-            filtered(index)
+            filtered(r)
             hidden_back(index, regular_taps(b))
             backward_aside(b, r)
             kernel_back(index, [(hid_of(b, r), regular_taps(b))])
@@ -861,22 +1010,23 @@
             @pl.when(r >= 2)
             def _():
                 slopes(index - 2)
+            backward_late(b, r)
             return c
         lax.fori_loop(0, SUB - 1, step, 0)
-        filtered(b * PER)
+        if plan.fused and b == 0:
+            values_start()
+        filtered(0)
 
     if plan.fused:
-        for unit in range(2):
-            gather_forward(unit)
-        gather_wait(0)
-        unpack_values()
+        wait_all(k.first, count_sems.at[1])
+        unpack_first()
     else:
+        wait_all(counts, count_sems.at[1])
         dw[...] = k.dw_in[...]
         for b in range(2):
             for r in range(SUB):
                 for h in HV:
                     split_taps(b, r, h)
-    wait_all(counts, count_sems.at[1])
     kept_first = forward_block(0)
 
     def store_middle(t0, h, values):
@@ -886,6 +1036,7 @@
         set_halo(hid.at[hid_of(1, 0)], h)
 
     def place_cot():
+        load_cot.wait()
         for h in HV:
             flat[h, 0:GAP] = jnp.zeros((GAP, LANES), F32)
             flat[h, GAP + plan.slots:] = jnp.zeros((flat.shape[1] - GAP - plan.slots, LANES), F32)
@@ -893,7 +1044,7 @@
         def place(i, c):
             rows = pl.ds(pl.multiple_of(i * 128, 128), 128)
             for h in HV:
-                flat[h, pl.ds(pl.multiple_of(i * 128 + GAP, 16), 128)] = cot[rows, h * LANES:(h + 1) * LANES]
+                flat[h, pl.ds(pl.multiple_of(i * 128 + GAP, 16), 128)] = k.cot_v[rows, h * LANES:(h + 1) * LANES]
             return c
         lax.fori_loop(0, plan.slots // 128, place, 0)
 
@@ -922,12 +1073,13 @@
         slot = i * 128 + lax.broadcasted_iota(jnp.int32, (128, LANES), 0)
         for h in HV:
             moved = flat[h, pl.ds(pl.multiple_of(i * 128 + GAP, 16), 128)]
-            out[rows, h * LANES:(h + 1) * LANES] = jnp.where(slot < half0, flat[h, rows], moved)
+            k.cot_v[rows, h * LANES:(h + 1) * LANES] = jnp.where(slot < half0, flat[h, rows], moved)
         return c
     tail_back_aside(1, kept_second, found)
     slopes(PER + SUB - 2)
     tail(1, kept_second[3], store_out)
     lax.fori_loop(0, plan.slots // 128, ungap, 0)
+    save_out.start()
     backward_block(1)
 
     def sum_back(t0, c):
@@ -940,14 +1092,21 @@
     slopes(SUB - 2)
     backward_aside(1, 0)
     kernel_back(PER, [(hid_of(1, 0), regular_taps(1))])
+    backward_late(1, 0)
     backward_block(0)
     pieces = block_pieces(0)
     backward_aside(0, 0)
+    if plan.fused:
+        scatter_sum(0, 1)
+        scatter_send(0)
     kernel_back(0, pieces)
     if plan.fused:
-        scatter_send(1, 0)
-        values_start()
-        scatter_send(0, 1)
+        last_start()
+        scatter_sum(1, 0)
+        scatter_send(1)
+        backward_late(0, 0)
+        scatter_z(2)
+        own_norms()
 
     def spread(t0, c):
         v = valid[pl.ds(t0, R)]
@@ -965,34 +1124,51 @@
         slot = i * 128 + lax.broadcasted_iota(jnp.int32, (128, LANES), 0)
         for h in HV:
             moved = wide[h, pl.ds(pl.multiple_of(i * 128 + 2 * GAP, 32), 128)]
-            frames_grad[rows, h * LANES:(h + 1) * LANES] = jnp.where(slot < len0, wide[h, rows], moved)
+            k.frames_grad_v[rows, h * LANES:(h + 1) * LANES] = jnp.where(slot < len0, wide[h, rows], moved)
         return c
-    lax.fori_loop(0, 2 * plan.slots // 128, ungap_wide, 0)
+    save_frames = []
+    pieces_out = 4
+    for piece in range(pieces_out):
+        size = 2 * plan.slots // pieces_out
+        lax.fori_loop(piece * size // 128, (piece + 1) * size // 128, ungap_wide, 0)
+        rows = pl.ds(piece * size, size)
+        save_frames.append(pltpu.make_async_copy(k.frames_grad_v.at[rows], k.frames_grad.at[rows],
+                                                 k.io_sems.at[3 + piece]))
+        save_frames[-1].start()
     if plan.fused:
-        pair_finish(0)
+        pair_finish(1)
         values_finish()
-
-    wait_all(counts, count_sems.at[0])
+        pair_finish(0, True)
+        last_finish()
+
+    save_out.wait()
+    for copy in save_frames:
+        copy.wait()
+    wait_all(k.first if plan.fused else counts, count_sems.at[0])
 
     def drain(slot, c):
         wait_all(recv4.at[0], send_sem.at[slot])
         return c
     lax.fori_loop(0, send4.shape[0], drain, 0)
     if plan.fused:
-        def drain_units(unit, c):
-            view = k.gath.at[0, pl.ds(0, chips - 1), 0]
-            pltpu.make_async_copy(view, view, k.unit_sems.at[0, unit]).wait()
-            view = k.gath.at[0, :, 0]
-            pltpu.make_async_copy(view, view, k.unit_sems.at[2, unit]).wait()
-            view = k.gained.at[0, pl.ds(0, chips - 1)]
-            pltpu.make_async_copy(view, view, k.unit_sems.at[6, unit]).wait()
-            return c
-        lax.fori_loop(0, 1 + PER, drain_units, 0)
+        for unit in range(1 + PER):
+            blocks_wait(chips - 1 if unit < 2 else 3, 0, unit)
+            if unit >= 2:
+                blocks_wait(12, 2, unit)
+                blocks_wait(3, 10, unit)
+            else:
+                blocks_wait(chips - 1, 8, unit)
+            blocks_wait(chips, 4, unit)
+        wait_all(k.last, k.last_sems.at[0])
 
 
 def call_kernel(plan, inputs):
     layers, halves, Q, channels = plan.layers, plan.halves, plan.steps, plan.channels
     vals, shard, hidden, devices = plan.values, plan.shard, plan.hidden, plan.devices
+    vmem = pl.BlockSpec(memory_space=pltpu.VMEM)
+    anywhere = pl.BlockSpec(memory_space=pl.ANY)
+    places = {"lens": pl.BlockSpec(memory_space=pltpu.SMEM), "frames": anywhere, "cot": anywhere,
+              "out": anywhere, "frames_grad": anywhere}
     slots = 2 * layers
 
     def shape(*dims, dtype=F32):
@@ -1027,6 +1203,9 @@
         "gqb": shape(plan.rows, channels, dtype=BF16),
         "pre": shape(2, halves, Q, 8, LANES),
         "wide": shape(halves, 2 * plan.slots + 4 * GAP, LANES),
+        "frames_v": shape(2 * plan.slots, channels, dtype=BF16),
+        "cot_v": shape(plan.slots, channels),
+        "frames_grad_v": shape(2 * plan.slots, channels),
         "first_mask": shape(Q, 8, LANES),
         "valid": shape(Q, 8, LANES),
         "slope": shape(halves, Q, 8, LANES),
@@ -1038,7 +1217,7 @@
         "counts": shape(devices, 4, LANES),
         "csend": shape(4, LANES),
     }
-    sems = {"send_sem": (slots,), "recv_sem": (slots,), "count_sems": (2,)}
+    sems = {"send_sem": (slots,), "recv_sem": (slots,), "count_sems": (2,), "io_sems": (7,)}
     if plan.fused:
         units, chips = 1 + plan.per, devices // 2
         outs.update({
@@ -1057,31 +1236,73 @@
             "point_t": shape(layers, channels, channels, dtype=BF16),
             "packed": shape(vals, LANES),
             "packed_t": shape(16, vals),
+            "first": shape(devices, 8, LANES),
+            "last_mine": shape(devices, 8, LANES),
+            "last": shape(devices, 8, LANES),
             "unpacked": shape(vals, LANES),
-            "gath": shape(units, chips, 2, 16, channels, dtype=BF16),
-            "shares": shape(2, chips, 2, 16, channels, dtype=BF16),
-            "inbox": shape(units, chips, 16, channels, dtype=BF16),
-            "sums": shape(units, chips, 16, channels, dtype=BF16),
-            "gained": shape(units, chips, 16, channels, dtype=BF16),
-            "own_norm": shape(2, channels, LANES),
+            "gath": shape(units, 4, 4, 2, 16, channels, dtype=BF16),
+            "shares": shape(2, 4, 4, 2, 16, channels, dtype=BF16),
+            "inbox": shape(units, 4, 4, 16, channels, dtype=BF16),
+            "sums": shape(3, 4, 4, 16, channels, dtype=BF16),
+            "gained": shape(2, chips, 16, channels, dtype=BF16),
+            "by_plane": shape(units, 4, 4, 16, channels, dtype=BF16),
+            "line": shape(units, 4, 16, channels, dtype=BF16),
+            "by_depth": shape(units, 4, 16, channels, dtype=BF16),
+            "own_norm": shape(channels, LANES),
         })
-        sems["unit_sems"] = (8, units)
+        sems["unit_sems"] = (12, units)
+        sems["last_sems"] = (2,)
+        sems["param_sems"] = (len(PARAMS),)
+        for name in PARAMS:
+            scratch[name + "_v"] = inputs[name]
+            places[name] = anywhere
     else:
         outs.update(grads)
         scratch["dw"] = params["dw"]
-    vmem = pl.BlockSpec(memory_space=pltpu.VMEM)
     names = list(inputs) + list(outs) + list(scratch) + list(sems)
     results = pl.pallas_call(
         functools.partial(kernel, plan, names),
         out_shape=list(outs.values()),
-        in_specs=[pl.BlockSpec(memory_space=pltpu.SMEM) if name == "lens" else vmem for name in inputs],
-        out_specs=[vmem] * len(outs),
+        in_specs=[places.get(name, vmem) for name in inputs],
+        out_specs=[places.get(name, vmem) for name in outs],
         scratch_shapes=[pltpu.VMEM(v.shape, v.dtype) for v in scratch.values()]
         + [pltpu.SemaphoreType.DMA(v) for v in sems.values()],
         compiler_params=pltpu.CompilerParams(
             collective_id=0, has_side_effects=True, vmem_limit_bytes=63 * 1024 * 1024),
     )(*inputs.values())
+    if plan.fused:
+        results = hand_on(results)
     return dict(zip(outs, results, strict=True))
+
+
+def hand_on(arrays):
+    n = len(arrays)
+    whole = 1024
+    parts = [(i, start, min(whole, v.shape[0] - start)) for i, v in enumerate(arrays)
+             for start in range(0, v.shape[0], whole)]
+
+    def move(*refs):
+        here, there, held, sems = refs[:n], refs[n:2 * n], refs[2 * n:3 * n], refs[3 * n]
+        into, out = [], []
+        for p, (i, start, size) in enumerate(parts):
+            rows = pl.ds(start, size)
+            into.append(pltpu.make_async_copy(here[i].at[rows], held[i].at[rows], sems.at[0, p]))
+            out.append(pltpu.make_async_copy(held[i].at[rows], there[i].at[rows], sems.at[1, p]))
+        for copy in into:
+            copy.start()
+        for p in range(len(parts)):
+            into[p].wait()
+            out[p].start()
+        for copy in out:
+            copy.wait()
+    anywhere = pl.BlockSpec(memory_space=pl.ANY)
+    return pl.pallas_call(
+        move,
+        out_shape=[jax.ShapeDtypeStruct(v.shape, v.dtype) for v in arrays],
+        in_specs=[anywhere] * n,
+        out_specs=[anywhere] * n,
+        scratch_shapes=[pltpu.VMEM(v.shape, v.dtype) for v in arrays] + [pltpu.SemaphoreType.DMA((2, len(parts)))],
+    )(*arrays)
 
 
 def body(frames, dw_first, dw_second, point, gains, shifts, se_down, se_up, cotangent, lengths, *, devices):

time: 184 us -> 171 us (0.929)
  local copies, waits for them, and re-layouts: 8 us -> 0 us
  Pallas kernels: 175 us -> 170 us
    unnamed x25 -> x0, local copies, waits for them, and re-layouts: 8 us -> none
    pallas_call x1, Pallas kernels: 175 us -> 167 us  [call_kernel(): pl.pallas_call(functools.partial(kernel, plan, names), out_shape=list(out...]
    pallas_call x0 -> x1, Pallas kernels: none -> 3.11 us  [hand_on(): pl.pallas_call(move, out_shape=[jax.ShapeDtypeStruct(v.shape, v.dtype) fo...]
where the time goes in v4:
time: 171 us
  Pallas kernels  170 us (99%)
    pallas_call x1, Pallas kernels, call_kernel(): pl.pallas_call(functools.partial(kernel, plan, names), out_shape=list(out...  167 us

profile of v4, /device:TPU:0, one launch (start us, length us, event | category | flops | bytes accessed | tf_op | source)
XLA Modules:
  0.0 171.2 jit_solution(17563318005197385992)
XLA Ops:
  0.6 167.3 %shard_map.169 = (f32[1024,256]{1,0:T(8,128)}, f32[2048,256]{1,0:T(8,128)}, f32[5,8,25]{2,1,0:T(8,128)}, f32[5,8,27]{2,1,0:T(8,128)}, f32[2,6,8,256]{3,2,1,0:T(8...) custom-call(s32[2]{0:T(128)} %refs_0_.1, ...), custom_call_target="tpu_custom_call" | custom-call | tf_op jit(solution)/shard_map/pallas_call | solution.py:1263
  167.9 3.1 %shard_map.170 = (f32[1024,256]{1,0:T(8,128)}, f32[2048,256]{1,0:T(8,128)}, f32[5,8,25]{2,1,0:T(8,128)}, f32[5,8,27]{2,1,0:T(8,128)}, f32[2,6,8,256]{3,2,1,0:T(8...) custom-call(f32[1024,256]{1,0:T(8,128)} %get-tuple-element.27.refs_0_, ...), custom_call_target="tpu_custom_call" | custom-call | tf_op jit(solution)/shard_map/pallas_call | solution.py:1299

commit v5 on v4

--- a/solution.py
+++ b/solution.py
@@ -13,7 +13,7 @@
 BF16 = jnp.bfloat16
 MESH = pl.DeviceIdType.MESH
 
-GAP = 16
+GAP = 32
 HALO = 13
 LANES = 128
 
@@ -34,14 +34,14 @@
         self.sub = sub_blocks
         self.hidden = hidden
         self.devices = devices
-        self.block = next(r for r in (26, 10, 2) if self.steps % r == 0)
-        self.fine = next(r for r in (10, 26, 2) if self.steps % r == 0)
+        self.block = next(r for r in (44, 12, 4) if self.steps % r == 0)
+        self.fine = next(r for r in (22, 12, 4) if self.steps % r == 0)
         self.pad = self.steps + 2 * HALO
         self.per = sub_blocks + 1
         self.layers = 2 * self.per
         self.tap_rows = 32
-        self.tap_sets = (32, 48, 64, 80)
-        self.dw_rows = 96
+        self.tap_sets = (32, 104)
+        self.dw_rows = 176
         self.values = 2 * LANES
         self.shard = channels // devices
         self.fused = self.shard == 8 and devices == 32 and sub_blocks == 5 and hidden == 32 and self.max_taps <= 32
@@ -152,6 +152,8 @@
     half0 = len0 // 2
     half1 = len1 // 2
     count = (half0 + half1).astype(F32)
+    inv_count = 1.0 / jnp.full((1, LANES), half0 + half1, jnp.int32).astype(F32)
+
     def steps_loop(width, body, init=0):
         return lax.fori_loop(0, Q // width, lambda i, c: body(i * width, c), init)
 
@@ -164,24 +166,6 @@
         valid[pl.ds(t0, RF)] = a + b
         return c
 
-    steps_loop(RF, mask_body)
-
-    top = 2 * GAP + 2 * plan.slots
-    for h in HV:
-        wide[h, 0:2 * GAP] = jnp.zeros((2 * GAP, LANES), F32)
-        wide[h, top:] = jnp.zeros((wide.shape[1] - top, LANES), F32)
-
-    load_frames.wait()
-
-    def widen(i, c):
-        rows = pl.ds(pl.multiple_of(i * 128, 128), 128)
-        for h in HV:
-            values = k.frames_v[rows, h * LANES:(h + 1) * LANES].astype(F32)
-            wide[h, pl.ds(pl.multiple_of(i * 128 + 2 * GAP, 32), 128)] = values
-        return c
-
-    lax.fori_loop(0, 2 * plan.slots // 128, widen, 0)
-
     def set_halo(ref, half):
         sub = lax.broadcasted_iota(jnp.int32, (HALO, 8, LANES), 1)
         low = pltpu.roll(ref[half, pl.ds(Q, HALO)], 1, 1)
@@ -189,24 +173,49 @@
         high = pltpu.roll(ref[half, pl.ds(HALO, HALO)], 7, 1)
         ref[half, pl.ds(HALO + Q, HALO)] = jnp.where(sub == 7, 0.0, high)
 
-    for phase in range(2):
-        def deinterleave(t0, c):
-            for j in range(RF):
-                a_mask = first_mask[t0 + j]
-                b_mask = valid[t0 + j] - a_mask
-                for h in HV:
-                    a = wide[h, pl.ds(2 * (t0 + j) + 2 * GAP + phase, 8, stride=2 * Q)]
-                    b = wide[h, pl.ds(2 * (t0 + j) + phase, 8, stride=2 * Q)]
-                    hid[phase, h, HALO + t0 + j] = a * a_mask + b * b_mask
+    def prepare_slots():
+        steps_loop(RF, mask_body)
+
+        top = 2 * GAP + 2 * plan.slots
+        for h in HV:
+            wide[h, 0:2 * GAP] = jnp.zeros((2 * GAP, LANES), F32)
+            wide[h, top:] = jnp.zeros((wide.shape[1] - top, LANES), F32)
+
+        load_frames.wait()
+
+        def widen(i, c):
+            rows = pl.ds(pl.multiple_of(i * 128, 128), 128)
+            for h in HV:
+                values = k.frames_v[rows, h * LANES:(h + 1) * LANES].astype(F32)
+                wide[h, pl.ds(pl.multiple_of(i * 128 + 2 * GAP, 32), 128)] = values
             return c
-        steps_loop(RF, deinterleave)
-        for h in HV:
-            set_halo(hid.at[phase], h)
+
+        lax.fori_loop(0, 2 * plan.slots // 128, widen, 0)
+
+        for phase in range(2):
+            def deinterleave(t0, c):
+                for j in range(RF):
+                    a_mask = first_mask[t0 + j]
+                    b_mask = valid[t0 + j] - a_mask
+                    for h in HV:
+                        a = wide[h, pl.ds(2 * (t0 + j) + 2 * GAP + phase, 8, stride=2 * Q)]
+                        b = wide[h, pl.ds(2 * (t0 + j) + phase, 8, stride=2 * Q)]
+                        hid[phase, h, HALO + t0 + j] = a * a_mask + b * b_mask
+                return c
+            steps_loop(RF, deinterleave)
+            for h in HV:
+                set_halo(hid.at[phase], h)
 
     def spread_lanes(values, lane):
         k.tile[...] = jnp.zeros((8, LANES), F32)
         k.tile[:, 0:values.shape[1]] = values
         return pltpu.roll(k.tile[...], lane, 1) if lane else k.tile[...]
+
+    def load_first():
+        taps = spread_lanes(k.dw_first_v[0].astype(F32), 0)
+        lane = lax.broadcasted_iota(jnp.int32, (8, LANES), 1)
+        taps = jnp.where(lane == plan.tap_rows - 1, count, taps)
+        k.first[me] = taps[0:4] + pltpu.roll(taps, plan.tap_rows, 1)[4:8]
 
     def load_shard():
         for b in range(2):
@@ -224,11 +233,10 @@
             tiles[1] = tiles[1] + jnp.transpose(k.packed[0:LANES])[0:8]
             for tile in range(2):
                 k.packed_t[8 * b:8 * b + 8, tile * LANES:(tile + 1) * LANES] = tiles[tile]
-            if b == 0:
-                lane = lax.broadcasted_iota(jnp.int32, (8, LANES), 1)
-                k.first[me] = jnp.where(lane == plan.tap_rows - 1, count, tiles[0])
         k.gath[0, depth, plane, core] = k.packed_t[...].astype(BF16)
-        for pair in range(PER):
+
+    def load_pairs(pairs):
+        for pair in pairs:
             rows = [k.point_in_v[i // PER, i % PER].astype(F32) for i in (2 * pair, 2 * pair + 1)]
             k.gath[1 + pair, depth, plane, core] = jnp.concatenate(rows, axis=0).astype(BF16)
 
@@ -265,44 +273,47 @@
     def gather_wait(unit):
         blocks_wait(chips, 5, unit)
 
+    def split_filter(rows):
+        even, odd = rows[0::2], rows[1::2]
+        full = odd + [jnp.zeros((1, LANES), F32)] * (len(even) - len(odd))
+        return even, odd, [o - e for e, o in zip(even, full)]
+
     def split_taps(b, r, h):
         taps = plan.taps[b]
-        row0, row1, row2, row3 = plan.tap_sets
-        low, high = (taps + 1) // 2, taps // 2
-        rows = [dw[b * PER + r, h, t:t + 1] for t in range(taps)] + [jnp.zeros((1, LANES), F32)]
-        dw[b * PER + r, h, row0:row0 + low] = jnp.concatenate(rows[0:taps:2], axis=0)
-        dw[b * PER + r, h, row1:row1 + high] = jnp.concatenate(rows[1:taps:2], axis=0)
-        dw[b * PER + r, h, row2:row2 + low] = jnp.concatenate(
-            [rows[2 * j + 1] - rows[2 * j] for j in range(low)], axis=0)
-        back = rows[taps - 1::-1] + [rows[taps]]
-        dw[b * PER + r, h, row3:row3 + low] = jnp.concatenate(
-            [back[2 * j + 1] - back[2 * j] for j in range(low)], axis=0)
+        rows = [dw[b * PER + r, h, t:t + 1] for t in range(taps)]
+        for base, ordered in zip(plan.tap_sets, (rows, rows[::-1])):
+            for i, part in enumerate(split_filter(ordered)):
+                for j, piece in enumerate(split_filter(part)):
+                    start = base + 24 * i + 8 * j
+                    dw[b * PER + r, h, start:start + len(piece)] = jnp.concatenate(piece, axis=0)
 
     def unpack_first():
-        got = k.first[...]
-        counts[...] = jnp.broadcast_to(got[:, 0:4, plan.tap_rows - 1:plan.tap_rows], counts.shape)
-        block = got.reshape(plan.channels, LANES)
+        got = k.first[...].reshape(4 * N, LANES)
+        lane = lax.broadcasted_iota(jnp.int32, (4 * N, LANES), 1)
+        low = jnp.where(lane < plan.tap_rows, got, 0.0).reshape(N, 4, LANES)
+        high = jnp.where(lane < plan.tap_rows, pltpu.roll(got, LANES - plan.tap_rows, 1), 0.0).reshape(N, 4, LANES)
+        counts[...] = jnp.broadcast_to(low[:, :, plan.tap_rows - 1:plan.tap_rows], counts.shape)
+        block = jnp.concatenate([low, high], axis=1).reshape(plan.channels, LANES)
         for h in HV:
             k.unpacked[0:LANES] = jnp.transpose(block[h * LANES:(h + 1) * LANES])
             dw[0, h, 0:plan.tap_rows] = k.unpacked[0:plan.tap_rows]
 
-    def unpack_values():
+    def unpack_values(b):
         got = k.gath[0].astype(F32).reshape(N, 16, plan.values)
-        for b in range(2):
-            block = got[:, 8 * b:8 * b + 8].reshape(plan.channels, plan.values)
-            for h in HV:
-                for tile in range(2):
-                    part = block[h * LANES:(h + 1) * LANES, tile * LANES:(tile + 1) * LANES]
-                    k.unpacked[tile * LANES:(tile + 1) * LANES] = jnp.transpose(part)
-                for r in range(SUB):
-                    dw[b * PER + r, h, 0:plan.tap_rows] = k.unpacked[plan.tap_row(r):plan.tap_row(r) + plan.tap_rows]
-                    split_taps(b, r, h)
-                for r in range(PER):
-                    gains[b * PER + r, h:h + 1] = k.unpacked[GAIN_ROW + r:GAIN_ROW + r + 1]
-                    shifts[b * PER + r, h:h + 1] = k.unpacked[SHIFT_ROW + r:SHIFT_ROW + r + 1]
-                lanes = slice(h * LANES, (h + 1) * LANES)
-                expand[b, :, lanes] = k.unpacked[EXPAND_ROW:EXPAND_ROW + plan.hidden]
-                squeeze_t[b, :, lanes] = k.unpacked[SQUEEZE_ROW:SQUEEZE_ROW + plan.hidden]
+        block = got[:, 8 * b:8 * b + 8].reshape(plan.channels, plan.values)
+        for h in HV:
+            for tile in range(2):
+                part = block[h * LANES:(h + 1) * LANES, tile * LANES:(tile + 1) * LANES]
+                k.unpacked[tile * LANES:(tile + 1) * LANES] = jnp.transpose(part)
+            for r in range(SUB):
+                dw[b * PER + r, h, 0:plan.tap_rows] = k.unpacked[plan.tap_row(r):plan.tap_row(r) + plan.tap_rows]
+                split_taps(b, r, h)
+            for r in range(PER):
+                gains[b * PER + r, h:h + 1] = k.unpacked[GAIN_ROW + r:GAIN_ROW + r + 1]
+                shifts[b * PER + r, h:h + 1] = k.unpacked[SHIFT_ROW + r:SHIFT_ROW + r + 1]
+            lanes = slice(h * LANES, (h + 1) * LANES)
+            expand[b, :, lanes] = k.unpacked[EXPAND_ROW:EXPAND_ROW + plan.hidden]
+            squeeze_t[b, :, lanes] = k.unpacked[SQUEEZE_ROW:SQUEEZE_ROW + plan.hidden]
 
     def unpack_pair(pair):
         got = k.gath[1 + pair].astype(F32).reshape(N, 16, plan.channels)
@@ -314,7 +325,7 @@
     if plan.fused:
         for copy in load_params:
             copy.wait()
-        load_shard()
+        load_first()
 
     if not plan.fused:
         csend[...] = jnp.full((4, LANES), count, F32)
@@ -331,12 +342,16 @@
 
     if plan.fused:
         send_to_all(k.first.at[me], k.first.at[me], count_sems.at[0], count_sems.at[1])
+        load_pairs(range(1))
         gather_send(1)
+        load_shard()
         gather_send(0)
+        load_pairs(range(1, PER))
         gather_z(2)
     else:
         send_to_all(csend, counts.at[me], count_sems.at[0], count_sems.at[1])
         counts[me] = csend[...]
+    prepare_slots()
 
     def exchange(slot, place, rows):
         send4[slot] = rows
@@ -356,16 +371,23 @@
     def accumulate(rows3):
         return jnp.sum(rows3, axis=0)
 
+    def count_slots():
+        inv_total = 1.0 / jnp.sum(counts[...], axis=0)
+        k.norm_count[...] = inv_total
+        counts[...] = counts[...] * inv_total
+
+    def shares():
+        return counts[...]
+
     def merge_stats(slot, index):
         got = received(slot, slot)
-        weight = counts[...]
-        total = jnp.sum(weight, axis=0)
-        mean = jnp.sum(weight * got, axis=0) / total
+        weight = shares()
+        mean = jnp.sum(weight * got, axis=0)
         mean4 = jnp.concatenate([mean[0:2], mean[0:2]], axis=0)
         diff = got - mean4
         between = jnp.sum(weight * diff * diff, axis=0)
         within = jnp.sum(got, axis=0)
-        var = (within[2:4] + between[0:2]) / total[0:2]
+        var = within[2:4] * k.norm_count[0:2] + between[0:2]
         inv = lax.rsqrt(var + EPSILON)
         scale = inv * gains[index]
         offset = shifts[index] - mean[0:2] * scale
@@ -384,25 +406,32 @@
             acc = term if acc is None else acc + term
         return acc
 
-    def paired(win, index, h, taps, back):
-        low, high = (taps + 1) // 2, taps // 2
-        row0, row1, row2, row3 = plan.tap_sets
-        m = R // 2
-        split = win.reshape(-1, 2, 8, LANES)
+    def paired(x, count, steps, levels, run, base):
+        if levels == 0:
+            return run(x, count, steps, base)
+        low, high = (count + 1) // 2, count // 2
+        m = steps // 2
+        if x.shape[0] % 2:
+            x = jnp.concatenate([x, x[-1:]], axis=0)
+        split = x.reshape(-1, 2, 8, LANES)
         x0, x1 = split[:, 0], split[:, 1]
-        both = x0[:m + low - 1] + x1[:m + low - 1]
-        late = x0[1:m + high] + x1[:m + high - 1]
-
-        def run(x, count, row):
+        gap = 24 if levels == 2 else 8
+
+        def part(values, n, i):
+            return paired(values, n, m, levels - 1, run, base + gap * i)
+        shared = part(x1[:m + low - 1], low, 2)
+        first = part(x0[:m + low - 1] + x1[:m + low - 1], low, 0) + shared
+        second = part(x0[1:m + high] + x1[:m + high - 1], high, 1) - shared
+        return jnp.stack([first, second], axis=1).reshape(steps, 8, LANES)
+
+    def all_taps(win, index, h, taps, back):
+        def run(x, count, steps, base):
             acc = None
             for j in range(count):
-                term = x[j:j + m] * tap(index, h, row(j))
+                term = x[j:j + steps] * tap(index, h, base + j)
                 acc = term if acc is None else acc + term
             return acc
-        shared = run(x1, low, lambda j: (row3 if back else row2) + j)
-        first = run(both, low, lambda j: row0 + (low - 1 - j if back else j)) + shared
-        second = run(late, high, lambda j: row1 + (high - 1 - j if back else j)) - shared
-        return jnp.stack([first, second], axis=1).reshape(R, 8, LANES)
+        return paired(win, taps, R, 2, run, plan.tap_sets[1 if back else 0])
 
     def layer_conv(index, pieces, between=None):
         def body(t0, c):
@@ -411,7 +440,7 @@
                 if len(pieces) == 1:
                     source, taps = pieces[0]
                     low = taps[0][1]
-                    acc = paired(hid[source, h, pl.ds(t0 + HALO + low, R + len(taps) - 1)], index, h, len(taps), False)
+                    acc = all_taps(hid[source, h, pl.ds(t0 + HALO + low, R + len(taps) - 1)], index, h, len(taps), False)
                 else:
                     for source, taps in pieces:
                         low, high = taps[0][1], taps[-1][1]
@@ -423,7 +452,7 @@
         if between is None:
             steps_loop(R, body)
         else:
-            cut = Q // R - 2
+            cut = Q // R - 1
             lax.fori_loop(0, cut, lambda i, c: body(i * R, c), 0)
             between()
             lax.fori_loop(cut, Q // R, lambda i, c: body(i * R, c), 0)
@@ -448,7 +477,7 @@
                 sums[h] = sums[h] + accumulate(dv)
                 squares[h] = squares[h] + accumulate(dv * d)
         n = jnp.full((1, LANES), count, F32)
-        shift = [jnp.sum(sums[h], axis=0, keepdims=True) / n for h in HV]
+        shift = [jnp.sum(sums[h], axis=0, keepdims=True) * inv_count for h in HV]
         spread = [jnp.sum(squares[h], axis=0, keepdims=True) - n * shift[h] * shift[h] for h in HV]
         return jnp.concatenate([pivot[h] + shift[h] for h in HV] + spread, axis=0)
 
@@ -589,7 +618,11 @@
             def _():
                 gather_core(0, True)
                 gather_wait(0)
-                unpack_values()
+                unpack_values(0)
+
+            @pl.when(step == 1)
+            def _():
+                unpack_values(1)
 
             @pl.when(jnp.logical_and(step >= 1, step < PER))
             def _():
@@ -719,11 +752,11 @@
             then()
         k.shifts_grad[index] = sums[0:2]
         k.gains_grad[index] = sums[2:4]
-        total = jnp.sum(counts[...], axis=0)[0:2]
+        inv_total = k.norm_count[0:2]
         st = stats[index]
         mean, inv, scale = st[0:2], st[2:4], st[4:6]
-        k1 = scale * sums[0:2] / total
-        k2 = scale * sums[2:4] / total * inv
+        k1 = scale * sums[0:2] * inv_total
+        k2 = scale * sums[2:4] * inv_total * inv
         rows3 = [[row(value[h:h + 1]) for value in (mean, scale, k1, k2)] for h in HV]
         for t0 in range(0, Q, R):
             v = valid[t0:t0 + R]
@@ -756,7 +789,7 @@
         low, high = -taps[-1][1], -taps[0][1]
         win = gd[h, pl.ds(t0 + HALO + low, R + high - low)]
         if len(taps) >= plan.taps[0]:
-            return paired(win, index, h, len(taps), True)
+            return all_taps(win, index, h, len(taps), True)
         return direct(win, low, index, h, [(t, -shift) for t, shift in taps])
 
     def kernel_back(index, pieces):
@@ -863,7 +896,9 @@
         for h in HV:
             k.packed[0:plan.tap_rows] = k.dw_grad[0, h]
             columns.append(jnp.transpose(k.packed[0:LANES]))
-        k.last_mine[...] = jnp.concatenate(columns, axis=0).reshape(N, 8, LANES)
+        whole = jnp.concatenate(columns, axis=0)
+        moved = pltpu.roll(whole, plan.tap_rows, 1).reshape(N, 8, LANES)
+        k.last_mine[...] = whole.reshape(N, 8, LANES)[:, 0:4] + moved[:, 4:8]
         k.last[me] = k.last_mine[me]
         for peer in peers:
             pltpu.make_async_remote_copy(src_ref=k.last_mine.at[peer], dst_ref=k.last.at[me],
@@ -872,7 +907,10 @@
 
     def last_finish():
         wait_all(k.last, k.last_sems.at[1])
-        k.dw_first_out[0] = jnp.sum(k.last[...], axis=0)[:, 0:plan.taps[0]]
+        total = jnp.sum(k.last[...], axis=0)
+        both = jnp.concatenate([total, pltpu.roll(jnp.concatenate([total, total], axis=0),
+                                                  LANES - plan.tap_rows, 1)[0:4]], axis=0)
+        k.dw_first_out[0] = both[:, 0:plan.taps[0]]
 
     def values_start():
         k.packed[...] = jnp.zeros((plan.values, LANES), F32)
@@ -1027,6 +1065,7 @@
             for r in range(SUB):
                 for h in HV:
                     split_taps(b, r, h)
+    count_slots()
     kept_first = forward_block(0)
 
     def store_middle(t0, h, values):
@@ -1124,16 +1163,19 @@
         slot = i * 128 + lax.broadcasted_iota(jnp.int32, (128, LANES), 0)
         for h in HV:
             moved = wide[h, pl.ds(pl.multiple_of(i * 128 + 2 * GAP, 32), 128)]
-            k.frames_grad_v[rows, h * LANES:(h + 1) * LANES] = jnp.where(slot < len0, wide[h, rows], moved)
+            k.frames_grad_v[lax.rem(i, 2 * per_piece), :, h * LANES:(h + 1) * LANES] = jnp.where(
+                slot < len0, wide[h, rows], moved)
         return c
+    pieces_out = 8
+    per_piece = 2 * plan.slots // pieces_out // 128
     save_frames = []
-    pieces_out = 4
     for piece in range(pieces_out):
-        size = 2 * plan.slots // pieces_out
-        lax.fori_loop(piece * size // 128, (piece + 1) * size // 128, ungap_wide, 0)
-        rows = pl.ds(piece * size, size)
-        save_frames.append(pltpu.make_async_copy(k.frames_grad_v.at[rows], k.frames_grad.at[rows],
-                                                 k.io_sems.at[3 + piece]))
+        if piece >= 2:
+            save_frames[piece - 2].wait()
+        lax.fori_loop(piece * per_piece, (piece + 1) * per_piece, ungap_wide, 0)
+        save_frames.append(pltpu.make_async_copy(
+            k.frames_grad_v.at[pl.ds((piece % 2) * per_piece, per_piece)],
+            k.frames_grad.at[pl.ds(piece * per_piece, per_piece)], k.io_sems.at[3 + piece]))
         save_frames[-1].start()
     if plan.fused:
         pair_finish(1)
@@ -1142,7 +1184,7 @@
         last_finish()
 
     save_out.wait()
-    for copy in save_frames:
+    for copy in save_frames[-2:]:
         copy.wait()
     wait_all(k.first if plan.fused else counts, count_sems.at[0])
 
@@ -1175,7 +1217,7 @@
         return jax.ShapeDtypeStruct(dims, dtype)
     outs = {
         "out": shape(plan.slots, channels),
-        "frames_grad": shape(2 * plan.slots, channels),
+        "frames_grad": shape(2 * plan.slots // 128, 128, channels),
     }
     params = {
         "dw": shape(layers, halves, plan.dw_rows, LANES),
@@ -1205,7 +1247,7 @@
         "wide": shape(halves, 2 * plan.slots + 4 * GAP, LANES),
         "frames_v": shape(2 * plan.slots, channels, dtype=BF16),
         "cot_v": shape(plan.slots, channels),
-        "frames_grad_v": shape(2 * plan.slots, channels),
+        "frames_grad_v": shape(plan.slots // 256, 128, channels),
         "first_mask": shape(Q, 8, LANES),
         "valid": shape(Q, 8, LANES),
         "slope": shape(halves, Q, 8, LANES),
@@ -1216,8 +1258,9 @@
         "recv4": shape(layers, devices, 4, LANES),
         "counts": shape(devices, 4, LANES),
         "csend": shape(4, LANES),
+        "norm_count": shape(4, LANES),
     }
-    sems = {"send_sem": (slots,), "recv_sem": (slots,), "count_sems": (2,), "io_sems": (7,)}
+    sems = {"send_sem": (slots,), "recv_sem": (slots,), "count_sems": (2,), "io_sems": (11,)}
     if plan.fused:
         units, chips = 1 + plan.per, devices // 2
         outs.update({
@@ -1236,9 +1279,9 @@
             "point_t": shape(layers, channels, channels, dtype=BF16),
             "packed": shape(vals, LANES),
             "packed_t": shape(16, vals),
-            "first": shape(devices, 8, LANES),
-            "last_mine": shape(devices, 8, LANES),
-            "last": shape(devices, 8, LANES),
+            "first": shape(devices, 4, LANES),
+            "last_mine": shape(devices, 4, LANES),
+            "last": shape(devices, 4, LANES),
             "unpacked": shape(vals, LANES),
             "gath": shape(units, 4, 4, 2, 16, channels, dtype=BF16),
             "shares": shape(2, 4, 4, 2, 16, channels, dtype=BF16),
@@ -1277,9 +1320,10 @@
 
 def hand_on(arrays):
     n = len(arrays)
-    whole = 1024
-    parts = [(i, start, min(whole, v.shape[0] - start)) for i, v in enumerate(arrays)
-             for start in range(0, v.shape[0], whole)]
+    parts = []
+    for i, v in enumerate(arrays):
+        rows = max(1, v.shape[0] * (1 << 20) // (4 * v.size))
+        parts += [(i, start, min(rows, v.shape[0] - start)) for start in range(0, v.shape[0], rows)]
 
     def move(*refs):
         here, there, held, sems = refs[:n], refs[n:2 * n], refs[2 * n:3 * n], refs[3 * n]
@@ -1318,7 +1362,7 @@
             "point_in": point, "gains_in": jnp.swapaxes(gains, 0, 1), "shifts_in": jnp.swapaxes(shifts, 0, 1),
             "se_down": se_down, "se_up": jnp.swapaxes(se_up, 1, 2)})
         return (
-            res["out"], res["frames_grad"], jnp.swapaxes(res["dw_first_out"], 1, 2),
+            res["out"], res["frames_grad"].reshape(2 * plan.slots, channels), jnp.swapaxes(res["dw_first_out"], 1, 2),
             jnp.swapaxes(res["dw_second_out"], 1, 2), res["point_out"], jnp.swapaxes(res["gains_out"], 0, 1),
             jnp.swapaxes(res["shifts_out"], 0, 1), res["squeeze_out"], jnp.swapaxes(res["expand_out"], 1, 2))
 
@@ -1360,7 +1404,7 @@
     def norm_out(v):
         return lax.dynamic_slice_in_dim(v.reshape(2, per, channels), lax.axis_index("dp") * shard, shard, 2)
     return (
-        res["out"], res["frames_grad"], g1.reshape(sub, taps_first, shard), g2.reshape(sub, taps_second, shard),
+        res["out"], res["frames_grad"].reshape(2 * plan.slots, channels), g1.reshape(sub, taps_first, shard), g2.reshape(sub, taps_second, shard),
         scatter(res["point_grad"].reshape(2, per, channels, channels), 2),
         norm_out(res["gains_grad"]), norm_out(res["shifts_grad"]),
         jnp.swapaxes(gsq.reshape(2, hidden, shard), 1, 2), gex.reshape(2, hidden, shard))

time: 171 us -> 163 us (0.953)
  Pallas kernels: 170 us -> 162 us
    pallas_call x1, Pallas kernels: 167 us -> 159 us  [call_kernel(): pl.pallas_call(functools.partial(kernel, plan, names), out_shape=list(out...]
where the time goes in v5:
time: 163 us
  Pallas kernels  162 us (99%)
    pallas_call x1, Pallas kernels, call_kernel(): pl.pallas_call(functools.partial(kernel, plan, names), out_shape=list(out...  159 us

profile of v5, /device:TPU:0, one launch (start us, length us, event | category | flops | bytes accessed | tf_op | source)
XLA Modules:
  0.0 162.6 jit_solution(15710946792903672158)
XLA Ops:
  0.6 158.7 %shard_map.169 = (f32[1024,256]{1,0:T(8,128)}, f32[16,128,256]{2,1,0:T(8,128)}, f32[5,8,25]{2,1,0:T(8,128)}, f32[5,8,27]{2,1,0:T(8,128)}, f32[2,6,8,256]{3,2,1,0...) custom-call(s32[2]{0:T(128)} %refs_0_.1, ...), custom_call_target="tpu_custom_call" | custom-call | tf_op jit(solution)/shard_map/pallas_call | solution.py:1306
  159.4 3.1 %shard_map.170 = (f32[1024,256]{1,0:T(8,128)}, f32[16,128,256]{2,1,0:T(8,128)}, f32[5,8,25]{2,1,0:T(8,128)}, f32[5,8,27]{2,1,0:T(8,128)}, f32[2,6,8,256]{3,2,1,0...) custom-call(f32[1024,256]{1,0:T(8,128)} %get-tuple-element.27.refs_0_, ...), custom_call_target="tpu_custom_call" | custom-call | tf_op jit(solution)/shard_map/pallas_call | solution.py:1343

commit v6 on v5

--- a/solution.py
+++ b/solution.py
@@ -249,6 +249,35 @@
         view = k.gained.at[0, pl.ds(0, count)]
         pltpu.make_async_copy(view, view, k.unit_sems.at[sem, unit]).wait()
 
+    def lead_wait(count, sem, side):
+        view = k.gained.at[0, pl.ds(0, count), :, pl.ds(0, LANES)]
+        pltpu.make_async_copy(view, view, k.lead_sems.at[sem, side]).wait()
+
+    def lead_copy(src, dst, sem, side, to):
+        pltpu.make_async_remote_copy(src_ref=src, dst_ref=dst, send_sem=k.lead_sems.at[sem, side],
+                                     recv_sem=k.lead_sems.at[sem + 1, side], device_id=(to,),
+                                     device_id_type=MESH).start()
+
+    def lead_send(side):
+        rows = k.point_in_v[0, side].astype(F32)
+        k.lead[side, depth, plane, core] = jnp.concatenate(
+            [rows[:, h * LANES:(h + 1) * LANES] for h in HV], axis=0).astype(BF16)
+        view = k.lead.at[side, depth, plane, core]
+        for peer in same_core:
+            lead_copy(view, view, 0, side, peer)
+
+    def lead_core(side):
+        lead_wait(chips - 1, 1, side)
+        view = k.lead.at[side, :, :, core]
+        lead_copy(view, view, 2, side, partner)
+
+    def lead_unpack(side):
+        lead_wait(chips, 3, side)
+        got = k.lead[side].astype(F32).reshape(N, 16, LANES)
+        block = jnp.concatenate([got[:, 8 * h:8 * h + 8].reshape(plan.channels, LANES) for h in HV], axis=1)
+        point[side] = block.astype(BF16)
+        k.point_t[side] = jnp.transpose(block).astype(BF16)
+
     def gather_send(unit):
         view = k.gath.at[unit, depth, plane, core]
         for peer in same_core:
@@ -281,7 +310,11 @@
     def split_taps(b, r, h):
         taps = plan.taps[b]
         rows = [dw[b * PER + r, h, t:t + 1] for t in range(taps)]
-        for base, ordered in zip(plan.tap_sets, (rows, rows[::-1])):
+        both = (rows, rows[::-1])
+        if b == 0 and r == 0:
+            start = (taps - 1) // 2 % 2
+            both = (rows[start::2], rows[1 - start::2])
+        for base, ordered in zip(plan.tap_sets, both):
             for i, part in enumerate(split_filter(ordered)):
                 for j, piece in enumerate(split_filter(part)):
                     start = base + 24 * i + 8 * j
@@ -297,6 +330,7 @@
         for h in HV:
             k.unpacked[0:LANES] = jnp.transpose(block[h * LANES:(h + 1) * LANES])
             dw[0, h, 0:plan.tap_rows] = k.unpacked[0:plan.tap_rows]
+            split_taps(0, 0, h)
 
     def unpack_values(b):
         got = k.gath[0].astype(F32).reshape(N, 16, plan.values)
@@ -305,7 +339,7 @@
             for tile in range(2):
                 part = block[h * LANES:(h + 1) * LANES, tile * LANES:(tile + 1) * LANES]
                 k.unpacked[tile * LANES:(tile + 1) * LANES] = jnp.transpose(part)
-            for r in range(SUB):
+            for r in range(1 - b, SUB):
                 dw[b * PER + r, h, 0:plan.tap_rows] = k.unpacked[plan.tap_row(r):plan.tap_row(r) + plan.tap_rows]
                 split_taps(b, r, h)
             for r in range(PER):
@@ -342,10 +376,10 @@
 
     if plan.fused:
         send_to_all(k.first.at[me], k.first.at[me], count_sems.at[0], count_sems.at[1])
-        load_pairs(range(1))
-        gather_send(1)
+        lead_send(0)
         load_shard()
         gather_send(0)
+        lead_send(1)
         load_pairs(range(1, PER))
         gather_z(2)
     else:
@@ -355,8 +389,8 @@
 
     def exchange(slot, place, rows):
         send4[slot] = rows
+        send_to_all(send4.at[slot], recv4.at[place, me], send_sem.at[slot], recv_sem.at[slot])
         recv4[place, me] = rows
-        send_to_all(send4.at[slot], recv4.at[place, me], send_sem.at[slot], recv_sem.at[slot])
 
     def received(slot, place):
         wait_all(recv4.at[place], recv_sem.at[slot])
@@ -424,14 +458,14 @@
         second = part(x0[1:m + high] + x1[:m + high - 1], high, 1) - shared
         return jnp.stack([first, second], axis=1).reshape(steps, 8, LANES)
 
-    def all_taps(win, index, h, taps, back):
+    def all_taps(win, index, h, taps, side):
         def run(x, count, steps, base):
             acc = None
             for j in range(count):
                 term = x[j:j + steps] * tap(index, h, base + j)
                 acc = term if acc is None else acc + term
             return acc
-        return paired(win, taps, R, 2, run, plan.tap_sets[1 if back else 0])
+        return paired(win, taps, R, 2, run, plan.tap_sets[side])
 
     def layer_conv(index, pieces, between=None):
         def body(t0, c):
@@ -440,11 +474,12 @@
                 if len(pieces) == 1:
                     source, taps = pieces[0]
                     low = taps[0][1]
-                    acc = all_taps(hid[source, h, pl.ds(t0 + HALO + low, R + len(taps) - 1)], index, h, len(taps), False)
+                    acc = all_taps(hid[source, h, pl.ds(t0 + HALO + low, R + len(taps) - 1)], index, h, len(taps), 0)
                 else:
-                    for source, taps in pieces:
+                    for side, (source, taps) in enumerate(pieces):
                         low, high = taps[0][1], taps[-1][1]
-                        part = direct(hid[source, h, pl.ds(t0 + HALO + low, R + high - low)], low, index, h, taps)
+                        win = hid[source, h, pl.ds(t0 + HALO + low, R + high - low)]
+                        part = all_taps(win, index, h, len(taps), side)
                         acc = part if acc is None else acc + part
                 rows = pl.ds(pl.multiple_of(8 * t0, 16), 8 * R)
                 acts[index, rows, h * LANES:(h + 1) * LANES] = acc.reshape(8 * R, LANES).astype(BF16)
@@ -617,7 +652,9 @@
             @pl.when(step == 0)
             def _():
                 gather_core(0, True)
+                lead_core(1)
                 gather_wait(0)
+                lead_unpack(1)
                 unpack_values(0)
 
             @pl.when(step == 1)
@@ -644,7 +681,7 @@
         def layer(r, pieces, before=None):
             index = b * PER + r
             first = before is not None
-            layer_conv(index, pieces, (lambda: gather_core(1, True)) if first else None)
+            layer_conv(index, pieces, (lambda: lead_core(0)) if first else None)
             if first:
                 before()
             exchange(index, index, pointwise(index))
@@ -662,8 +699,7 @@
                     gather_plane(2 + step)
 
         def first_matrices():
-            gather_wait(1)
-            unpack_pair(0)
+            lead_unpack(0)
         layer(0, block_pieces(b), first_matrices if plan.fused and b == 0 else None)
         activate(b * PER, hid_of(b, 1))
 
@@ -789,7 +825,7 @@
         low, high = -taps[-1][1], -taps[0][1]
         win = gd[h, pl.ds(t0 + HALO + low, R + high - low)]
         if len(taps) >= plan.taps[0]:
-            return all_taps(win, index, h, len(taps), True)
+            return all_taps(win, index, h, len(taps), 1)
         return direct(win, low, index, h, [(t, -shift) for t, shift in taps])
 
     def kernel_back(index, pieces):
@@ -802,7 +838,29 @@
                     g = gd[h, pl.ds(HALO + t0, RF)]
                     win = hid[source, h, pl.ds(t0 + HALO + low, RF + high - low)]
                     return tuple(acc + accumulate(g * win[s - low:s - low + RF]) for acc, (_, s) in zip(c, taps))
-                accs = steps_loop(RF, body, tuple(jnp.zeros((8, LANES), F32) for _ in taps))
+                def paired_body(t0, c):
+                    g = gd[h, pl.ds(HALO + t0, RF)].reshape(RF // 2, 2, 8, LANES)
+                    win = hid[source, h, pl.ds(t0 + HALO + low, RF + high - low)]
+                    if win.shape[0] % 2:
+                        win = jnp.concatenate([win, win[-1:]], axis=0)
+                    x = win.reshape(-1, 2, 8, LANES)
+                    g0, g1, x0, x1 = g[:, 0], g[:, 1], x[:, 0], x[:, 1]
+                    n, even, odd = RF // 2, (len(taps) + 1) // 2, len(taps) // 2
+                    both = x0[:n + even - 1] + x1[:n + even - 1]
+                    late = x0[1:n + odd] + x1[:n + odd - 1]
+                    gap = g0 - g1
+                    new = ([accumulate(g0 * both[i:i + n]) for i in range(even)]
+                           + [accumulate(gap * x1[i:i + n]) for i in range(even)]
+                           + [accumulate(g1 * late[i:i + n]) for i in range(odd)])
+                    return tuple(acc + value for acc, value in zip(c, new))
+                if len(taps) < plan.taps[0]:
+                    even, odd = (len(taps) + 1) // 2, len(taps) // 2
+                    parts = steps_loop(RF, paired_body, tuple(
+                        jnp.zeros((8, LANES), F32) for _ in range(2 * even + odd)))
+                    accs = [parts[2 * even + i // 2] + parts[even + i // 2] if i % 2
+                            else parts[i // 2] - parts[even + i // 2] for i in range(len(taps))]
+                else:
+                    accs = steps_loop(RF, body, tuple(jnp.zeros((8, LANES), F32) for _ in taps))
                 for acc, (tap, _) in zip(accs, taps):
                     k.dw_grad[index, h, pl.ds(tap, 1)] = jnp.sum(acc, axis=0, keepdims=True)
 
@@ -1194,13 +1252,17 @@
     lax.fori_loop(0, send4.shape[0], drain, 0)
     if plan.fused:
         for unit in range(1 + PER):
-            blocks_wait(chips - 1 if unit < 2 else 3, 0, unit)
+            if unit != 1:
+                blocks_wait(chips - 1 if unit < 2 else 3, 0, unit)
+                blocks_wait(chips, 4, unit)
             if unit >= 2:
                 blocks_wait(12, 2, unit)
                 blocks_wait(3, 10, unit)
             else:
                 blocks_wait(chips - 1, 8, unit)
-            blocks_wait(chips, 4, unit)
+        for side in range(2):
+            lead_wait(chips - 1, 0, side)
+            lead_wait(chips, 2, side)
         wait_all(k.last, k.last_sems.at[0])
 
 
@@ -1284,6 +1346,7 @@
             "last": shape(devices, 4, LANES),
             "unpacked": shape(vals, LANES),
             "gath": shape(units, 4, 4, 2, 16, channels, dtype=BF16),
+            "lead": shape(2, 4, 4, 2, 16, LANES, dtype=BF16),
             "shares": shape(2, 4, 4, 2, 16, channels, dtype=BF16),
             "inbox": shape(units, 4, 4, 16, channels, dtype=BF16),
             "sums": shape(3, 4, 4, 16, channels, dtype=BF16),
@@ -1295,6 +1358,7 @@
         })
         sems["unit_sems"] = (12, units)
         sems["last_sems"] = (2,)
+        sems["lead_sems"] = (4, 2)
         sems["param_sems"] = (len(PARAMS),)
         for name in PARAMS:
             scratch[name + "_v"] = inputs[name]

time: 163 us -> 161 us (0.988)
  Pallas kernels: 162 us -> 160 us
    pallas_call x1, Pallas kernels: 159 us -> 157 us  [call_kernel(): pl.pallas_call(functools.partial(kernel, plan, names), out_shape=list(out...]
where the time goes in v6:
time: 161 us
  Pallas kernels  160 us (99%)
    pallas_call x1, Pallas kernels, call_kernel(): pl.pallas_call(functools.partial(kernel, plan, names), out_shape=list(out...  157 us

profile of v6, /device:TPU:0, one launch (start us, length us, event | category | flops | bytes accessed | tf_op | source)
XLA Modules:
  0.0 161.0 jit_solution(3609697990159132472)
XLA Ops:
  0.6 157.1 %shard_map.169 = (f32[1024,256]{1,0:T(8,128)}, f32[16,128,256]{2,1,0:T(8,128)}, f32[5,8,25]{2,1,0:T(8,128)}, f32[5,8,27]{2,1,0:T(8,128)}, f32[2,6,8,256]{3,2,1,0...) custom-call(s32[2]{0:T(128)} %refs_0_.1, ...), custom_call_target="tpu_custom_call" | custom-call | tf_op jit(solution)/shard_map/pallas_call | solution.py:1370
  157.7 3.1 %shard_map.170 = (f32[1024,256]{1,0:T(8,128)}, f32[16,128,256]{2,1,0:T(8,128)}, f32[5,8,25]{2,1,0:T(8,128)}, f32[5,8,27]{2,1,0:T(8,128)}, f32[2,6,8,256]{3,2,1,0...) custom-call(f32[1024,256]{1,0:T(8,128)} %get-tuple-element.27.refs_0_, ...), custom_call_target="tpu_custom_call" | custom-call | tf_op jit(solution)/shard_map/pallas_call | solution.py:1407

commit v7 on v6

--- a/solution.py
+++ b/solution.py
@@ -1078,6 +1078,10 @@
                 def _():
                     scatter_z(1 + HALF * b + 2)
                 if b == 0:
+                    @pl.when(r == 0)
+                    def _():
+                        scatter_send(0)
+
                     @pl.when(r == SUB - 1)
                     def _():
                         scatter_z(1 + HALF + 1)
@@ -1111,6 +1115,7 @@
         lax.fori_loop(0, SUB - 1, step, 0)
         if plan.fused and b == 0:
             values_start()
+            scatter_sum(0, 1)
         filtered(0)
 
     if plan.fused:
@@ -1193,9 +1198,6 @@
     backward_block(0)
     pieces = block_pieces(0)
     backward_aside(0, 0)
-    if plan.fused:
-        scatter_sum(0, 1)
-        scatter_send(0)
     kernel_back(0, pieces)
     if plan.fused:
         last_start()

time: 161 us -> 161 us (level)
  no operation moved by 1% of the time
where the time goes in v7:
time: 161 us; the launch traced here: 160 us
  Pallas kernels  160 us (99%)
    pallas_call x1, Pallas kernels, call_kernel(): pl.pallas_call(functools.partial(kernel, plan, names), out_shape=list(out...  157 us

profile of v7, /device:TPU:0, one launch (start us, length us, event | category | flops | bytes accessed | tf_op | source)
XLA Modules:
  0.0 160.5 jit_solution(16163562400487189127)
XLA Ops:
  0.6 156.6 %shard_map.169 = (f32[1024,256]{1,0:T(8,128)}, f32[16,128,256]{2,1,0:T(8,128)}, f32[5,8,25]{2,1,0:T(8,128)}, f32[5,8,27]{2,1,0:T(8,128)}, f32[2,6,8,256]{3,2,1,0...) custom-call(s32[2]{0:T(128)} %refs_0_.1, ...), custom_call_target="tpu_custom_call" | custom-call | tf_op jit(solution)/shard_map/pallas_call | solution.py:1372
  157.2 3.1 %shard_map.170 = (f32[1024,256]{1,0:T(8,128)}, f32[16,128,256]{2,1,0:T(8,128)}, f32[5,8,25]{2,1,0:T(8,128)}, f32[5,8,27]{2,1,0:T(8,128)}, f32[2,6,8,256]{3,2,1,0...) custom-call(f32[1024,256]{1,0:T(8,128)} %get-tuple-element.27.refs_0_, ...), custom_call_target="tpu_custom_call" | custom-call | tf_op jit(solution)/shard_map/pallas_call | solution.py:1409
